TPU v7x, 256 devices: a whole 4x4x8 slice. The times are simulated.
256 devices in a mesh: seq: 32 (over y, z_lo, core), tensor: 8 (over x, z_hi).
Axes of the slice: x: 4, y: 4, z: 8 (z_hi: 2, z_lo: 4; z = z_hi * 4 + z_lo), core: 2. Of those that a mesh axis runs over, the one named last changes fastest.
Arguments:
- features: bfloat16 [4, 40, 64, 512], P(None, 'tensor', 'seq'), may hold values from -6 to 6
- conv_weight: bfloat16 [3, 3, 3, 512, 16], replicated, may hold values from -0.0546875 to 0.0546875
- conv_bias: float32 [16], replicated, may hold values from -4 to 4
- embed_weight: bfloat16 [16, 5120], replicated, may hold values from -1.5 to 1.5
- position_table: bfloat16 [10240, 5120], P('seq'), may hold values from -6 to 6
- norm_gain: bfloat16 [5120], replicated, may hold values from 0.099609375 to 1.8984375
- qkv_weight: bfloat16 [5120, 6144], P('seq', 'tensor'), may hold values from -1 to 1
- page_owner: int32 [1280], P('seq'), may hold values from 0 to 31, as said below
- page_slot: int32 [1280], P('seq'), may hold values from 0 to 39, as said below
Outputs:
- attention: bfloat16 [10240, 4096], P('seq', 'tensor')
- kv_cache: bfloat16 [1280, 8, 2, 1024], P('seq', None, None, 'tensor')
Inputs may be any that keep to these rules, and one draw needn't show every extreme that they name: `page_owner`: of the 40 pages of one index of seq, at most 3 have the same owner, and exactly 3 for some owner. Every owner keeps exactly 40 pages. `page_slot`: the pages of one owner use each slot 0 to 39 once.
All inputs are finite; a program needn't handle non-finite values.
Results may differ from a plain program's by a relative error of at most 0.0084.
Values may be sent and summed in bfloat16 or wider, within the bound.
No kernel may reach another device: no remote copies, remote signals or barrier semaphores. Data moves between devices by JAX's collectives and lax.ppermute only.
A program may use at most 128 MiB of HBM per device.

v0:
```python
import jax
import jax.numpy as jnp
from jax import lax
from jax.sharding import PartitionSpec as P

HD = 128
PAGE = 8
GROUP = 4


def padded_2(block, sides, width):
    for axis, dim in sides:
        count = lax.axis_size(axis)
        forward = [(i, i + 1) for i in range(count - 1)]
        backward = [(target, source) for source, target in forward]
        low = lax.ppermute(
            lax.slice_in_dim(block, block.shape[dim] - width, None, axis=dim), axis, forward
        )
        high = lax.ppermute(lax.slice_in_dim(block, 0, width, axis=dim), axis, backward)
        block = jnp.concatenate([low, block, high], axis=dim)
    return block


def convolve(padded, conv_weight, conv_bias, frames, height, columns):
    pieces = []
    for offset_time in range(3):
        for offset_row in range(3):
            for offset_col in range(3):
                pieces.append(
                    padded[
                        offset_time : offset_time + frames,
                        offset_row : offset_row + height,
                        offset_col : offset_col + columns,
                        :,
                    ]
                )
    stacked = jnp.concatenate(pieces, axis=-1).reshape(frames * height * columns, -1)
    kernel = conv_weight.reshape(-1, conv_weight.shape[-1])
    latent = jnp.dot(stacked, kernel, preferred_element_type=jnp.float32) + conv_bias
    return latent.reshape(frames, height, columns, -1)


def pick_block(length):
    for candidate in range(min(length, 1024), 0, -1):
        if length % candidate == 0:
            return candidate
    return 1


def keep_state(operands):
    return operands[0]


def attend_group(operands):
    previous, group_queries, group_index, key_block, value_block, key_index = operands
    best, total, summed = previous
    scale = 1.0 / group_queries.shape[-1] ** 0.5
    scores = (
        jnp.einsum("kgqd,nkd->kgqn", group_queries, key_block, preferred_element_type=jnp.float32)
        * scale
    )
    allowed = key_index[None, :] <= group_index[:, None]
    scores = jnp.where(allowed, scores, -1e30)
    new_best = jnp.maximum(best, jnp.max(scores, axis=-1))
    factor = jnp.exp(best - new_best)
    weights = jnp.where(allowed, jnp.exp(scores - new_best[..., None]), 0.0)
    total = total * factor + jnp.sum(weights, axis=-1)
    summed = summed * factor[..., None] + jnp.einsum(
        "kgqn,nkd->kgqd",
        weights.astype(jnp.bfloat16),
        value_block,
        preferred_element_type=jnp.float32,
    )
    return (new_best, total, summed)


def on_device(
    features,
    conv_weight,
    conv_bias,
    embed_weight,
    position_table,
    norm_gain,
    qkv_weight,
    page_owner,
    page_slot,
):
    seq_count = lax.axis_size("seq")
    frames, height, columns, channels = features.shape
    active = jax.nn.silu(features.astype(jnp.float32)).astype(jnp.bfloat16)
    padded = padded_2(active, (("seq", 2), ("tensor", 1)), 1)
    padded = jnp.pad(padded, ((2, 0), (0, 0), (0, 0), (0, 0)))
    local_latent = convolve(padded, conv_weight, conv_bias, frames, height, columns)
    latent = lax.all_gather(local_latent, "tensor", axis=1, tiled=True)
    full_height = latent.shape[1]
    latent_width = latent.shape[3]
    per_device_rows = frames * full_height // seq_count
    grouped = latent.reshape(seq_count, per_device_rows, columns, latent_width)
    token_latent = lax.all_to_all(grouped, "seq", split_axis=0, concat_axis=2, tiled=True).reshape(
        -1, latent_width
    )
    token_count = token_latent.shape[0]
    hidden = jnp.dot(
        token_latent, embed_weight.astype(jnp.float32), precision=lax.Precision.HIGHEST
    ) + position_table.astype(jnp.float32)
    normed = (
        hidden
        * lax.rsqrt(jnp.mean(hidden * hidden, axis=-1, keepdims=True) + 1e-05)
        * norm_gain.astype(jnp.float32)
    ).astype(jnp.bfloat16)
    proj_width = qkv_weight.shape[1]
    qkv = jnp.dot(
        normed,
        lax.all_gather(qkv_weight, "seq", axis=0, tiled=True),
        preferred_element_type=jnp.float32,
    ).astype(jnp.bfloat16)
    kv_local = proj_width // ((GROUP + 2) * HD)
    split = qkv.reshape(token_count, kv_local, GROUP + 2, HD)
    keys = split[:, :, GROUP, :].reshape(token_count, kv_local * HD)
    values = split[:, :, GROUP + 1, :].reshape(token_count, kv_local * HD)
    my_index = lax.axis_index("seq")
    group_count = 1
    query_set = jnp.transpose(split[:, :, :GROUP, :], (1, 2, 0, 3)).reshape(
        kv_local, GROUP, 1, token_count, HD
    )
    query_index = (my_index * token_count + jnp.arange(token_count, dtype=jnp.int32)).reshape(
        1, token_count
    )
    group_last = jnp.max(query_index, axis=1)
    rows_group = query_set.shape[3]
    start_state = tuple(
        (
            (
                jnp.full((kv_local, GROUP, rows_group), -1e30, jnp.float32),
                jnp.zeros((kv_local, GROUP, rows_group), jnp.float32),
                jnp.zeros((kv_local, GROUP, rows_group, HD), jnp.float32),
            )
            for group in range(group_count)
        )
    )
    state = start_state
    start = jnp.int32(0)
    key_piece = lax.all_gather(keys, "seq", axis=0, tiled=True)
    value_piece = lax.all_gather(values, "seq", axis=0, tiled=True)
    length = key_piece.shape[0]
    block = pick_block(length)
    key_blocks = key_piece.reshape(length // block, block, kv_local, HD)
    value_blocks = value_piece.reshape(length // block, block, kv_local, HD)

    def step(current, inputs):
        block_index, key_block, value_block = inputs
        first = start + block_index * block
        key_index = first + jnp.arange(block, dtype=jnp.int32)
        operands = (
            current[0],
            query_set[:, :, 0],
            query_index[0],
            key_block,
            value_block,
            key_index,
        )
        updated = [lax.cond(first > group_last[0], keep_state, attend_group, operands)]
        return (tuple(updated), None)

    state, unused = lax.scan(
        step, state, (jnp.arange(length // block, dtype=jnp.int32), key_blocks, value_blocks)
    )
    result = jnp.stack([state[0][2] / state[0][1][..., None]], axis=2).astype(jnp.bfloat16)
    attention = jnp.transpose(
        result.reshape(kv_local, GROUP, token_count, HD), (2, 0, 1, 3)
    ).reshape(token_count, -1)
    block_count = token_count // PAGE
    capacity = max(2, (block_count + seq_count // 2 - 1) // (seq_count // 2))
    page_width = kv_local * HD
    page_blocks = jnp.stack([keys, values], axis=1).reshape(block_count, PAGE, 2, page_width)
    positions = jnp.arange(block_count, dtype=jnp.int32)
    same_owner = page_owner[:, None] == page_owner[None, :]
    earlier = positions[None, :] < positions[:, None]
    ranking = jnp.sum((same_owner & earlier).astype(jnp.int32), axis=1)
    target = page_owner * capacity + ranking
    send_pages = (
        jnp.zeros((seq_count * capacity, PAGE, 2, page_width), jnp.bfloat16)
        .at[target]
        .set(page_blocks)
    )
    send_slots = jnp.full((seq_count * capacity,), block_count, jnp.int32).at[target].set(page_slot)
    got_pages, got_slots = (
        lax.all_to_all(
            send_pages.reshape(seq_count, capacity, PAGE, 2, page_width),
            "seq",
            split_axis=0,
            concat_axis=0,
            tiled=True,
        ),
        lax.all_to_all(
            send_slots.reshape(seq_count, capacity), "seq", split_axis=0, concat_axis=0, tiled=True
        ),
    )
    kv_cache = (
        jnp.zeros((block_count, PAGE, 2, page_width), jnp.bfloat16)
        .at[got_slots.reshape(-1)]
        .set(got_pages.reshape(-1, PAGE, 2, page_width), mode="drop")
    )
    return (attention, kv_cache)


def solution(mesh):
    placed = (
        P(None, "tensor", "seq", None),
        P(),
        P(),
        P(),
        P("seq", None),
        P(),
        P("seq", "tensor"),
        P("seq"),
        P("seq"),
    )
    return jax.shard_map(
        on_device,
        mesh=mesh,
        in_specs=placed,
        out_specs=(P("seq", "tensor"), P("seq", None, None, "tensor")),
        check_vma=False,
    )
```

profile of v0, /device:TPU:25, one launch (start us, length us, event | category | flops | bytes accessed | tf_op | source)
XLA Modules:
  0.0 352.3 jit_solution(9246164682374376813)
XLA Ops:
  7.9 0.9 fusion.42
  8.9 4.1 %collective-permute-start = (bf16[4,5,1,512]{3,2,1,0:T(2,128)(2,1)S(1)}, bf16[4,5,1,512]{3,2,1,0:T(2,128)(2,1)S(1)}, u32[]{:S(2)}, u32[]{:S(2)}) collective-permute-start(bf16[4,5,1,512]{3,2,1,0:T(2,128)(2,1)S(1)} %get-tuple-element.246), channel_id=1, source_target_pairs={{0,8},{8,16},{16,24},{24,32},{32,40},{40,48},{48,56},{56,64},{64,7... | collective-permute-start | bytes 61448 | tf_op jit(solution)/shard_map/ppermute | solution.py:16
  13.0 1.9 collective-permute-start.1
  14.9 3.4 collective-permute-done.1
  18.4 7.9 %collective-permute-start.2 = (bf16[4,1,4,512]{3,2,1,0:T(4,128)(2,1)S(1)}, bf16[4,1,4,512]{3,2,1,0:T(4,128)(2,1)S(1)}, u32[]{:S(2)}, u32[]{:S(2)}) collective-permute-start(bf16[4,1,4,512]{3,2,1,0:T(4,128)(2,1)S(1)} %get-tuple-element.244), channel_id=1, source_target_pairs={{0,1},{1,2},{2,3},{3,4},{4,5},{5,6},{6,7},{8,9},{9,10},{10,11},{11... | collective-permute-start | bytes 49160 | tf_op jit(solution)/shard_map/ppermute | solution.py:16
  26.3 1.3 collective-permute-start.3
  27.6 1.4 copy.43
  29.0 1.4 reshape.153
  30.4 4.4 %collective-permute-done.3 = bf16[4,1,4,512]{3,2,1,0:T(4,128)(2,1)S(1)} collective-permute-done((bf16[4,1,4,512]{3,2,1,0:T(4,128)(2,1)S(1)}, bf16[4,1,4,512]{3,2,1,0:T(4,128)(2,1)S(1)}, u32[]{:S(2)}, u32[]{:S(2)}) %collective-permute-start.3) | collective-permute-done | bytes 16416 | tf_op jit(solution)/shard_map/ppermute | solution.py:19
  53.4 3.7 %reshape.152 = bf16[40,13824]{1,0:T(8,128)(2,1)} reshape(bf16[4,5,2,13824]{3,2,1,0:T(2,128)(2,1)} %constant_dynamic-update-slice_fusion) | data formatting | bytes 2211840 | tf_op jit(solution)/shard_map/reshape | solution.py:37
  57.1 1.8 convolution_add_fusion.1
  59.0 40.7 %all_gather.12 = f32[4,40,2,16]{3,2,1,0:T(2,128)} all-gather(f32[4,5,2,16]{3,2,1,0:T(2,128)S(1)} %bitcast.103), channel_id=1, replica_groups=mesh['seq'=32,'tensor'=8] {'tensor'}, dimensions={1}, use_global_device_ids=true | all-gather | bytes 23040 | tf_op jit(solution)/shard_map/all_gather | solution.py:94
  99.7 1.7 reshape.207
  101.4 13.8 %all-to-all-start = ((f32[32,1,160]{2,1,0:T(1,128)}), f32[32,1,160]{2,1,0:T(1,128)S(1)}, u32[]{:S(2)}, u32[]{:S(2)}) async-start(f32[32,1,160]{2,1,0:T(1,128)} %reshape.207), calls=%async_computation | async-start | bytes 65536 | tf_op jit(solution)/shard_map/all_to_all | solution.py:99
  115.3 5.4 %all-to-all-done = f32[32,1,160]{2,1,0:T(1,128)S(1)} async-done(((f32[32,1,160]{2,1,0:T(1,128)}), f32[32,1,160]{2,1,0:T(1,128)S(1)}, u32[]{:S(2)}, u32[]{:S(2)}) %all-to-all-start) | async-done | bytes 20512 | tf_op jit(solution)/shard_map/all_to_all | solution.py:99
  122.8 1.0 copy.45
  123.8 5.3 %multiply_reduce_fusion = (f32[320]{0:T(512)S(1)}, f32[320,5120]{1,0:T(8,128)}) fusion(bf16[320,5120]{1,0:T(8,128)(2,1)S(1)} %copy-done.1, f32[320,16]{1,0:T(8,128)S(1)} %bitcast.95, bf16[16,5120]{1,0:T(8,128)(2,1)S(1)} %copy-done), kind=kOutput, calls=%fused_computation.33 | convolution fusion | flops 321126080 | bytes 10016000 | tf_op jit(solution)/shard_map/dot_general | solution.py:103
  129.1 7.9 %fusion.29 = bf16[320,768]{1,0:T(8,128)(2,1)S(1)} fusion(bf16[5120,768]{1,0:T(8,128)(2,1)} %all-gather.6.cloned.1.call-done, f32[320,5120]{1,0:T(8,128)} %get-tuple-element.249, f32[5120]{0:T(1024)S(1)} %convert_element_type.42, f32[320]{0:T(512)S(1)} %add_rsqrt_fusion), kind=kOutput, calls=%fused_computation.37 | convolution fusion | flops 2521743360 | bytes 14931200 | tf_op jit(solution)/shard_map/dot_general | solution.py:112
  139.1 0.8 scatter_custom_fusion
  140.6 6.2 %all-to-all-start.1 = ((s32[32,1,3]{2,1,0:T(1,128)}), s32[32,1,3]{2,1,0:T(1,128)S(1)}, u32[]{:S(2)}, u32[]{:S(2)}) async-start(s32[32,1,3]{2,1,0:T(1,128)} %bitcast.25), calls=%async_computation.1 | async-start | bytes 32768 | tf_op jit(solution)/shard_map/all_to_all | solution.py:195
  146.9 0.9 pad_maximum_fusion
  148.7 5.1 %scatter_fusion = bf16[96,8,2,128]{3,1,2,0:T(8,128)(2,1)} fusion(bf16[96,8,2,128]{3,1,2,0:T(8,128)(2,1)} %broadcast_in_dim.48, s32[40]{0:T(128)S(1)} %compare_select_fusion.1, bf16[40,8,2,128]{3,1,2,0:T(8,128)(2,1)S(1)} %copy.56), kind=kCustom, calls=%fused_computation.1 | custom fusion | bytes 491680 | tf_op jit(solution)/shard_map/scatter | solution.py:184
  153.8 7.7 %all-to-all-start.2 = ((bf16[32,3,8,2,128]{4,2,3,1,0:T(8,128)(2,1)}), bf16[32,3,8,2,128]{4,2,3,1,0:T(8,128)(2,1)S(1)}, u32[]{:S(2)}, u32[]{:S(2)}) async-start(bf16[32,3,8,2,128]{4,2,3,1,0:T(8,128)(2,1)} %bitcast.29), calls=%async_computation.2 | async-start | bytes 786432 | tf_op jit(solution)/shard_map/all_to_all | solution.py:188
  163.8 12.7 %all-to-all-done.2 = bf16[32,3,8,2,128]{4,2,3,1,0:T(8,128)(2,1)S(1)} async-done(((bf16[32,3,8,2,128]{4,2,3,1,0:T(8,128)(2,1)}), bf16[32,3,8,2,128]{4,2,3,1,0:T(8,128)(2,1)S(1)}, u32[]{:S(2)}, u32[]{:S(2)}) %all-to-all-start.2) | async-done | bytes 393248 | tf_op jit(solution)/shard_map/all_to_all | solution.py:188
  176.5 3.6 %scatter_fusion.1 = bf16[40,8,2,128]{3,1,2,0:T(8,128)(2,1)S(1)} fusion(bf16[40,8,2,128]{3,1,2,0:T(8,128)(2,1)S(1)} %broadcast_in_dim.46, s32[96]{0:T(128)S(1)} %fusion.44, bf16[96,8,2,128]{3,1,2,0:T(8,128)(2,1)S(1)} %bitcast.93), kind=kCustom, calls=%fused_computation.2 | custom fusion | bytes 1180032 | tf_op jit(solution)/shard_map/scatter | solution.py:202
  180.9 17.3 %all-gather.8.cloned.1.call-done = bf16[10240,1,1,128]{3,0,2,1:T(8,128)(2,1)} async-done(((bf16[320,1,1,128]{3,0,2,1:T(8,128)(2,1)}), bf16[10240,1,1,128]{3,0,2,1:T(8,128)(2,1)}) %all-gather.8.cloned.1.call-update) | async-done | bytes 2621456 | tf_op jit(solution)/shard_map/all_gather | solution.py:143
  198.2 62.4 %all-gather.10.cloned.1.call-done = bf16[10240,1,1,128]{3,0,2,1:T(8,128)(2,1)} async-done(((bf16[320,1,1,128]{3,0,2,1:T(8,128)(2,1)}), bf16[10240,1,1,128]{3,0,2,1:T(8,128)(2,1)}) %all-gather.10.cloned.1.call-update) | async-done | bytes 2621456 | tf_op jit(solution)/shard_map/all_gather | solution.py:144
  260.7 83.8 %while.15 = (s32[]{:T(128)}, f32[1,4,320]{2,1,0:T(4,128)S(1)}, f32[1,4,320]{2,1,0:T(4,128)S(1)}, f32[1,4,320,128]{3,2,1,0:T(8,128)S(1)}, s32[10]{0:T(128)S(1)}, ...) while((s32[]{:T(128)}, f32[1,4,320]{2,1,0:T(4,128)S(1)}, ...), condition=%wide.region_7.8_spmd.clone, body=%wide.region_2.7_spmd.clone.sunk | while | flops 688788544 | bytes 19306796 | solution.py:165
  262.6 7.1 %conditional.3 = (f32[1,4,320]{2,1,0:T(4,128)S(1)}, f32[1,4,320]{2,1,0:T(4,128)S(1)}, f32[1,4,320,128]{3,2,1,0:T(8,128)S(1)}) conditional(s32[]{:T(128)} %convert_element_type.80, (s32[]{:T(128)}, s32[1024]{0:T(1024)S(1)}, s32[]{:T(128)}, bf16[10,1024,1,128]{3,1,2,0:T(8,128)(2,1)}, s32[]{:T(128)}, /*index=5*/bf16[1,4,320,128]{3,2,1,0:T(8,128)(2,1)S(1)}, ...), branch_computations={%region_3.5_spmd, %region_6.6_spmd} | conditional | flops 688788544 | bytes 19290912 | solution.py:162
  262.9 2.2 fusion.2
  265.1 1.8 fusion.4
  267.0 2.8 fusion.11
  271.7 7.1 %conditional.3 = (f32[1,4,320]{2,1,0:T(4,128)S(1)}, f32[1,4,320]{2,1,0:T(4,128)S(1)}, f32[1,4,320,128]{3,2,1,0:T(8,128)S(1)}) conditional(s32[]{:T(128)} %convert_element_type.80, (s32[]{:T(128)}, s32[1024]{0:T(1024)S(1)}, s32[]{:T(128)}, bf16[10,1024,1,128]{3,1,2,0:T(8,128)(2,1)}, s32[]{:T(128)}, /*index=5*/bf16[1,4,320,128]{3,2,1,0:T(8,128)(2,1)S(1)}, ...), branch_computations={%region_3.5_spmd, %region_6.6_spmd} | conditional | flops 688788544 | bytes 19290912 | solution.py:162
  272.0 2.2 fusion.2
  274.2 1.8 fusion.4
  276.1 2.8 fusion.11
  280.8 7.1 %conditional.3 = (f32[1,4,320]{2,1,0:T(4,128)S(1)}, f32[1,4,320]{2,1,0:T(4,128)S(1)}, f32[1,4,320,128]{3,2,1,0:T(8,128)S(1)}) conditional(s32[]{:T(128)} %convert_element_type.80, (s32[]{:T(128)}, s32[1024]{0:T(1024)S(1)}, s32[]{:T(128)}, bf16[10,1024,1,128]{3,1,2,0:T(8,128)(2,1)}, s32[]{:T(128)}, /*index=5*/bf16[1,4,320,128]{3,2,1,0:T(8,128)(2,1)S(1)}, ...), branch_computations={%region_3.5_spmd, %region_6.6_spmd} | conditional | flops 688788544 | bytes 19290912 | solution.py:162
  281.1 2.2 fusion.2
  283.3 1.8 fusion.4
  285.1 2.8 fusion.11
  289.9 7.1 %conditional.3 = (f32[1,4,320]{2,1,0:T(4,128)S(1)}, f32[1,4,320]{2,1,0:T(4,128)S(1)}, f32[1,4,320,128]{3,2,1,0:T(8,128)S(1)}) conditional(s32[]{:T(128)} %convert_element_type.80, (s32[]{:T(128)}, s32[1024]{0:T(1024)S(1)}, s32[]{:T(128)}, bf16[10,1024,1,128]{3,1,2,0:T(8,128)(2,1)}, s32[]{:T(128)}, /*index=5*/bf16[1,4,320,128]{3,2,1,0:T(8,128)(2,1)S(1)}, ...), branch_computations={%region_3.5_spmd, %region_6.6_spmd} | conditional | flops 688788544 | bytes 19290912 | solution.py:162
  290.2 2.2 fusion.2
  292.4 1.8 fusion.4
  294.2 2.8 fusion.11
  299.0 7.1 %conditional.3 = (f32[1,4,320]{2,1,0:T(4,128)S(1)}, f32[1,4,320]{2,1,0:T(4,128)S(1)}, f32[1,4,320,128]{3,2,1,0:T(8,128)S(1)}) conditional(s32[]{:T(128)} %convert_element_type.80, (s32[]{:T(128)}, s32[1024]{0:T(1024)S(1)}, s32[]{:T(128)}, bf16[10,1024,1,128]{3,1,2,0:T(8,128)(2,1)}, s32[]{:T(128)}, /*index=5*/bf16[1,4,320,128]{3,2,1,0:T(8,128)(2,1)S(1)}, ...), branch_computations={%region_3.5_spmd, %region_6.6_spmd} | conditional | flops 688788544 | bytes 19290912 | solution.py:162
  299.3 2.2 fusion.2
  301.5 1.8 fusion.4
  303.3 2.8 fusion.11
  308.1 7.1 %conditional.3 = (f32[1,4,320]{2,1,0:T(4,128)S(1)}, f32[1,4,320]{2,1,0:T(4,128)S(1)}, f32[1,4,320,128]{3,2,1,0:T(8,128)S(1)}) conditional(s32[]{:T(128)} %convert_element_type.80, (s32[]{:T(128)}, s32[1024]{0:T(1024)S(1)}, s32[]{:T(128)}, bf16[10,1024,1,128]{3,1,2,0:T(8,128)(2,1)}, s32[]{:T(128)}, /*index=5*/bf16[1,4,320,128]{3,2,1,0:T(8,128)(2,1)S(1)}, ...), branch_computations={%region_3.5_spmd, %region_6.6_spmd} | conditional | flops 688788544 | bytes 19290912 | solution.py:162
  308.4 2.2 fusion.2
  310.6 1.8 fusion.4
  312.4 2.8 fusion.11
  317.2 7.1 %conditional.3 = (f32[1,4,320]{2,1,0:T(4,128)S(1)}, f32[1,4,320]{2,1,0:T(4,128)S(1)}, f32[1,4,320,128]{3,2,1,0:T(8,128)S(1)}) conditional(s32[]{:T(128)} %convert_element_type.80, (s32[]{:T(128)}, s32[1024]{0:T(1024)S(1)}, s32[]{:T(128)}, bf16[10,1024,1,128]{3,1,2,0:T(8,128)(2,1)}, s32[]{:T(128)}, /*index=5*/bf16[1,4,320,128]{3,2,1,0:T(8,128)(2,1)S(1)}, ...), branch_computations={%region_3.5_spmd, %region_6.6_spmd} | conditional | flops 688788544 | bytes 19290912 | solution.py:162
  317.5 2.2 fusion.2
  319.7 1.8 fusion.4
  321.5 2.8 fusion.11
  326.3 7.1 %conditional.3 = (f32[1,4,320]{2,1,0:T(4,128)S(1)}, f32[1,4,320]{2,1,0:T(4,128)S(1)}, f32[1,4,320,128]{3,2,1,0:T(8,128)S(1)}) conditional(s32[]{:T(128)} %convert_element_type.80, (s32[]{:T(128)}, s32[1024]{0:T(1024)S(1)}, s32[]{:T(128)}, bf16[10,1024,1,128]{3,1,2,0:T(8,128)(2,1)}, s32[]{:T(128)}, /*index=5*/bf16[1,4,320,128]{3,2,1,0:T(8,128)(2,1)S(1)}, ...), branch_computations={%region_3.5_spmd, %region_6.6_spmd} | conditional | flops 688788544 | bytes 19290912 | solution.py:162
  326.6 2.2 fusion.2
  328.8 1.8 fusion.4
  330.6 2.8 fusion.11
  335.4 7.1 %conditional.3 = (f32[1,4,320]{2,1,0:T(4,128)S(1)}, f32[1,4,320]{2,1,0:T(4,128)S(1)}, f32[1,4,320,128]{3,2,1,0:T(8,128)S(1)}) conditional(s32[]{:T(128)} %convert_element_type.80, (s32[]{:T(128)}, s32[1024]{0:T(1024)S(1)}, s32[]{:T(128)}, bf16[10,1024,1,128]{3,1,2,0:T(8,128)(2,1)}, s32[]{:T(128)}, /*index=5*/bf16[1,4,320,128]{3,2,1,0:T(8,128)(2,1)S(1)}, ...), branch_computations={%region_3.5_spmd, %region_6.6_spmd} | conditional | flops 688788544 | bytes 19290912 | solution.py:162
  335.7 2.2 fusion.2
  337.8 1.8 fusion.4
  339.7 2.8 fusion.11
  (171 shorter events, 38.3 us)
Async XLA Ops:
  7.2 116.6 %copy-start = (bf16[16,5120]{1,0:T(8,128)(2,1)S(1)}, bf16[16,5120]{1,0:T(8,128)(2,1)}, u32[]{:S(2)}) copy-start(bf16[16,5120]{1,0:T(8,128)(2,1)} %param.16) | copy-start | bytes 491524
  7.2 121.9 %all-gather.6.cloned.1.call-start = ((), (), s32[]{:S(2)}) async-start(), calls=%async_computation.3 | async-start | bytes 8110080 | tf_op jit(solution)/shard_map/all_gather | solution.py:114
  8.9 6.0 %collective-permute-start = (bf16[4,5,1,512]{3,2,1,0:T(2,128)(2,1)S(1)}, bf16[4,5,1,512]{3,2,1,0:T(2,128)(2,1)S(1)}, u32[]{:S(2)}, u32[]{:S(2)}) collective-permute-start(bf16[4,5,1,512]{3,2,1,0:T(2,128)(2,1)S(1)} %get-tuple-element.246), channel_id=1, source_target_pairs={{0,8},{8,16},{16,24},{24,32},{32,40},{40,48},{48,56},{56,64},{64,7... | collective-permute-start | bytes 61448 | tf_op jit(solution)/shard_map/ppermute | solution.py:16
  13.0 5.3 %collective-permute-start.1 = (bf16[4,5,1,512]{3,2,1,0:T(2,128)(2,1)S(1)}, bf16[4,5,1,512]{3,2,1,0:T(2,128)(2,1)S(1)}, u32[]{:S(2)}, u32[]{:S(2)}) collective-permute-start(bf16[4,5,1,512]{3,2,1,0:T(2,128)(2,1)S(1)} %get-tuple-element.247), channel_id=1, source_target_pairs={{8,0},{16,8},{24,16},{32,24},{40,32},{48,40},{56,48},{64,56},{72,6... | collective-permute-start | bytes 61448 | tf_op jit(solution)/shard_map/ppermute | solution.py:19
  18.4 12.0 %collective-permute-start.2 = (bf16[4,1,4,512]{3,2,1,0:T(4,128)(2,1)S(1)}, bf16[4,1,4,512]{3,2,1,0:T(4,128)(2,1)S(1)}, u32[]{:S(2)}, u32[]{:S(2)}) collective-permute-start(bf16[4,1,4,512]{3,2,1,0:T(4,128)(2,1)S(1)} %get-tuple-element.244), channel_id=1, source_target_pairs={{0,1},{1,2},{2,3},{3,4},{4,5},{5,6},{6,7},{8,9},{9,10},{10,11},{11... | collective-permute-start | bytes 49160 | tf_op jit(solution)/shard_map/ppermute | solution.py:16
  26.3 8.5 %collective-permute-start.3 = (bf16[4,1,4,512]{3,2,1,0:T(4,128)(2,1)S(1)}, bf16[4,1,4,512]{3,2,1,0:T(4,128)(2,1)S(1)}, u32[]{:S(2)}, u32[]{:S(2)}) collective-permute-start(bf16[4,1,4,512]{3,2,1,0:T(4,128)(2,1)S(1)} %get-tuple-element.245), channel_id=1, source_target_pairs={{1,0},{2,1},{3,2},{4,3},{5,4},{6,5},{7,6},{9,8},{10,9},{11,10},{12... | collective-permute-start | bytes 49160 | tf_op jit(solution)/shard_map/ppermute | solution.py:19
  35.0 14.9 %copy-start.2 = (bf16[4,5,2,512]{3,2,1,0:T(2,128)(2,1)S(1)}, bf16[4,5,2,512]{3,2,1,0:T(2,128)(2,1)}, u32[]{:S(2)}) copy-start(bf16[4,5,2,512]{3,2,1,0:T(2,128)(2,1)} %param.13) | copy-start | bytes 122884
  52.7 4.4 %copy-start.4 = (f32[16]{0:T(128)S(1)}, f32[16]{0:T(128)}, u32[]{:S(2)}) copy-start(f32[16]{0:T(128)} %param.15) | copy-start | bytes 196
  53.4 70.4 %copy-start.1 = (bf16[320,5120]{1,0:T(8,128)(2,1)S(1)}, bf16[320,5120]{1,0:T(8,128)(2,1)}, u32[]{:S(2)}) copy-start(bf16[320,5120]{1,0:T(8,128)(2,1)} %param.17) | copy-start | bytes 9830404
  57.1 58.2 %copy-start.3 = (bf16[5120]{0:T(1024)(128)(2,1)S(1)}, bf16[5120]{0:T(1024)(128)(2,1)}, u32[]{:S(2)}) copy-start(bf16[5120]{0:T(1024)(128)(2,1)} %param.18) | copy-start | bytes 30724
  101.4 19.3 %all-to-all-start = ((f32[32,1,160]{2,1,0:T(1,128)}), f32[32,1,160]{2,1,0:T(1,128)S(1)}, u32[]{:S(2)}, u32[]{:S(2)}) async-start(f32[32,1,160]{2,1,0:T(1,128)} %reshape.207), calls=%async_computation | async-start | bytes 65536 | tf_op jit(solution)/shard_map/all_to_all | solution.py:99
  115.2 82.9 %all-gather.8.cloned.1.call-start = ((), (), s32[]{:S(2)}) async-start(), calls=%async_computation.4 | async-start | bytes 2703360 | tf_op jit(solution)/shard_map/all_gather | solution.py:143
  136.9 1.9 copy-start.5
  138.1 122.6 %all-gather.10.cloned.1.call-start = ((), (), s32[]{:S(2)}) async-start(), calls=%async_computation.5 | async-start | bytes 2703360 | tf_op jit(solution)/shard_map/all_gather | solution.py:144
  140.6 13.2 %all-to-all-start.1 = ((s32[32,1,3]{2,1,0:T(1,128)}), s32[32,1,3]{2,1,0:T(1,128)S(1)}, u32[]{:S(2)}, u32[]{:S(2)}) async-start(s32[32,1,3]{2,1,0:T(1,128)} %bitcast.25), calls=%async_computation.1 | async-start | bytes 32768 | tf_op jit(solution)/shard_map/all_to_all | solution.py:195
  153.8 22.7 %all-to-all-start.2 = ((bf16[32,3,8,2,128]{4,2,3,1,0:T(8,128)(2,1)}), bf16[32,3,8,2,128]{4,2,3,1,0:T(8,128)(2,1)S(1)}, u32[]{:S(2)}, u32[]{:S(2)}) async-start(bf16[32,3,8,2,128]{4,2,3,1,0:T(8,128)(2,1)} %bitcast.29), calls=%async_computation.2 | async-start | bytes 786432 | tf_op jit(solution)/shard_map/all_to_all | solution.py:188
Sparse Core Ops, SparseCore 0:
  9.9 71.6 all-gather.5
  138.2 59.9 all-gather.7
  200.0 60.5 all-gather.9
where the time goes:
time: 359 us; the launch traced here: 352 us
  waiting for transfers between devices  106 us (30%)
  matrix products  59.3 us (17%)
  local copies, waits for them, and re-layouts  48.3 us (13%)
  starting transfers between devices  43.1 us (12%)
  blocking collectives  40.7 us (11%)
  other arithmetic  26.1 us (7%)
  loops' own time  14.4 us (4%)
  between operations  14.1 us (4%)
    all_gather x1, waiting for transfers between devices, on_device(): value_piece = lax.all_gather(values, 'seq', axis=0, tiled=True)  62.4 us
    all_gather x1, blocking collectives, on_device(): latent = lax.all_gather(local_latent, 'tensor', axis=1, tiled=True)  40.7 us
    dot_general x9, matrix products, attend_group(): jnp.einsum('kgqn,nkd->kgqd', weights.astype(jnp.bfloat16), value_block, p...  25 us
    unnamed x41, local copies, waits for them, and re-layouts  21.1 us
    dot_general x9, matrix products, attend_group(): jnp.einsum('kgqd,nkd->kgqn', group_queries, key_block, preferred_element_...  19.4 us
    all_gather x1, waiting for transfers between devices, on_device(): key_piece = lax.all_gather(keys, 'seq', axis=0, tiled=True)  17.3 us
    reduce_sum x9, other arithmetic, attend_group(): total = total * factor + jnp.sum(weights, axis=-1)  16.5 us
    another operation x1, loops' own time, on_device(): lax.scan(step, state, (jnp.arange(length // block, dtype=jnp.int32), key_...  13.9 us
  transfers between devices with their start and end apart: 10, of which 6 were waited for; matrix products, arithmetic and copies ran while one was open for 15% of the time, Pallas kernels for 0%

commit v1 on v0

v1 whole, which is shorter than its diff:
```python
import functools

import jax
import jax.numpy as jnp
import numpy as np
from jax import lax
from jax.experimental import pallas as pl
from jax.experimental.pallas import tpu as pltpu
from jax.sharding import PartitionSpec as P

HD = 128
PAGE = 8
GROUP = 4
LAT = 16
BLK = 320
PAGES = 40
SEQ = 32
ROWS = 5
COLS = 2
FRAMES = 4
EXT = (ROWS + 2) * (COLS + 2)
TOK = 384
CHUNK = 1280
TILE = 256
QROWS = GROUP * BLK
VMEM = 56 * 1024 * 1024


def params(**extra):
    return pltpu.CompilerParams(vmem_limit_bytes=VMEM, **extra)


def roll_lanes(value, shift):
    shift = shift % value.shape[1]
    return pltpu.roll(value, shift, 1) if shift else value


def conv_kernel(feat_ref, weight_ref, out_ref, grid_ref):
    grid_ref[...] = jnp.zeros_like(grid_ref)
    for frame in range(FRAMES):
        for row in range(ROWS):
            start = frame * EXT + (row + 1) * (COLS + 2) + 1
            value = feat_ref[frame, row].astype(jnp.float32)
            grid_ref[start : start + COLS, :] = value / (1.0 + jnp.exp(-value))
    active = grid_ref[...].astype(jnp.bfloat16)
    product = lax.dot_general(
        weight_ref[...], active, (((1,), (1,)), ((), ())), preferred_element_type=jnp.float32
    )
    lane = lax.broadcasted_iota(jnp.int32, (LAT, 128), 1)
    total = jnp.zeros((LAT, 128), jnp.float32)
    for time in range(3):
        part = jnp.zeros((LAT, 128), jnp.float32)
        for row in range(3):
            for col in range(3):
                index = (time * 3 + row) * 3 + col
                piece = product[index * LAT : (index + 1) * LAT, :]
                part = part + roll_lanes(piece, -((row - 1) * (COLS + 2) + col - 1))
        delay = (2 - time) * EXT
        if delay:
            part = jnp.where(lane >= delay, roll_lanes(part, delay), 0.0)
        total = total + part
    padded = jnp.concatenate([total, jnp.zeros((128 - LAT, 128), jnp.float32)], axis=0)
    out_ref[...] = jnp.transpose(padded)[:, :LAT]


def partial_latents(features, conv_weight):
    weight = jnp.transpose(conv_weight, (0, 1, 2, 4, 3)).reshape(-1, conv_weight.shape[3])
    return pl.pallas_call(
        conv_kernel,
        out_shape=jax.ShapeDtypeStruct((128, LAT), jnp.float32),
        scratch_shapes=[pltpu.VMEM((128, features.shape[-1]), jnp.float32)],
        compiler_params=params(),
        name="conv",
    )(features, weight)


def split_three(value):
    high = value.astype(jnp.bfloat16)
    rest = value - high.astype(jnp.float32)
    middle = rest.astype(jnp.bfloat16)
    low = (rest - middle.astype(jnp.float32)).astype(jnp.bfloat16)
    return high, middle, low


def place_kernel(parts_ref, token_ref, out_ref):
    count = parts_ref.shape[0]
    token = lax.broadcasted_iota(jnp.int32, (count, TOK), 1)
    pick = jnp.where(token == token_ref[...], 1.0, 0.0).astype(jnp.bfloat16)
    total = jnp.zeros((LAT, TOK), jnp.float32)
    for part in reversed(split_three(parts_ref[...])):
        total = total + lax.dot_general(
            part, pick, (((0,), (0,)), ((), ())), preferred_element_type=jnp.float32
        )
    out_ref[...] = total


def place_table():
    table = np.full((3, SEQ, ROWS + 2, COLS + 2), -1, np.int32)
    for case in range(3):
        for source in range(SEQ):
            for row in range(ROWS + 2):
                for col in range(COLS + 2):
                    height = row - 1 + ROWS * (case - 1)
                    width = source * COLS - 1 + col
                    if 0 <= height < ROWS and 0 <= width < SEQ * COLS:
                        table[case, source, row, col] = height * SEQ * COLS + width
    return table.reshape(3, SEQ * EXT, 1)


def place_latents(parts, offset):
    table = jnp.asarray(place_table())
    token = lax.dynamic_index_in_dim(table, jnp.clip(offset + 1, 0, 2), 0, keepdims=False)
    token = jnp.where(jnp.abs(offset) <= 1, token, -1)
    return pl.pallas_call(
        place_kernel,
        out_shape=jax.ShapeDtypeStruct((LAT, TOK), jnp.float32),
        compiler_params=params(),
        name="place",
    )(parts, token)


def hidden_kernel(latent_ref, bias_ref, embed_ref, table_ref, gain_ref, out_ref, hid_ref, sq_ref):
    step = pl.program_id(0)
    width = table_ref.shape[1]
    latent = latent_ref[...][:, :BLK] + bias_ref[...]
    latent = jnp.concatenate(split_three(latent), axis=0)
    embed = embed_ref[...]
    hidden = lax.dot_general(
        latent,
        jnp.concatenate([embed, embed, embed], axis=0),
        (((0,), (0,)), ((), ())),
        preferred_element_type=jnp.float32,
    ) + table_ref[...].astype(jnp.float32)
    hid_ref[step] = hidden
    squares = jnp.zeros((BLK, 128), jnp.float32)
    for lane in range(0, width, 128):
        piece = hidden[:, lane : lane + 128]
        squares = squares + piece * piece

    @pl.when(step == 0)
    def _():
        sq_ref[...] = squares

    @pl.when(step > 0)
    def _():
        sq_ref[...] += squares

    @pl.when(step == pl.num_programs(0) - 1)
    def _():
        count = hid_ref.shape[0]
        mean = jnp.sum(sq_ref[...], axis=1, keepdims=True) / (count * width)
        factor = lax.rsqrt(mean + 1e-05)
        for tile in range(count):
            cut = slice(tile * width, (tile + 1) * width)
            gain = gain_ref[:, cut].astype(jnp.float32)
            out_ref[:, cut] = (hid_ref[tile] * factor * gain).astype(jnp.bfloat16)


def normed_hidden(latent, conv_bias, embed_weight, position_table, norm_gain):
    depth = position_table.shape[1]
    steps = 8
    width = depth // steps
    return pl.pallas_call(
        hidden_kernel,
        grid=(steps,),
        in_specs=[
            pl.BlockSpec((LAT, TOK), lambda i: (0, 0)),
            pl.BlockSpec((LAT, 1), lambda i: (0, 0)),
            pl.BlockSpec((LAT, width), lambda i: (0, i)),
            pl.BlockSpec((BLK, width), lambda i: (0, i)),
            pl.BlockSpec((1, depth), lambda i: (0, 0)),
        ],
        out_specs=pl.BlockSpec((BLK, depth), lambda i: (0, 0)),
        out_shape=jax.ShapeDtypeStruct((BLK, depth), jnp.bfloat16),
        scratch_shapes=[
            pltpu.VMEM((steps, BLK, width), jnp.float32),
            pltpu.VMEM((BLK, 128), jnp.float32),
        ],
        compiler_params=params(dimension_semantics=("arbitrary",)),
        name="hidden",
    )(latent, conv_bias.reshape(LAT, 1), embed_weight, position_table, norm_gain.reshape(1, depth))


def attend_chunk(masked, first_key, first_query, q_ref, kv_ref, best_ref, total_ref, sum_ref):
    scale = 1.4426950408889634 / HD**0.5
    keys = kv_ref[:, :HD]
    values = kv_ref[:, HD:]
    for start in range(0, QROWS, TILE):
        cut = slice(start, start + TILE)
        scores = lax.dot_general(
            keys, q_ref[cut, :], (((1,), (1,)), ((), ())), preferred_element_type=jnp.float32
        )
        if masked:
            key = first_key + lax.broadcasted_iota(jnp.int32, scores.shape, 0)
            query = start + lax.broadcasted_iota(jnp.int32, (1, TILE), 1)
            for head in range(GROUP - 1, 0, -1):
                query = jnp.where(query >= head * BLK, query - head * BLK, query)
            scores = jnp.where(key <= first_query + query, scores, -1e30)
        old = best_ref[:, cut]
        best = jnp.maximum(old, jnp.max(scores, axis=0, keepdims=True))
        factor = jnp.exp2((old - best) * scale)
        weights = jnp.exp2((scores - best) * scale)
        best_ref[:, cut] = best
        total_ref[:, cut] = total_ref[:, cut] * factor + jnp.sum(weights, axis=0, keepdims=True)
        sum_ref[:, cut] = sum_ref[:, cut] * factor + lax.dot_general(
            values,
            weights.astype(jnp.bfloat16),
            (((0,), (0,)), ((), ())),
            preferred_element_type=jnp.float32,
        )


def attention_kernel(me_ref, qkv_ref, kv_ref, out_ref, q_ref, best_ref, total_ref, sum_ref, row_ref):
    step = pl.program_id(0)
    me = me_ref[0]
    mine = me // (CHUNK // BLK)

    @pl.when(step == 0)
    def _():
        best_ref[...] = jnp.full_like(best_ref, -1e30)
        total_ref[...] = jnp.zeros_like(total_ref)
        sum_ref[...] = jnp.zeros_like(sum_ref)
        for head in range(GROUP):
            q_ref[head * BLK : (head + 1) * BLK, :] = qkv_ref[:, head * HD : (head + 1) * HD]

    state = (q_ref, kv_ref, best_ref, total_ref, sum_ref)

    @pl.when(step < mine)
    def _():
        attend_chunk(False, 0, 0, *state)

    @pl.when(step == mine)
    def _():
        attend_chunk(True, step * CHUNK, me * BLK, *state)

    @pl.when(step == pl.num_programs(0) - 1)
    def _():
        for start in range(0, QROWS, TILE):
            cut = slice(start, start + TILE)
            row_ref[cut, :] = jnp.transpose(sum_ref[:, cut] / total_ref[:, cut])
        for head in range(GROUP):
            rows = row_ref[head * BLK : (head + 1) * BLK, :]
            out_ref[:, head * HD : (head + 1) * HD] = rows.astype(jnp.bfloat16)


def attend(me, qkv, kv):
    steps = kv.shape[0] // CHUNK
    return pl.pallas_call(
        attention_kernel,
        grid_spec=pltpu.PrefetchScalarGridSpec(
            num_scalar_prefetch=1,
            grid=(steps,),
            in_specs=[
                pl.BlockSpec(qkv.shape, lambda i, me: (0, 0)),
                pl.BlockSpec(
                    (CHUNK, 2 * HD), lambda i, me: (jnp.minimum(i, me[0] // (CHUNK // BLK)), 0)
                ),
            ],
            out_specs=pl.BlockSpec((BLK, GROUP * HD), lambda i, me: (0, 0)),
            scratch_shapes=[
                pltpu.VMEM((QROWS, HD), jnp.bfloat16),
                pltpu.VMEM((1, QROWS), jnp.float32),
                pltpu.VMEM((1, QROWS), jnp.float32),
                pltpu.VMEM((HD, QROWS), jnp.float32),
                pltpu.VMEM((QROWS, HD), jnp.float32),
            ],
        ),
        out_shape=jax.ShapeDtypeStruct((BLK, GROUP * HD), jnp.bfloat16),
        compiler_params=params(dimension_semantics=("arbitrary",)),
        name="attend",
    )(me.reshape(1), qkv, kv)


def page_kernel(page_ref, kv_ref, out_ref, held_ref, sems):
    def copy(slot):
        first = pl.multiple_of((page_ref[slot] // 2) * 2 * PAGE, 2 * PAGE)
        return pltpu.make_async_copy(
            kv_ref.at[pl.ds(first, 2 * PAGE), :], held_ref.at[slot], sems.at[slot]
        )

    for slot in range(PAGES):
        copy(slot).start()
    for pair in range(PAGES // 2):
        halves = []
        for slot in (2 * pair, 2 * pair + 1):
            copy(slot).wait()
            rows = held_ref[slot].astype(jnp.float32)
            odd = page_ref[slot] % 2 == 1
            halves.append(jnp.where(odd, rows[PAGE:], rows[:PAGE]))
        both = jnp.concatenate(halves, axis=0).astype(jnp.bfloat16)
        out_ref[pair * 2 * PAGE : (pair + 1) * 2 * PAGE, :] = both


def fetch_pages(pages, kv):
    return pl.pallas_call(
        page_kernel,
        in_specs=[
            pl.BlockSpec(memory_space=pltpu.SMEM),
            pl.BlockSpec(memory_space=pl.ANY),
        ],
        out_shape=jax.ShapeDtypeStruct((PAGES * PAGE, 2 * HD), jnp.bfloat16),
        scratch_shapes=[
            pltpu.VMEM((PAGES, 2 * PAGE, 2 * HD), jnp.bfloat16),
            pltpu.SemaphoreType.DMA((PAGES,)),
        ],
        compiler_params=params(),
        name="pages",
    )(pages, kv)


def on_device(
    features,
    conv_weight,
    conv_bias,
    embed_weight,
    position_table,
    norm_gain,
    qkv_weight,
    page_owner,
    page_slot,
):
    me = lax.axis_index("seq").astype(jnp.int32)
    tensor = lax.axis_index("tensor").astype(jnp.int32)
    tensor_count = lax.axis_size("tensor")
    weight = lax.all_gather(qkv_weight, "seq", axis=0, tiled=True)
    parts = partial_latents(features, conv_weight)
    own = parts[: FRAMES * EXT].reshape(FRAMES, EXT * LAT)
    target = (page_owner * PAGES + page_slot).astype(jnp.float32)
    target = jnp.broadcast_to(target, (FRAMES, PAGES))
    message = jnp.concatenate([own, target], axis=1)
    message = jnp.pad(message, ((0, 0), (0, 512 - message.shape[1])))
    message = jnp.broadcast_to(message[:, None], (FRAMES, SEQ // FRAMES, 512)).reshape(SEQ, 512)
    message = lax.all_to_all(message, "seq", split_axis=0, concat_axis=0, tiled=True)
    targets = message[:, EXT * LAT : EXT * LAT + PAGES].astype(jnp.int32).reshape(-1)
    mine = me * PAGES + jnp.arange(PAGES, dtype=jnp.int32)
    index = jnp.arange(SEQ * PAGES, dtype=jnp.int32)
    pages = jnp.sum(jnp.where(targets[None, :] == mine[:, None], index[None, :], 0), axis=1)
    offset = tensor - me % (SEQ // FRAMES)
    latent = place_latents(message[:, : EXT * LAT].reshape(SEQ * EXT, LAT), offset)
    for bit in (1, 2, 4):
        swap = [(i, i ^ bit) for i in range(tensor_count)]
        latent = latent + lax.ppermute(latent, "tensor", swap)
    normed = normed_hidden(latent, conv_bias, embed_weight, position_table, norm_gain)
    qkv = jnp.dot(normed, weight, preferred_element_type=jnp.float32).astype(jnp.bfloat16)
    kv = lax.all_gather(qkv[:, GROUP * HD :], "seq", axis=0, tiled=True)
    attention = attend(me, qkv, kv)
    kv_cache = fetch_pages(pages, kv).reshape(PAGES, PAGE, 2, HD)
    return (attention, kv_cache)


def solution(mesh):
    placed = (
        P(None, "tensor", "seq", None),
        P(),
        P(),
        P(),
        P("seq", None),
        P(),
        P("seq", "tensor"),
        P("seq"),
        P("seq"),
    )
    return jax.shard_map(
        on_device,
        mesh=mesh,
        in_specs=placed,
        out_specs=(P("seq", "tensor"), P("seq", None, None, "tensor")),
        check_vma=False,
    )
```

time: 359 us -> 199 us (0.55)
  matrix products: 59.3 us -> 6.92 us
  Pallas kernels: 0 us -> 48.5 us
  blocking collectives: 40.7 us -> 0 us
  local copies, waits for them, and re-layouts: 48.3 us -> 8.9 us
  starting transfers between devices: 43.1 us -> 17.5 us
  other arithmetic: 26.1 us -> 3.61 us
  loops' own time: 14.4 us -> 0 us
  waiting for transfers between devices: 106 us -> 96.3 us
    dot_general x21 -> x1, matrix products: 59.3 us -> 6.92 us  [on_device(): jnp.dot(normed, weight, preferred_element_type=jnp.float32)]
    pallas_call x0 -> x5, Pallas kernels: none -> 48.5 us  [the longest x1 31.8 us: attend(): pl.pallas_call(attention_kernel, grid_spec=pltpu.PrefetchScalarGridSpec(n...]
    all_gather x1 -> x0, blocking collectives: 40.7 us -> none  [on_device(): latent = lax.all_gather(local_latent, 'tensor', axis=1, tiled=True)]
    unnamed x41 -> x4, local copies, waits for them, and re-layouts: 21.1 us -> 1.72 us
    all_to_all x3 -> x1, starting transfers between devices: 27.7 us -> 9.27 us  [on_device(): lax.all_to_all(message, 'seq', split_axis=0, concat_axis=0, tiled=True)]
    reduce_sum x10 -> x1, other arithmetic: 16.6 us -> 0.79 us  [on_device(): jnp.sum(jnp.where(targets[None, :] == mine[:, None], index[None, :], 0),...]
    another operation x11 -> x0, loops' own time: 14.4 us -> none  [the longest x1 13.9 us: on_device(): lax.scan(step, state, (jnp.arange(length // block, dtype=jnp.int32), key_...]
    all_to_all x3 -> x1, waiting for transfers between devices: 18 us -> 3.86 us  [on_device(): lax.all_to_all(message, 'seq', split_axis=0, concat_axis=0, tiled=True)]
  transfers between devices with their start and end apart: 10 -> 6, of which waited for: 6 -> 5; matrix products, arithmetic and copies ran while one was open for 15% -> 5% of each run, Pallas kernels for 0% -> 7%
where the time goes in v1:
time: 199 us; the launch traced here: 196 us
  waiting for transfers between devices  96.3 us (48%)
  Pallas kernels  48.5 us (24%)
  starting transfers between devices  17.5 us (9%)
  between operations  14.1 us (7%)
  local copies, waits for them, and re-layouts  8.9 us (4%)
  matrix products  6.92 us (3%)
  other arithmetic  3.61 us (2%)
    all_gather x1, waiting for transfers between devices, on_device(): kv = lax.all_gather(qkv[:, GROUP * HD:], 'seq', axis=0, tiled=True)  63 us
    pallas_call x1, Pallas kernels, attend(): pl.pallas_call(attention_kernel, grid_spec=pltpu.PrefetchScalarGridSpec(n...  31.8 us
    all_gather x1, waiting for transfers between devices, on_device(): weight = lax.all_gather(qkv_weight, 'seq', axis=0, tiled=True)  24.1 us
    all_to_all x1, starting transfers between devices, on_device(): lax.all_to_all(message, 'seq', split_axis=0, concat_axis=0, tiled=True)  9.27 us
    pallas_call x1, Pallas kernels, normed_hidden(): pl.pallas_call(hidden_kernel, grid=(steps,), in_specs=[pl.BlockSpec((LAT,...  9.19 us
    ppermute x3, starting transfers between devices, on_device(): latent = latent + lax.ppermute(latent, 'tensor', swap)  8.17 us
    dot_general x1, matrix products, on_device(): jnp.dot(normed, weight, preferred_element_type=jnp.float32)  6.92 us
    ppermute x3, waiting for transfers between devices, on_device(): latent = latent + lax.ppermute(latent, 'tensor', swap)  4.6 us
  transfers between devices with their start and end apart: 6, of which 5 were waited for; matrix products, arithmetic and copies ran while one was open for 5% of the time, Pallas kernels for 7%

profile of v1, /device:TPU:25, one launch (start us, length us, event | category | flops | bytes accessed | tf_op | source)
XLA Modules:
  0.0 195.8 jit_solution(1691962191395040134)
XLA Ops:
  7.2 0.0 all-gather.3.cloned.1.call-start
  7.2 0.7 all-gather.3.cloned.1.call-update
  7.9 2.2 %conv.1 = f32[128,16]{1,0:T(8,128)} custom-call(bf16[4,5,2,512]{3,2,1,0:T(2,128)(2,1)} %feat_ref.1, bf16[432,512]{1,0:T(8,128)(2,1)} %bitcast.15), custom_call_target="tpu_custom_call" | custom-call | tf_op jit(solution)/shard_map/conv/pallas_call | solution.py:68
  10.1 0.8 slice.16
  10.9 0.1 reshape.52
  11.0 0.7 add_convert_fusion
  11.7 0.1 pad.6.clone
  11.8 0.7 all_to_all.8
  12.5 9.3 %all-to-all-start = ((f32[32,1,512]{2,1,0:T(1,128)}), f32[32,1,512]{2,1,0:T(1,128)S(1)}, u32[]{:S(2)}, u32[]{:S(2)}) async-start(f32[32,1,512]{2,1,0:T(1,128)} %all_to_all.8), calls=%async_computation | async-start | bytes 131072 | tf_op jit(solution)/shard_map/all_to_all | solution.py:333
  21.8 0.0 all-gather.5.cloned.1.call-start
  21.8 0.7 fusion
  22.5 1.0 copy.20.token_ref
  23.6 3.9 %all-to-all-done = f32[32,1,512]{2,1,0:T(1,128)S(1)} async-done(((f32[32,1,512]{2,1,0:T(1,128)}), f32[32,1,512]{2,1,0:T(1,128)S(1)}, u32[]{:S(2)}, u32[]{:S(2)}) %all-to-all-start) | async-done | bytes 65568 | tf_op jit(solution)/shard_map/all_to_all | solution.py:333
  27.4 1.0 reshape.53.parts_ref
  28.4 2.4 %place.1 = f32[16,384]{1,0:T(8,128)} custom-call(f32[896,16]{1,0:T(8,128)} %reshape.53.parts_ref, s32[896,1]{1,0:T(8,128)} %copy.20.token_ref), custom_call_target="tpu_custom_call" | custom-call | tf_op jit(solution)/shard_map/place/pallas_call | solution.py:114
  30.8 4.2 %collective-permute-start = (f32[16,384]{1,0:T(8,128)}, f32[16,384]{1,0:T(8,128)S(1)}, u32[]{:S(2)}, u32[]{:S(2)}) collective-permute-start(f32[16,384]{1,0:T(8,128)} %place.1), channel_id=1, source_target_pairs={{0,1},{1,0},{2,3},{3,2},{4,5},{5,4},{6,7},{7,6},{8,9},{9,8},{10,11... | collective-permute-start | bytes 73736 | tf_op jit(solution)/shard_map/ppermute | solution.py:342
  35.0 2.7 %collective-permute-done = f32[16,384]{1,0:T(8,128)S(1)} collective-permute-done((f32[16,384]{1,0:T(8,128)}, f32[16,384]{1,0:T(8,128)S(1)}, u32[]{:S(2)}, u32[]{:S(2)}) %collective-permute-start) | collective-permute-done | bytes 24608 | tf_op jit(solution)/shard_map/ppermute | solution.py:342
  37.8 0.7 add.36
  38.5 1.2 collective-permute-start.1
  39.7 1.9 collective-permute-done.1
  41.6 2.8 %collective-permute-start.2 = (f32[16,384]{1,0:T(8,128)S(1)}, f32[16,384]{1,0:T(8,128)S(1)}, u32[]{:S(2)}, u32[]{:S(2)}) collective-permute-start(f32[16,384]{1,0:T(8,128)S(1)} %add.37), channel_id=1, source_target_pairs={{0,4},{1,5},{2,6},{3,7},{4,0},{5,1},{6,2},{7,3},{8,12},{9,13},{10,... | collective-permute-start | bytes 73736 | tf_op jit(solution)/shard_map/ppermute | solution.py:342
  44.4 1.3 copy.21.bias_ref
  45.7 1.3 reshape.55.gain_ref
  47.0 0.0 collective-permute-done.2
  47.0 0.6 add.38.latent_ref
  47.6 9.2 %hidden.1 = bf16[320,5120]{1,0:T(8,128)(2,1)} custom-call(f32[16,384]{1,0:T(8,128)} %add.38.latent_ref, f32[16,1]{1,0:T(8,128)} %copy.21.bias_ref, bf16[16,5120]{1,0:T(8,128)(2,1)} %embed_ref.1, bf16[320,5120]{1,0:T(8,128)(2,1)} %table_ref.1, bf16[1,5120]{1,0:T(2,128)(2,1)} %reshape.55.gain_ref), custom_call_target="tpu_custom_call" | custom-call | tf_op jit(solution)/shard_map/hidden/pallas_call | solution.py:163
  56.8 24.1 %all-gather.3.cloned.1.call-done = bf16[5120,768]{1,0:T(8,128)(2,1)} async-done(((bf16[160,768]{1,0:T(8,128)(2,1)}), bf16[5120,768]{1,0:T(8,128)(2,1)}) %all-gather.3.cloned.1.call-update) | async-done | bytes 7864336 | tf_op jit(solution)/shard_map/all_gather | solution.py:325
  80.9 6.9 %convolution_convert_fusion.qkv_ref = bf16[320,768]{1,0:T(8,128)(2,1)S(1)} fusion(bf16[320,5120]{1,0:T(8,128)(2,1)} %hidden.1, bf16[5120,768]{1,0:T(8,128)(2,1)} %all-gather.3.cloned.1.call-done), kind=kOutput, calls=%fused_computation | convolution fusion | flops 2516828160 | bytes 11632640 | tf_op jit(solution)/shard_map/dot_general | solution.py:344
  87.9 0.0 copy-start
  87.9 0.7 slice.18
  88.6 0.0 all-gather.5.cloned.1.call-update
  88.6 0.1 slice_convert_fusion
  88.7 0.1 eq.17
  88.8 0.8 select_reduce_fusion.page_ref
  89.6 63.0 %all-gather.5.cloned.1.call-done.kv_ref = bf16[10240,256]{1,0:T(8,128)(2,1)} async-done(((bf16[320,256]{1,0:T(8,128)(2,1)}), bf16[10240,256]{1,0:T(8,128)(2,1)}) %all-gather.5.cloned.1.call-update) | async-done | bytes 5242896 | tf_op jit(solution)/shard_map/all_gather | solution.py:345
  152.6 2.9 %pages.1 = bf16[320,256]{1,0:T(8,128)(2,1)} custom-call(s32[40]{0:T(128)} %select_reduce_fusion.page_ref, bf16[10240,256]{1,0:T(8,128)(2,1)} %all-gather.5.cloned.1.call-done.kv_ref), custom_call_target="tpu_custom_call" | custom-call | tf_op jit(solution)/shard_map/pages/pallas_call | solution.py:295
  155.5 1.7 copy.22
  157.2 0.0 copy-done
  157.2 31.8 %attend.1 = bf16[320,512]{1,0:T(8,128)(2,1)} custom-call(s32[1]{0:T(128)} %bitcast.me_ref, bf16[320,768]{1,0:T(8,128)(2,1)} %copy-done, bf16[10240,256]{1,0:T(8,128)(2,1)} %all-gather.5.cloned.1.call-done.kv_ref), custom_call_target="tpu_custom_call" | custom-call | tf_op jit(solution)/shard_map/attend/pallas_call | solution.py:248
  (6 shorter events, 0.0 us)
Async XLA Ops:
  7.2 73.8 %all-gather.3.cloned.1.call-start = ((), (), s32[]{:S(2)}) async-start(), calls=%async_computation.1 | async-start | bytes 8110080 | tf_op jit(solution)/shard_map/all_gather | solution.py:325
  12.5 14.9 %all-to-all-start = ((f32[32,1,512]{2,1,0:T(1,128)}), f32[32,1,512]{2,1,0:T(1,128)S(1)}, u32[]{:S(2)}, u32[]{:S(2)}) async-start(f32[32,1,512]{2,1,0:T(1,128)} %all_to_all.8), calls=%async_computation | async-start | bytes 131072 | tf_op jit(solution)/shard_map/all_to_all | solution.py:333
  21.8 130.8 %all-gather.5.cloned.1.call-start = ((), (), s32[]{:S(2)}) async-start(), calls=%async_computation.2 | async-start | bytes 5406720 | tf_op jit(solution)/shard_map/all_gather | solution.py:345
  30.8 6.9 %collective-permute-start = (f32[16,384]{1,0:T(8,128)}, f32[16,384]{1,0:T(8,128)S(1)}, u32[]{:S(2)}, u32[]{:S(2)}) collective-permute-start(f32[16,384]{1,0:T(8,128)} %place.1), channel_id=1, source_target_pairs={{0,1},{1,0},{2,3},{3,2},{4,5},{5,4},{6,7},{7,6},{8,9},{9,8},{10,11... | collective-permute-start | bytes 73736 | tf_op jit(solution)/shard_map/ppermute | solution.py:342
  38.5 3.1 %collective-permute-start.1 = (f32[16,384]{1,0:T(8,128)S(1)}, f32[16,384]{1,0:T(8,128)S(1)}, u32[]{:S(2)}, u32[]{:S(2)}) collective-permute-start(f32[16,384]{1,0:T(8,128)S(1)} %add.36), channel_id=1, source_target_pairs={{0,2},{1,3},{2,0},{3,1},{4,6},{5,7},{6,4},{7,5},{8,10},{9,11},{10,... | collective-permute-start | bytes 73736 | tf_op jit(solution)/shard_map/ppermute | solution.py:342
  41.6 5.4 %collective-permute-start.2 = (f32[16,384]{1,0:T(8,128)S(1)}, f32[16,384]{1,0:T(8,128)S(1)}, u32[]{:S(2)}, u32[]{:S(2)}) collective-permute-start(f32[16,384]{1,0:T(8,128)S(1)} %add.37), channel_id=1, source_target_pairs={{0,4},{1,5},{2,6},{3,7},{4,0},{5,1},{6,2},{7,3},{8,12},{9,13},{10,... | collective-permute-start | bytes 73736 | tf_op jit(solution)/shard_map/ppermute | solution.py:342
  87.9 69.3 %copy-start = (bf16[320,768]{1,0:T(8,128)(2,1)}, bf16[320,768]{1,0:T(8,128)(2,1)S(1)}, u32[]{:S(2)}) copy-start(bf16[320,768]{1,0:T(8,128)(2,1)S(1)} %convolution_convert_fusion.qkv_ref) | copy-start | bytes 1474564
Sparse Core Ops, SparseCore 0:
  9.9 71.0 all-gather.2
  88.7 63.7 all-gather.4

commit v2 on v1

--- a/solution.py
+++ b/solution.py
@@ -20,14 +20,19 @@
 FRAMES = 4
 EXT = (ROWS + 2) * (COLS + 2)
 TOK = 384
-CHUNK = 1280
 TILE = 256
 QROWS = GROUP * BLK
-VMEM = 56 * 1024 * 1024
+STATE = HD + 8
+VMEM = 24 * 1024 * 1024
 
 
 def params(**extra):
     return pltpu.CompilerParams(vmem_limit_bytes=VMEM, **extra)
+
+
+def cost(blocks):
+    scores = blocks * 2 * QROWS * BLK
+    return pl.CostEstimate(flops=4 * HD * scores, bytes_accessed=3 << 20, transcendentals=scores)
 
 
 def roll_lanes(value, shift):
@@ -181,131 +186,298 @@
     )(latent, conv_bias.reshape(LAT, 1), embed_weight, position_table, norm_gain.reshape(1, depth))
 
 
-def attend_chunk(masked, first_key, first_query, q_ref, kv_ref, best_ref, total_ref, sum_ref):
+def attend_block(masked, partner_full, keys, values, q_ref, state_ref):
     scale = 1.4426950408889634 / HD**0.5
-    keys = kv_ref[:, :HD]
-    values = kv_ref[:, HD:]
-    for start in range(0, QROWS, TILE):
-        cut = slice(start, start + TILE)
-        scores = lax.dot_general(
-            keys, q_ref[cut, :], (((1,), (1,)), ((), ())), preferred_element_type=jnp.float32
+    tiles = 2 * QROWS // TILE
+
+    def score(tile):
+        return lax.dot_general(
+            keys,
+            q_ref[tile * TILE : (tile + 1) * TILE, :],
+            (((1,), (1,)), ((), ())),
+            preferred_element_type=jnp.float32,
         )
+
+    upcoming = score(0)
+    for tile in range(tiles):
+        scores = upcoming
+        if tile + 1 < tiles:
+            upcoming = score(tile + 1)
+        cut = slice(tile * TILE, (tile + 1) * TILE)
+        allowed = None
         if masked:
-            key = first_key + lax.broadcasted_iota(jnp.int32, scores.shape, 0)
-            query = start + lax.broadcasted_iota(jnp.int32, (1, TILE), 1)
-            for head in range(GROUP - 1, 0, -1):
-                query = jnp.where(query >= head * BLK, query - head * BLK, query)
-            scores = jnp.where(key <= first_query + query, scores, -1e30)
-        old = best_ref[:, cut]
-        best = jnp.maximum(old, jnp.max(scores, axis=0, keepdims=True))
-        factor = jnp.exp2((old - best) * scale)
+            key = lax.broadcasted_iota(jnp.int32, scores.shape, 0)
+            query = tile * TILE + lax.broadcasted_iota(jnp.int32, (1, TILE), 1)
+            if tile * TILE >= QROWS:
+                query = jnp.where(partner_full, BLK, -1) + 0 * query
+            else:
+                for head in range(GROUP - 1, 0, -1):
+                    query = jnp.where(query >= head * BLK, query - head * BLK, query)
+            allowed = key <= query
+            scores = jnp.where(allowed, scores, -1e30)
+        peak = jnp.max(scores, axis=0, keepdims=True)
+        if masked:
+            best = peak
+        else:
+            old = state_ref[HD : HD + 1, cut]
+            best = jnp.maximum(old, peak)
+            factor = jnp.exp2((old - best) * scale)
         weights = jnp.exp2((scores - best) * scale)
-        best_ref[:, cut] = best
-        total_ref[:, cut] = total_ref[:, cut] * factor + jnp.sum(weights, axis=0, keepdims=True)
-        sum_ref[:, cut] = sum_ref[:, cut] * factor + lax.dot_general(
+        if masked:
+            weights = jnp.where(allowed, weights, 0.0)
+        total = jnp.sum(weights, axis=0, keepdims=True)
+        summed = lax.dot_general(
             values,
             weights.astype(jnp.bfloat16),
             (((0,), (0,)), ((), ())),
             preferred_element_type=jnp.float32,
         )
-
-
-def attention_kernel(me_ref, qkv_ref, kv_ref, out_ref, q_ref, best_ref, total_ref, sum_ref, row_ref):
-    step = pl.program_id(0)
-    me = me_ref[0]
-    mine = me // (CHUNK // BLK)
-
-    @pl.when(step == 0)
-    def _():
-        best_ref[...] = jnp.full_like(best_ref, -1e30)
-        total_ref[...] = jnp.zeros_like(total_ref)
-        sum_ref[...] = jnp.zeros_like(sum_ref)
+        if not masked:
+            total = total + state_ref[HD + 1 : HD + 2, cut] * factor
+            summed = summed + state_ref[:HD, cut] * factor
+        state_ref[HD : HD + 1, cut] = best
+        state_ref[HD + 1 : HD + 2, cut] = total
+        state_ref[:HD, cut] = summed
+
+
+def set_queries(own_ref, pair_ref, q_ref):
+    for index, ref in enumerate((own_ref, pair_ref)):
         for head in range(GROUP):
-            q_ref[head * BLK : (head + 1) * BLK, :] = qkv_ref[:, head * HD : (head + 1) * HD]
-
-    state = (q_ref, kv_ref, best_ref, total_ref, sum_ref)
-
-    @pl.when(step < mine)
-    def _():
-        attend_chunk(False, 0, 0, *state)
-
-    @pl.when(step == mine)
-    def _():
-        attend_chunk(True, step * CHUNK, me * BLK, *state)
-
-    @pl.when(step == pl.num_programs(0) - 1)
-    def _():
-        for start in range(0, QROWS, TILE):
-            cut = slice(start, start + TILE)
-            row_ref[cut, :] = jnp.transpose(sum_ref[:, cut] / total_ref[:, cut])
-        for head in range(GROUP):
-            rows = row_ref[head * BLK : (head + 1) * BLK, :]
-            out_ref[:, head * HD : (head + 1) * HD] = rows.astype(jnp.bfloat16)
-
-
-def attend(me, qkv, kv):
-    steps = kv.shape[0] // CHUNK
-    return pl.pallas_call(
-        attention_kernel,
-        grid_spec=pltpu.PrefetchScalarGridSpec(
-            num_scalar_prefetch=1,
-            grid=(steps,),
-            in_specs=[
-                pl.BlockSpec(qkv.shape, lambda i, me: (0, 0)),
-                pl.BlockSpec(
-                    (CHUNK, 2 * HD), lambda i, me: (jnp.minimum(i, me[0] // (CHUNK // BLK)), 0)
-                ),
-            ],
-            out_specs=pl.BlockSpec((BLK, GROUP * HD), lambda i, me: (0, 0)),
-            scratch_shapes=[
-                pltpu.VMEM((QROWS, HD), jnp.bfloat16),
-                pltpu.VMEM((1, QROWS), jnp.float32),
-                pltpu.VMEM((1, QROWS), jnp.float32),
-                pltpu.VMEM((HD, QROWS), jnp.float32),
-                pltpu.VMEM((QROWS, HD), jnp.float32),
-            ],
-        ),
+            start = (index * GROUP + head) * BLK
+            q_ref[start : start + BLK, :] = ref[:, head * HD : (head + 1) * HD]
+
+
+def first_kernel(core_ref, own_ref, pair_ref, kv_ref, state_ref, q_ref):
+    set_queries(own_ref, pair_ref, q_ref)
+    state_ref[HD + 2 :, :] = jnp.zeros((STATE - HD - 2, 2 * QROWS), jnp.float32)
+    attend_block(True, core_ref[0] == 0, kv_ref[:, :HD], kv_ref[:, HD:], q_ref, state_ref)
+
+
+def attend_first(core, own, pair, kv):
+    return pl.pallas_call(
+        first_kernel,
+        in_specs=[pl.BlockSpec(memory_space=pltpu.SMEM)]
+        + [pl.BlockSpec(memory_space=pltpu.VMEM)] * 3,
+        out_shape=jax.ShapeDtypeStruct((STATE, 2 * QROWS), jnp.float32),
+        scratch_shapes=[pltpu.VMEM((2 * QROWS, HD), jnp.bfloat16)],
+        compiler_params=params(),
+        cost_estimate=cost(1),
+        name="first",
+    )(core.reshape(1), own, pair, kv)
+
+
+def more_kernel(sizes, split, flag_ref, own_ref, pair_ref, state_ref, *rest):
+    arrays, rest = rest[: len(sizes)], rest[len(sizes) :]
+    if split:
+        own_out_ref, pair_out_ref, q_ref, held_ref, sems, work_ref = rest
+    else:
+        work_ref, q_ref, held_ref, sems = rest
+    copies = []
+    first = 0
+    for index, size in enumerate(sizes):
+        copies.append(
+            pltpu.make_async_copy(
+                arrays[index], held_ref.at[pl.ds(first, size * BLK), :], sems.at[index]
+            )
+        )
+        copies[-1].start()
+        first += size * BLK
+    set_queries(own_ref, pair_ref, q_ref)
+    work_ref[...] = state_ref[...]
+    for copy in copies:
+        copy.wait()
+
+    def body(index, carry):
+        @pl.when(flag_ref[index] != 0)
+        def _():
+            rows = pl.ds(pl.multiple_of(index * BLK, BLK), BLK)
+            attend_block(False, None, held_ref[rows, :HD], held_ref[rows, HD:], q_ref, work_ref)
+
+        return carry
+
+    lax.fori_loop(0, sum(sizes), body, 0)
+    if split:
+        own_out_ref[...] = work_ref[:, :QROWS]
+        pair_out_ref[...] = work_ref[:, QROWS:]
+
+
+def attend_more(flags, own, pair, state, arrays, split=False):
+    sizes = tuple(array.shape[0] // BLK for array in arrays)
+    half = jax.ShapeDtypeStruct((STATE, QROWS), jnp.float32)
+    whole = jax.ShapeDtypeStruct((STATE, 2 * QROWS), jnp.float32)
+    scratch = [
+        pltpu.VMEM((2 * QROWS, HD), jnp.bfloat16),
+        pltpu.VMEM((sum(sizes) * BLK, 2 * HD), jnp.bfloat16),
+        pltpu.SemaphoreType.DMA((len(sizes),)),
+    ]
+    if split:
+        scratch.append(pltpu.VMEM((STATE, 2 * QROWS), jnp.float32))
+    return pl.pallas_call(
+        functools.partial(more_kernel, sizes, split),
+        in_specs=[pl.BlockSpec(memory_space=pltpu.SMEM)]
+        + [pl.BlockSpec(memory_space=pltpu.VMEM)] * 3
+        + [pl.BlockSpec(memory_space=pl.ANY)] * len(sizes),
+        out_shape=(half, half) if split else whole,
+        scratch_shapes=scratch,
+        compiler_params=params(),
+        cost_estimate=cost(sum(sizes)),
+        name="more",
+    )(flags, own, pair, state, *arrays)
+
+
+def finish_kernel(own_ref, got_ref, out_ref, row_ref):
+    scale = 1.4426950408889634 / HD**0.5
+    for start in range(0, QROWS, TILE):
+        cut = slice(start, start + TILE)
+        first, second = own_ref[HD : HD + 1, cut], got_ref[HD : HD + 1, cut]
+        best = jnp.maximum(first, second)
+        first = jnp.exp2((first - best) * scale)
+        second = jnp.exp2((second - best) * scale)
+        total = own_ref[HD + 1 : HD + 2, cut] * first + got_ref[HD + 1 : HD + 2, cut] * second
+        summed = own_ref[:HD, cut] * first + got_ref[:HD, cut] * second
+        row_ref[cut, :] = jnp.transpose(summed / total)
+    for head in range(GROUP):
+        rows = row_ref[head * BLK : (head + 1) * BLK, :]
+        out_ref[:, head * HD : (head + 1) * HD] = rows.astype(jnp.bfloat16)
+
+
+def finish(own, got):
+    return pl.pallas_call(
+        finish_kernel,
         out_shape=jax.ShapeDtypeStruct((BLK, GROUP * HD), jnp.bfloat16),
-        compiler_params=params(dimension_semantics=("arbitrary",)),
-        name="attend",
-    )(me.reshape(1), qkv, kv)
-
-
-def page_kernel(page_ref, kv_ref, out_ref, held_ref, sems):
-    def copy(slot):
-        first = pl.multiple_of((page_ref[slot] // 2) * 2 * PAGE, 2 * PAGE)
-        return pltpu.make_async_copy(
-            kv_ref.at[pl.ds(first, 2 * PAGE), :], held_ref.at[slot], sems.at[slot]
-        )
-
-    for slot in range(PAGES):
-        copy(slot).start()
-    for pair in range(PAGES // 2):
+        scratch_shapes=[pltpu.VMEM((QROWS, HD), jnp.float32)],
+        compiler_params=params(),
+        name="finish",
+    )(own, got)
+
+
+def page_kernel(code_ref, row_ref, odd_ref, *rest):
+    arrays, (own_ref, pair_ref, held_ref, sems) = rest[:-4], rest[-4:]
+    count = 2 * PAGES
+
+    def start(slot, carry):
+        row = pl.multiple_of(row_ref[slot], 2 * PAGE)
+        for index, array in enumerate(arrays):
+
+            @pl.when(code_ref[slot] == index)
+            def _():
+                pltpu.make_async_copy(
+                    array.at[pl.ds(row, 2 * PAGE), :], held_ref.at[slot], sems.at[slot]
+                ).start()
+
+        return carry
+
+    lax.fori_loop(0, count, start, 0)
+    for pair in range(count // 2):
         halves = []
         for slot in (2 * pair, 2 * pair + 1):
-            copy(slot).wait()
+            pltpu.make_async_copy(
+                arrays[0].at[pl.ds(0, 2 * PAGE), :], held_ref.at[slot], sems.at[slot]
+            ).wait()
             rows = held_ref[slot].astype(jnp.float32)
-            odd = page_ref[slot] % 2 == 1
-            halves.append(jnp.where(odd, rows[PAGE:], rows[:PAGE]))
+            halves.append(jnp.where(odd_ref[slot] == 1, rows[PAGE:], rows[:PAGE]))
         both = jnp.concatenate(halves, axis=0).astype(jnp.bfloat16)
-        out_ref[pair * 2 * PAGE : (pair + 1) * 2 * PAGE, :] = both
-
-
-def fetch_pages(pages, kv):
+        out_ref = own_ref if 2 * pair < PAGES else pair_ref
+        place = (2 * pair % PAGES) * PAGE
+        out_ref[place : place + 2 * PAGE, :] = both
+
+
+def fetch_pages(code, row, odd, arrays):
+    out = jax.ShapeDtypeStruct((PAGES * PAGE, 2 * HD), jnp.bfloat16)
     return pl.pallas_call(
         page_kernel,
-        in_specs=[
-            pl.BlockSpec(memory_space=pltpu.SMEM),
-            pl.BlockSpec(memory_space=pl.ANY),
-        ],
-        out_shape=jax.ShapeDtypeStruct((PAGES * PAGE, 2 * HD), jnp.bfloat16),
+        in_specs=[pl.BlockSpec(memory_space=pltpu.SMEM)] * 3
+        + [pl.BlockSpec(memory_space=pl.ANY)] * len(arrays),
+        out_shape=(out, out),
         scratch_shapes=[
-            pltpu.VMEM((PAGES, 2 * PAGE, 2 * HD), jnp.bfloat16),
-            pltpu.SemaphoreType.DMA((PAGES,)),
+            pltpu.VMEM((2 * PAGES, 2 * PAGE, 2 * HD), jnp.bfloat16),
+            pltpu.SemaphoreType.DMA((2 * PAGES,)),
         ],
         compiler_params=params(),
         name="pages",
-    )(pages, kv)
+    )(code, row, odd, *arrays)
+
+
+def moves(step):
+    pairs = []
+    for y in range(4):
+        for z in range(4):
+            for core in range(2):
+                to_y, to_z, to_core = step(y, z, core)
+                pairs.append(((y * 4 + z) * 2 + core, (to_y * 4 + to_z) * 2 + to_core))
+    return pairs
+
+
+def along_y(value, count):
+    return lax.ppermute(value, "seq", moves(lambda y, z, c: ((y + count) % 4, z, c)))
+
+
+def along_z(value, count):
+    return lax.ppermute(value, "seq", moves(lambda y, z, c: (y, (z + count) % 4, c)))
+
+
+def other_core(value):
+    return lax.ppermute(value, "seq", moves(lambda y, z, c: (y, z, 1 - c)))
+
+
+def pages_of(targets, owner):
+    mine = owner * PAGES + jnp.arange(PAGES, dtype=jnp.int32)
+    index = jnp.arange(SEQ * PAGES, dtype=jnp.int32)
+    return jnp.sum(jnp.where(targets[None, :] == mine[:, None], index[None, :], 0), axis=1)
+
+
+def attention_and_pages(me, targets, qkv):
+    core, z, y = me % 2, (me // 2) % 4, me // 8
+    queries, kv = qkv[:, : GROUP * HD], qkv[:, GROUP * HD :]
+    pair = other_core(queries)
+    by_z = {0: kv}
+    for count in (1, 2, 3):
+        by_z[count] = along_z(kv, count)
+    zero = {count: along_y(kv, count) for count in (1, 3, 2)}
+    one = {count: along_y(by_z[1], count) for count in (1, 3, 2)}
+    last = jnp.concatenate([by_z[2], by_z[3]], axis=0)
+    rest = {count: along_y(last, count) for count in (1, 3, 2)}
+
+    def flag(*conditions):
+        return jnp.stack([jnp.asarray(value, jnp.int32) for value in conditions])
+
+    state = attend_first(core, queries, pair, kv)
+    state = attend_more(
+        flag(z >= 1, z >= 2, z >= 3, y >= 1, y >= 2, y >= 3),
+        queries,
+        pair,
+        state,
+        [by_z[1], by_z[2], by_z[3], zero[1], zero[2], zero[3]],
+    )
+    state = attend_more(
+        flag(y >= 1, y >= 2, y >= 3), queries, pair, state, [one[1], one[2], one[3]]
+    )
+    state = attend_more(
+        flag(y >= 1, y >= 1, y >= 3, y >= 3), queries, pair, state, [rest[1], rest[3]]
+    )
+    own, sent = attend_more(
+        flag(y >= 2, y >= 2), queries, pair, state, [rest[2]], split=True
+    )
+    got = other_core(sent)
+
+    page = jnp.concatenate([pages_of(targets, me), pages_of(targets, me ^ 1)])
+    source = page // PAGES
+    by_y = (y - source // 8) % 4
+    by_zz = (z - (source // 2) % 4) % 4
+    held = source % 2 == core
+    code = jnp.where(by_y == 0, by_zz, jnp.minimum(by_zz, 2) * 3 + 3 + by_y)
+    offset = jnp.where((by_y > 0) & (by_zz == 3), BLK, 0)
+    row = offset + (page % PAGES) // 2 * 2 * PAGE
+    arrays = [by_z[count] for count in range(4)]
+    for group in (zero, one, rest):
+        arrays += [group[count] for count in (1, 2, 3)]
+    own_pages, sent_pages = fetch_pages(code, row, page % 2, arrays)
+    got_pages = other_core(sent_pages)
+    attention = finish(own, got)
+    keep = held[:PAGES].reshape(PAGES, 1, 1, 1)
+    shape = (PAGES, PAGE, 2, HD)
+    kv_cache = jnp.where(keep, own_pages.reshape(shape), got_pages.reshape(shape))
+    return attention, kv_cache
 
 
 def on_device(
@@ -332,9 +504,6 @@
     message = jnp.broadcast_to(message[:, None], (FRAMES, SEQ // FRAMES, 512)).reshape(SEQ, 512)
     message = lax.all_to_all(message, "seq", split_axis=0, concat_axis=0, tiled=True)
     targets = message[:, EXT * LAT : EXT * LAT + PAGES].astype(jnp.int32).reshape(-1)
-    mine = me * PAGES + jnp.arange(PAGES, dtype=jnp.int32)
-    index = jnp.arange(SEQ * PAGES, dtype=jnp.int32)
-    pages = jnp.sum(jnp.where(targets[None, :] == mine[:, None], index[None, :], 0), axis=1)
     offset = tensor - me % (SEQ // FRAMES)
     latent = place_latents(message[:, : EXT * LAT].reshape(SEQ * EXT, LAT), offset)
     for bit in (1, 2, 4):
@@ -342,10 +511,7 @@
         latent = latent + lax.ppermute(latent, "tensor", swap)
     normed = normed_hidden(latent, conv_bias, embed_weight, position_table, norm_gain)
     qkv = jnp.dot(normed, weight, preferred_element_type=jnp.float32).astype(jnp.bfloat16)
-    kv = lax.all_gather(qkv[:, GROUP * HD :], "seq", axis=0, tiled=True)
-    attention = attend(me, qkv, kv)
-    kv_cache = fetch_pages(pages, kv).reshape(PAGES, PAGE, 2, HD)
-    return (attention, kv_cache)
+    return attention_and_pages(me, targets, qkv)
 
 
 def solution(mesh):

time: 199 us -> 173 us (0.87); the launches traced: 196 us -> 173 us
  waiting for transfers between devices: 96.3 us -> 56.5 us
  starting transfers between devices: 17.5 us -> 34.7 us
  local copies, waits for them, and re-layouts: 8.9 us -> 11.4 us
  Pallas kernels: 48.5 us -> 46.2 us
    all_gather x1 -> x0, waiting for transfers between devices: 63 us -> none  [on_device(): kv = lax.all_gather(qkv[:, GROUP * HD:], 'seq', axis=0, tiled=True)]
    ppermute x0 -> x15, waiting for transfers between devices: none -> 19.6 us  [the longest x3 9.81 us: along_z(): lax.ppermute(value, 'seq', moves(lambda y, z, c: (y, (z + count) % 4, c)))]
    ppermute x0 -> x15, starting transfers between devices: none -> 17.2 us  [the longest x9 11.4 us: along_y(): lax.ppermute(value, 'seq', moves(lambda y, z, c: ((y + count) % 4, z, c)))]
    pallas_call x1, Pallas kernels: 2.89 us -> 11.8 us  [fetch_pages(): pl.pallas_call(page_kernel, in_specs=[pl.BlockSpec(memory_space=pltpu.SME...]
    unnamed x4 -> x16, local copies, waits for them, and re-layouts: 1.72 us -> 6.81 us
    pallas_call x1, Pallas kernels: 9.19 us -> 4.75 us  [normed_hidden(): pl.pallas_call(hidden_kernel, grid=(steps,), in_specs=[pl.BlockSpec((LAT,...]
    all_gather x1, waiting for transfers between devices: 24.1 us -> 28.4 us  [on_device(): weight = lax.all_gather(qkv_weight, 'seq', axis=0, tiled=True)]
    pallas_call x1 -> x6, Pallas kernels: 31.8 us -> 28.5 us  [the longest x4 25.6 us: attend_more(): pl.pallas_call(functools.partial(more_kernel, sizes, split), in_specs=[pl...]
  transfers between devices with their start and end apart: 6 -> 20, of which waited for: 5 -> 10; matrix products, arithmetic and copies ran while one was open for 5% -> 4% of each run, Pallas kernels for 7% -> 24%
where the time goes in v2:
time: 173 us
  waiting for transfers between devices  56.5 us (33%)
  Pallas kernels  46.2 us (27%)
  starting transfers between devices  34.7 us (20%)
  between operations  14.3 us (8%)
  local copies, waits for them, and re-layouts  11.4 us (7%)
  matrix products  6.92 us (4%)
  other arithmetic  2.97 us (2%)
    all_gather x1, waiting for transfers between devices, on_device(): weight = lax.all_gather(qkv_weight, 'seq', axis=0, tiled=True)  28.4 us
    pallas_call x4, Pallas kernels, attend_more(): pl.pallas_call(functools.partial(more_kernel, sizes, split), in_specs=[pl...  25.6 us
    pallas_call x1, Pallas kernels, fetch_pages(): pl.pallas_call(page_kernel, in_specs=[pl.BlockSpec(memory_space=pltpu.SME...  11.8 us
    ppermute x9, starting transfers between devices, along_y(): lax.ppermute(value, 'seq', moves(lambda y, z, c: ((y + count) % 4, z, c)))  11.4 us
    ppermute x3, waiting for transfers between devices, along_z(): lax.ppermute(value, 'seq', moves(lambda y, z, c: (y, (z + count) % 4, c)))  9.81 us
    all_to_all x1, starting transfers between devices, on_device(): lax.all_to_all(message, 'seq', split_axis=0, concat_axis=0, tiled=True)  9.26 us
    ppermute x9, waiting for transfers between devices, along_y(): lax.ppermute(value, 'seq', moves(lambda y, z, c: ((y + count) % 4, z, c)))  8.38 us
    ppermute x3, starting transfers between devices, on_device(): latent = latent + lax.ppermute(latent, 'tensor', swap)  8.19 us
  transfers between devices with their start and end apart: 20, of which 10 were waited for; matrix products, arithmetic and copies ran while one was open for 4% of the time, Pallas kernels for 24%

profile of v2, /device:TPU:25, one launch (start us, length us, event | category | flops | bytes accessed | tf_op | source)
XLA Modules:
  0.0 173.0 jit_solution(17615436298877732520)
XLA Ops:
  7.2 0.7 all-gather.2.cloned.1.call-update
  7.9 1.2 copy-done.4
  9.2 0.8 copy-done.6
  9.9 0.5 conv.1
  10.5 0.1 reshape.60
  10.6 0.7 add_convert_fusion
  11.2 0.1 pad.15.clone
  11.4 0.7 all_to_all.8
  12.1 9.3 %all-to-all-start = ((f32[32,1,512]{2,1,0:T(1,128)}), f32[32,1,512]{2,1,0:T(1,128)S(1)}, u32[]{:S(2)}, u32[]{:S(2)}) async-start(f32[32,1,512]{2,1,0:T(1,128)} %all_to_all.8), calls=%async_computation | async-start | bytes 131072 | tf_op jit(solution)/shard_map/all_to_all | solution.py:505
  21.4 0.7 fusion
  22.1 0.1 pad_add_fusion.1.flag_ref
  22.1 1.1 copy.24.token_ref
  23.2 3.8 %all-to-all-done = f32[32,1,512]{2,1,0:T(1,128)S(1)} async-done(((f32[32,1,512]{2,1,0:T(1,128)}), f32[32,1,512]{2,1,0:T(1,128)S(1)}, u32[]{:S(2)}, u32[]{:S(2)}) %all-to-all-start) | async-done | bytes 65568 | tf_op jit(solution)/shard_map/all_to_all | solution.py:505
  27.0 1.0 reshape.61.parts_ref
  28.0 1.0 copy-done.2
  29.0 1.0 copy-done.3
  30.1 0.6 place.1
  30.7 4.3 %collective-permute-start = (f32[16,384]{1,0:T(8,128)S(1)}, f32[16,384]{1,0:T(8,128)S(1)}, u32[]{:S(2)}, u32[]{:S(2)}) collective-permute-start(f32[16,384]{1,0:T(8,128)S(1)} %place.1), channel_id=1, source_target_pairs={{0,1},{1,0},{2,3},{3,2},{4,5},{5,4},{6,7},{7,6},{8,9},{9,8},{10,11... | collective-permute-start | bytes 73736 | tf_op jit(solution)/shard_map/ppermute | solution.py:511
  34.9 0.1 pad_add_fusion.2.flag_ref
  35.0 2.6 %collective-permute-done = f32[16,384]{1,0:T(8,128)S(1)} collective-permute-done((f32[16,384]{1,0:T(8,128)S(1)}, f32[16,384]{1,0:T(8,128)S(1)}, u32[]{:S(2)}, u32[]{:S(2)}) %collective-permute-start) | collective-permute-done | bytes 24608 | tf_op jit(solution)/shard_map/ppermute | solution.py:511
  37.6 1.2 collective-permute-start.1
  38.8 0.1 pad_add_fusion.flag_ref
  38.9 0.7 copy.25.bias_ref
  39.6 0.7 reshape.63.gain_ref
  40.3 0.1 stack.72.flag_ref
  40.4 0.2 collective-permute-done.1
  40.6 2.7 %collective-permute-start.2 = (f32[16,384]{1,0:T(8,128)S(1)}, f32[16,384]{1,0:T(8,128)S(1)}, u32[]{:S(2)}, u32[]{:S(2)}) collective-permute-start(f32[16,384]{1,0:T(8,128)S(1)} %add.94), channel_id=1, source_target_pairs={{0,4},{1,5},{2,6},{3,7},{4,0},{5,1},{6,2},{7,3},{8,12},{9,13},{10,... | collective-permute-start | bytes 73736 | tf_op jit(solution)/shard_map/ppermute | solution.py:511
  43.4 0.1 eq.49
  43.5 1.3 collective-permute-done.2
  44.8 0.9 copy-done.5
  45.7 4.8 %hidden.1 = bf16[320,5120]{1,0:T(8,128)(2,1)S(1)} custom-call(f32[16,384]{1,0:T(8,128)S(1)} %add.95.latent_ref, f32[16,1]{1,0:T(8,128)S(1)} %copy.25.bias_ref, bf16[16,5120]{1,0:T(8,128)(2,1)S(1)} %copy-done.5, bf16[320,5120]{1,0:T(8,128)(2,1)S(1)} %copy-done, bf16[1,5120]{1,0:T(2,128)(2,1)S(1)} %reshape.63.gain_ref), custom_call_target="tpu_custom_call" | custom-call | tf_op jit(solution)/shard_map/hidden/pallas_call | solution.py:168
  50.5 1.8 %copy-done.1 = bf16[320,5120]{1,0:T(8,128)(2,1)} copy-done((bf16[320,5120]{1,0:T(8,128)(2,1)}, bf16[320,5120]{1,0:T(8,128)(2,1)S(1)}, u32[]{:S(2)}) %copy-start.1) | copy-done | bytes 3276824
  52.3 28.4 %all-gather.2.cloned.1.call-done = bf16[5120,768]{1,0:T(8,128)(2,1)} async-done(((bf16[160,768]{1,0:T(8,128)(2,1)}), bf16[5120,768]{1,0:T(8,128)(2,1)}) %all-gather.2.cloned.1.call-update) | async-done | bytes 7864336 | tf_op jit(solution)/shard_map/all_gather | solution.py:497
  80.7 6.9 %convolution_convert_fusion = bf16[320,768]{1,0:T(8,128)(2,1)S(1)} fusion(bf16[320,5120]{1,0:T(8,128)(2,1)} %copy-done.1, bf16[5120,768]{1,0:T(8,128)(2,1)} %all-gather.2.cloned.1.call-done), kind=kOutput, calls=%fused_computation | convolution fusion | flops 2516828160 | bytes 11632640 | tf_op jit(solution)/shard_map/dot_general | solution.py:513
  87.6 2.2 %collective-permute-start.6 = (bf16[320,256]{1,0:T(8,128)(2,1)S(1)}, bf16[320,256]{1,0:T(8,128)(2,1)S(1)}, u32[]{:S(2)}, u32[]{:S(2)}) collective-permute-start(bf16[320,256]{1,0:T(8,128)(2,1)S(1)} %slice.27.kv_ref.rest_0_), channel_id=1, source_target_pairs={{0,48},{8,56},{16,0},{24,8},{32,16},{40,24},{48,32},{56,40},{64,11... | collective-permute-start | bytes 491528 | tf_op jit(solution)/shard_map/ppermute | solution.py:416
  89.8 0.3 collective-permute-start.5
  90.1 0.2 collective-permute-start.4
  90.3 0.2 select_reduce_fusion.1
  90.5 1.2 collective-permute-start.3
  91.7 0.1 and_select_fusion
  91.8 1.3 collective-permute-start.9
  93.1 0.1 collective-permute-done.6.rest_2_.rest_3_
  93.2 1.7 %collective-permute-start.8 = (bf16[320,256]{1,0:T(8,128)(2,1)S(1)}, bf16[320,256]{1,0:T(8,128)(2,1)S(1)}, u32[]{:S(2)}, u32[]{:S(2)}) collective-permute-start(bf16[320,256]{1,0:T(8,128)(2,1)S(1)} %slice.27.kv_ref.rest_0_), channel_id=1, source_target_pairs={{0,128},{8,136},{16,144},{24,152},{32,160},{40,168},{48,176},{56,1... | collective-permute-start | bytes 491528 | tf_op jit(solution)/shard_map/ppermute | solution.py:412
  94.9 9.7 %collective-permute-done.5.rest_1_.rest_2_ = bf16[320,256]{1,0:T(8,128)(2,1)S(1)} collective-permute-done((bf16[320,256]{1,0:T(8,128)(2,1)S(1)}, bf16[320,256]{1,0:T(8,128)(2,1)S(1)}, u32[]{:S(2)}, u32[]{:S(2)}) %collective-permute-start.5) | collective-permute-done | bytes 163872 | tf_op jit(solution)/shard_map/ppermute | solution.py:416
  104.6 1.1 collective-permute-start.7
  105.7 0.4 collective-permute-start.12
  106.2 1.8 %collective-permute-start.15 = (bf16[640,256]{1,0:T(8,128)(2,1)S(1)}, bf16[640,256]{1,0:T(8,128)(2,1)S(1)}, u32[]{:S(2)}, u32[]{:S(2)}) collective-permute-start(bf16[640,256]{1,0:T(8,128)(2,1)S(1)} %constant_dynamic-update-slice_fusion), channel_id=1, source_target_pairs={{0,128},{8,136},{16,144},{24,152},{32,160},{40,168},{48,176},{56,1... | collective-permute-start | bytes 983048 | tf_op jit(solution)/shard_map/ppermute | solution.py:412
  108.0 2.0 %first.1.state_ref = f32[136,2560]{1,0:T(8,128)S(1)} custom-call(s32[1]{0:T(128)} %bitcast.10.core_ref, bf16[320,512]{1,0:T(8,128)(2,1)S(1)} %slice.26.own_ref, bf16[320,512]{1,0:T(8,128)(2,1)S(1)} %collective-permute-done.3.pair_ref, bf16[320,256]{1,0:T(8,128)(2,1)S(1)} %slice.27.kv_ref.rest_0_), custom_call_target="tpu_custom_call" | custom-call | flops 419430400 | bytes 3145728 | tf_op jit(solution)/shard_map/first/pallas_call | solution.py:257
  110.0 1.2 collective-permute-start.14
  111.2 1.6 collective-permute-start.13
  112.8 0.3 collective-permute-start.11
  113.1 2.0 %collective-permute-start.10 = (bf16[320,256]{1,0:T(8,128)(2,1)S(1)}, bf16[320,256]{1,0:T(8,128)(2,1)S(1)}, u32[]{:S(2)}, u32[]{:S(2)}) collective-permute-start(bf16[320,256]{1,0:T(8,128)(2,1)S(1)} %collective-permute-done.4.rest_0_.rest_1_), channel_id=1, source_target_pairs={{0,64},{8,72},{16,80},{24,88},{32,96},{40,104},{48,112},{56,120},{... | collective-permute-start | bytes 491528 | tf_op jit(solution)/shard_map/ppermute | solution.py:412
  115.1 7.2 %more.4.state_ref = f32[136,2560]{1,0:T(8,128)S(1)} custom-call(s32[6]{0:T(128)S(1)} %stack.72.flag_ref, bf16[320,512]{1,0:T(8,128)(2,1)S(1)} %slice.26.own_ref, bf16[320,512]{1,0:T(8,128)(2,1)S(1)} %collective-permute-done.3.pair_ref, f32[136,2560]{1,0:T(8,128)S(1)} %first.1.state_ref, bf16[320,256]{1,0:T(8,128)(2,1)S(1)} %collective-permute-done.4.rest_0_.rest_1_, ...), custom_call_target="tpu_custom_call" | custom-call | flops 2516582400 | bytes 3145728 | tf_op jit(solution)/shard_map/more/pallas_call | solution.py:315
  122.3 5.7 %collective-permute-done.11.rest_1_.rest_8_ = bf16[320,256]{1,0:T(8,128)(2,1)S(1)} collective-permute-done((bf16[320,256]{1,0:T(8,128)(2,1)S(1)}, bf16[320,256]{1,0:T(8,128)(2,1)S(1)}, u32[]{:S(2)}, u32[]{:S(2)}) %collective-permute-start.11) | collective-permute-done | bytes 163872 | tf_op jit(solution)/shard_map/ppermute | solution.py:412
  128.0 2.6 %collective-permute-done.10.rest_0_.rest_7_ = bf16[320,256]{1,0:T(8,128)(2,1)S(1)} collective-permute-done((bf16[320,256]{1,0:T(8,128)(2,1)S(1)}, bf16[320,256]{1,0:T(8,128)(2,1)S(1)}, u32[]{:S(2)}, u32[]{:S(2)}) %collective-permute-start.10) | collective-permute-done | bytes 163872 | tf_op jit(solution)/shard_map/ppermute | solution.py:412
  130.6 6.4 %more.5.state_ref = f32[136,2560]{1,0:T(8,128)S(1)} custom-call(s32[3]{0:T(128)S(1)} %pad_add_fusion.2.flag_ref, bf16[320,512]{1,0:T(8,128)(2,1)S(1)} %slice.26.own_ref, bf16[320,512]{1,0:T(8,128)(2,1)S(1)} %collective-permute-done.3.pair_ref, f32[136,2560]{1,0:T(8,128)S(1)} %more.4.state_ref, bf16[320,256]{1,0:T(8,128)(2,1)S(1)} %collective-permute-done.10.rest_0_.rest_7_, ...), custom_call_target="tpu_custom_call" | custom-call | flops 1258291200 | bytes 3145728 | tf_op jit(solution)/shard_map/more/pallas_call | solution.py:315
  137.1 7.7 %more.6.state_ref = f32[136,2560]{1,0:T(8,128)S(1)} custom-call(s32[4]{0:T(128)S(1)} %pad_add_fusion.1.flag_ref, bf16[320,512]{1,0:T(8,128)(2,1)S(1)} %slice.26.own_ref, bf16[320,512]{1,0:T(8,128)(2,1)S(1)} %collective-permute-done.3.pair_ref, f32[136,2560]{1,0:T(8,128)S(1)} %more.5.state_ref, bf16[640,256]{1,0:T(8,128)(2,1)S(1)} %collective-permute-done.13.rest_0_.rest_10_, ...), custom_call_target="tpu_custom_call" | custom-call | flops 1677721600 | bytes 3145728 | tf_op jit(solution)/shard_map/more/pallas_call | solution.py:315
  144.8 4.3 %more.7 = (f32[136,1280]{1,0:T(8,128)S(1)}, f32[136,1280]{1,0:T(8,128)S(1)}) custom-call(s32[2]{0:T(128)S(1)} %pad_add_fusion.flag_ref, bf16[320,512]{1,0:T(8,128)(2,1)S(1)} %slice.26.own_ref, bf16[320,512]{1,0:T(8,128)(2,1)S(1)} %collective-permute-done.3.pair_ref, f32[136,2560]{1,0:T(8,128)S(1)} %more.6.state_ref, ...), custom_call_target="tpu_custom_call" | custom-call | flops 838860800 | bytes 3145728 | tf_op jit(solution)/shard_map/more/pallas_call | solution.py:315
  149.1 1.8 %collective-permute-start.16 = (f32[136,1280]{1,0:T(8,128)S(1)}, f32[136,1280]{1,0:T(8,128)S(1)}, u32[]{:S(2)}, u32[]{:S(2)}) collective-permute-start(f32[136,1280]{1,0:T(8,128)S(1)} %get-tuple-element.7), channel_id=1, source_target_pairs={{0,8},{8,0},{16,24},{24,16},{32,40},{40,32},{48,56},{56,48},{64,72... | collective-permute-start | bytes 2088968 | tf_op jit(solution)/shard_map/ppermute | solution.py:420
  151.0 11.8 %pages.1 = (bf16[320,256]{1,0:T(8,128)(2,1)S(1)}, bf16[320,256]{1,0:T(8,128)(2,1)S(1)}) custom-call(s32[80]{0:T(128)S(1)} %compare_select_fusion.8.code_ref, s32[80]{0:T(128)S(1)} %get-tuple-element.14.row_ref, s32[80]{0:T(128)S(1)} %get-tuple-element.12.odd_ref, bf16[320,256]{1,0:T(8,128)(2,1)S(1)} %slice.27.kv_ref.rest_0_, ...), custom_call_target="tpu_custom_call" | custom-call | tf_op jit(solution)/shard_map/pages/pallas_call | solution.py:387
  162.8 0.1 collective-permute-start.17
  162.9 1.4 collective-permute-done.17
  164.3 0.9 broadcast_select_fusion
  165.2 1.0 finish.1
  (36 shorter events, 0.3 us)
Async XLA Ops:
  7.2 37.6 %copy-start = (bf16[320,5120]{1,0:T(8,128)(2,1)S(1)}, bf16[320,5120]{1,0:T(8,128)(2,1)}, u32[]{:S(2)}) copy-start(bf16[320,5120]{1,0:T(8,128)(2,1)} %table_ref.1) | copy-start | bytes 9830404
  7.2 73.5 %all-gather.2.cloned.1.call-start = ((), (), s32[]{:S(2)}) async-start(), calls=%async_computation.1 | async-start | bytes 8110080 | tf_op jit(solution)/shard_map/all_gather | solution.py:497
  7.9 1.3 copy-start.4
  9.2 0.8 copy-start.6
  12.1 14.9 %all-to-all-start = ((f32[32,1,512]{2,1,0:T(1,128)}), f32[32,1,512]{2,1,0:T(1,128)S(1)}, u32[]{:S(2)}, u32[]{:S(2)}) async-start(f32[32,1,512]{2,1,0:T(1,128)} %all_to_all.8), calls=%async_computation | async-start | bytes 131072 | tf_op jit(solution)/shard_map/all_to_all | solution.py:505
  28.0 1.0 copy-start.2
  29.0 1.0 copy-start.3
  30.7 6.9 %collective-permute-start = (f32[16,384]{1,0:T(8,128)S(1)}, f32[16,384]{1,0:T(8,128)S(1)}, u32[]{:S(2)}, u32[]{:S(2)}) collective-permute-start(f32[16,384]{1,0:T(8,128)S(1)} %place.1), channel_id=1, source_target_pairs={{0,1},{1,0},{2,3},{3,2},{4,5},{5,4},{6,7},{7,6},{8,9},{9,8},{10,11... | collective-permute-start | bytes 73736 | tf_op jit(solution)/shard_map/ppermute | solution.py:511
  37.6 3.0 %collective-permute-start.1 = (f32[16,384]{1,0:T(8,128)S(1)}, f32[16,384]{1,0:T(8,128)S(1)}, u32[]{:S(2)}, u32[]{:S(2)}) collective-permute-start(f32[16,384]{1,0:T(8,128)S(1)} %add.93), channel_id=1, source_target_pairs={{0,2},{1,3},{2,0},{3,1},{4,6},{5,7},{6,4},{7,5},{8,10},{9,11},{10,... | collective-permute-start | bytes 73736 | tf_op jit(solution)/shard_map/ppermute | solution.py:511
  40.6 4.2 %collective-permute-start.2 = (f32[16,384]{1,0:T(8,128)S(1)}, f32[16,384]{1,0:T(8,128)S(1)}, u32[]{:S(2)}, u32[]{:S(2)}) collective-permute-start(f32[16,384]{1,0:T(8,128)S(1)} %add.94), channel_id=1, source_target_pairs={{0,4},{1,5},{2,6},{3,7},{4,0},{5,1},{6,2},{7,3},{8,12},{9,13},{10,... | collective-permute-start | bytes 73736 | tf_op jit(solution)/shard_map/ppermute | solution.py:511
  44.8 0.9 copy-start.5
  50.5 1.8 %copy-start.1 = (bf16[320,5120]{1,0:T(8,128)(2,1)}, bf16[320,5120]{1,0:T(8,128)(2,1)S(1)}, u32[]{:S(2)}) copy-start(bf16[320,5120]{1,0:T(8,128)(2,1)S(1)} %hidden.1) | copy-start | bytes 9830404
  87.6 5.6 %collective-permute-start.6 = (bf16[320,256]{1,0:T(8,128)(2,1)S(1)}, bf16[320,256]{1,0:T(8,128)(2,1)S(1)}, u32[]{:S(2)}, u32[]{:S(2)}) collective-permute-start(bf16[320,256]{1,0:T(8,128)(2,1)S(1)} %slice.27.kv_ref.rest_0_), channel_id=1, source_target_pairs={{0,48},{8,56},{16,0},{24,8},{32,16},{40,24},{48,32},{56,40},{64,11... | collective-permute-start | bytes 491528 | tf_op jit(solution)/shard_map/ppermute | solution.py:416
  89.8 14.9 %collective-permute-start.5 = (bf16[320,256]{1,0:T(8,128)(2,1)S(1)}, bf16[320,256]{1,0:T(8,128)(2,1)S(1)}, u32[]{:S(2)}, u32[]{:S(2)}) collective-permute-start(bf16[320,256]{1,0:T(8,128)(2,1)S(1)} %slice.27.kv_ref.rest_0_), channel_id=1, source_target_pairs={{0,32},{8,40},{16,48},{24,56},{32,0},{40,8},{48,16},{56,24},{64,96... | collective-permute-start | bytes 491528 | tf_op jit(solution)/shard_map/ppermute | solution.py:416
  90.1 15.7 %collective-permute-start.4 = (bf16[320,256]{1,0:T(8,128)(2,1)S(1)}, bf16[320,256]{1,0:T(8,128)(2,1)S(1)}, u32[]{:S(2)}, u32[]{:S(2)}) collective-permute-start(bf16[320,256]{1,0:T(8,128)(2,1)S(1)} %slice.27.kv_ref.rest_0_), channel_id=1, source_target_pairs={{0,16},{8,24},{16,32},{24,40},{32,48},{40,56},{48,0},{56,8},{64,80... | collective-permute-start | bytes 491528 | tf_op jit(solution)/shard_map/ppermute | solution.py:416
  90.5 15.6 %collective-permute-start.3 = (bf16[320,512]{1,0:T(8,128)(2,1)S(1)}, bf16[320,512]{1,0:T(8,128)(2,1)S(1)}, u32[]{:S(2)}, u32[]{:S(2)}) collective-permute-start(bf16[320,512]{1,0:T(8,128)(2,1)S(1)} %slice.26.own_ref), channel_id=1, source_target_pairs={{0,8},{8,0},{16,24},{24,16},{32,40},{40,32},{48,56},{56,48},{64,72... | collective-permute-start | bytes 983048 | tf_op jit(solution)/shard_map/ppermute | solution.py:420
  91.8 18.3 %collective-permute-start.9 = (bf16[320,256]{1,0:T(8,128)(2,1)S(1)}, bf16[320,256]{1,0:T(8,128)(2,1)S(1)}, u32[]{:S(2)}, u32[]{:S(2)}) collective-permute-start(bf16[320,256]{1,0:T(8,128)(2,1)S(1)} %slice.27.kv_ref.rest_0_), channel_id=1, source_target_pairs={{0,192},{8,200},{16,208},{24,216},{32,224},{40,232},{48,240},{56,2... | collective-permute-start | bytes 491528 | tf_op jit(solution)/shard_map/ppermute | solution.py:412
  93.2 18.0 %collective-permute-start.8 = (bf16[320,256]{1,0:T(8,128)(2,1)S(1)}, bf16[320,256]{1,0:T(8,128)(2,1)S(1)}, u32[]{:S(2)}, u32[]{:S(2)}) collective-permute-start(bf16[320,256]{1,0:T(8,128)(2,1)S(1)} %slice.27.kv_ref.rest_0_), channel_id=1, source_target_pairs={{0,128},{8,136},{16,144},{24,152},{32,160},{40,168},{48,176},{56,1... | collective-permute-start | bytes 491528 | tf_op jit(solution)/shard_map/ppermute | solution.py:412
  104.6 8.2 %collective-permute-start.7 = (bf16[320,256]{1,0:T(8,128)(2,1)S(1)}, bf16[320,256]{1,0:T(8,128)(2,1)S(1)}, u32[]{:S(2)}, u32[]{:S(2)}) collective-permute-start(bf16[320,256]{1,0:T(8,128)(2,1)S(1)} %slice.27.kv_ref.rest_0_), channel_id=1, source_target_pairs={{0,64},{8,72},{16,80},{24,88},{32,96},{40,104},{48,112},{56,120},{... | collective-permute-start | bytes 491528 | tf_op jit(solution)/shard_map/ppermute | solution.py:412
  105.7 7.4 %collective-permute-start.12 = (bf16[320,256]{1,0:T(8,128)(2,1)S(1)}, bf16[320,256]{1,0:T(8,128)(2,1)S(1)}, u32[]{:S(2)}, u32[]{:S(2)}) collective-permute-start(bf16[320,256]{1,0:T(8,128)(2,1)S(1)} %collective-permute-done.4.rest_0_.rest_1_), channel_id=1, source_target_pairs={{0,192},{8,200},{16,208},{24,216},{32,224},{40,232},{48,240},{56,2... | collective-permute-start | bytes 491528 | tf_op jit(solution)/shard_map/ppermute | solution.py:412
  106.2 38.6 %collective-permute-start.15 = (bf16[640,256]{1,0:T(8,128)(2,1)S(1)}, bf16[640,256]{1,0:T(8,128)(2,1)S(1)}, u32[]{:S(2)}, u32[]{:S(2)}) collective-permute-start(bf16[640,256]{1,0:T(8,128)(2,1)S(1)} %constant_dynamic-update-slice_fusion), channel_id=1, source_target_pairs={{0,128},{8,136},{16,144},{24,152},{32,160},{40,168},{48,176},{56,1... | collective-permute-start | bytes 983048 | tf_op jit(solution)/shard_map/ppermute | solution.py:412
  110.0 27.0 %collective-permute-start.14 = (bf16[640,256]{1,0:T(8,128)(2,1)S(1)}, bf16[640,256]{1,0:T(8,128)(2,1)S(1)}, u32[]{:S(2)}, u32[]{:S(2)}) collective-permute-start(bf16[640,256]{1,0:T(8,128)(2,1)S(1)} %constant_dynamic-update-slice_fusion), channel_id=1, source_target_pairs={{0,192},{8,200},{16,208},{24,216},{32,224},{40,232},{48,240},{56,2... | collective-permute-start | bytes 983048 | tf_op jit(solution)/shard_map/ppermute | solution.py:412
  111.2 25.8 %collective-permute-start.13 = (bf16[640,256]{1,0:T(8,128)(2,1)S(1)}, bf16[640,256]{1,0:T(8,128)(2,1)S(1)}, u32[]{:S(2)}, u32[]{:S(2)}) collective-permute-start(bf16[640,256]{1,0:T(8,128)(2,1)S(1)} %constant_dynamic-update-slice_fusion), channel_id=1, source_target_pairs={{0,64},{8,72},{16,80},{24,88},{32,96},{40,104},{48,112},{56,120},{... | collective-permute-start | bytes 983048 | tf_op jit(solution)/shard_map/ppermute | solution.py:412
  112.8 15.2 %collective-permute-start.11 = (bf16[320,256]{1,0:T(8,128)(2,1)S(1)}, bf16[320,256]{1,0:T(8,128)(2,1)S(1)}, u32[]{:S(2)}, u32[]{:S(2)}) collective-permute-start(bf16[320,256]{1,0:T(8,128)(2,1)S(1)} %collective-permute-done.4.rest_0_.rest_1_), channel_id=1, source_target_pairs={{0,128},{8,136},{16,144},{24,152},{32,160},{40,168},{48,176},{56,1... | collective-permute-start | bytes 491528 | tf_op jit(solution)/shard_map/ppermute | solution.py:412
  113.1 17.5 %collective-permute-start.10 = (bf16[320,256]{1,0:T(8,128)(2,1)S(1)}, bf16[320,256]{1,0:T(8,128)(2,1)S(1)}, u32[]{:S(2)}, u32[]{:S(2)}) collective-permute-start(bf16[320,256]{1,0:T(8,128)(2,1)S(1)} %collective-permute-done.4.rest_0_.rest_1_), channel_id=1, source_target_pairs={{0,64},{8,72},{16,80},{24,88},{32,96},{40,104},{48,112},{56,120},{... | collective-permute-start | bytes 491528 | tf_op jit(solution)/shard_map/ppermute | solution.py:412
  149.1 16.1 %collective-permute-start.16 = (f32[136,1280]{1,0:T(8,128)S(1)}, f32[136,1280]{1,0:T(8,128)S(1)}, u32[]{:S(2)}, u32[]{:S(2)}) collective-permute-start(f32[136,1280]{1,0:T(8,128)S(1)} %get-tuple-element.7), channel_id=1, source_target_pairs={{0,8},{8,0},{16,24},{24,16},{32,40},{40,32},{48,56},{56,48},{64,72... | collective-permute-start | bytes 2088968 | tf_op jit(solution)/shard_map/ppermute | solution.py:420
  162.8 1.5 collective-permute-start.17
Sparse Core Ops, SparseCore 0:
  9.9 70.7 all-gather.1

commit v3 on v2

--- a/solution.py
+++ b/solution.py
@@ -14,6 +14,7 @@
 LAT = 16
 BLK = 320
 PAGES = 40
+MOST = 3
 SEQ = 32
 ROWS = 5
 COLS = 2
@@ -266,22 +267,16 @@
     )(core.reshape(1), own, pair, kv)
 
 
-def more_kernel(sizes, split, flag_ref, own_ref, pair_ref, state_ref, *rest):
-    arrays, rest = rest[: len(sizes)], rest[len(sizes) :]
+def more_kernel(unit, count, split, flag_ref, own_ref, pair_ref, state_ref, *rest):
+    arrays, rest = rest[:count], rest[count:]
     if split:
         own_out_ref, pair_out_ref, q_ref, held_ref, sems, work_ref = rest
     else:
         work_ref, q_ref, held_ref, sems = rest
     copies = []
-    first = 0
-    for index, size in enumerate(sizes):
-        copies.append(
-            pltpu.make_async_copy(
-                arrays[index], held_ref.at[pl.ds(first, size * BLK), :], sems.at[index]
-            )
-        )
+    for index, array in enumerate(arrays):
+        copies.append(pltpu.make_async_copy(array, held_ref.at[index], sems.at[index]))
         copies[-1].start()
-        first += size * BLK
     set_queries(own_ref, pair_ref, q_ref)
     work_ref[...] = state_ref[...]
     for copy in copies:
@@ -290,37 +285,37 @@
     def body(index, carry):
         @pl.when(flag_ref[index] != 0)
         def _():
-            rows = pl.ds(pl.multiple_of(index * BLK, BLK), BLK)
-            attend_block(False, None, held_ref[rows, :HD], held_ref[rows, HD:], q_ref, work_ref)
+            keys, values = held_ref[index, :, :HD], held_ref[index, :, HD:]
+            attend_block(False, None, keys, values, q_ref, work_ref)
 
         return carry
 
-    lax.fori_loop(0, sum(sizes), body, 0)
+    lax.fori_loop(0, count, body, 0)
     if split:
         own_out_ref[...] = work_ref[:, :QROWS]
         pair_out_ref[...] = work_ref[:, QROWS:]
 
 
 def attend_more(flags, own, pair, state, arrays, split=False):
-    sizes = tuple(array.shape[0] // BLK for array in arrays)
+    unit, count = arrays[0].shape[0], len(arrays)
     half = jax.ShapeDtypeStruct((STATE, QROWS), jnp.float32)
     whole = jax.ShapeDtypeStruct((STATE, 2 * QROWS), jnp.float32)
     scratch = [
         pltpu.VMEM((2 * QROWS, HD), jnp.bfloat16),
-        pltpu.VMEM((sum(sizes) * BLK, 2 * HD), jnp.bfloat16),
-        pltpu.SemaphoreType.DMA((len(sizes),)),
+        pltpu.VMEM((count, unit, 2 * HD), jnp.bfloat16),
+        pltpu.SemaphoreType.DMA((count,)),
     ]
     if split:
         scratch.append(pltpu.VMEM((STATE, 2 * QROWS), jnp.float32))
     return pl.pallas_call(
-        functools.partial(more_kernel, sizes, split),
+        functools.partial(more_kernel, unit, count, split),
         in_specs=[pl.BlockSpec(memory_space=pltpu.SMEM)]
         + [pl.BlockSpec(memory_space=pltpu.VMEM)] * 3
-        + [pl.BlockSpec(memory_space=pl.ANY)] * len(sizes),
+        + [pl.BlockSpec(memory_space=pl.ANY)] * count,
         out_shape=(half, half) if split else whole,
         scratch_shapes=scratch,
         compiler_params=params(),
-        cost_estimate=cost(sum(sizes)),
+        cost_estimate=cost(count * unit // BLK),
         name="more",
     )(flags, own, pair, state, *arrays)
 
@@ -351,51 +346,44 @@
     )(own, got)
 
 
-def page_kernel(code_ref, row_ref, odd_ref, *rest):
-    arrays, (own_ref, pair_ref, held_ref, sems) = rest[:-4], rest[-4:]
-    count = 2 * PAGES
-
-    def start(slot, carry):
-        row = pl.multiple_of(row_ref[slot], 2 * PAGE)
-        for index, array in enumerate(arrays):
-
-            @pl.when(code_ref[slot] == index)
-            def _():
-                pltpu.make_async_copy(
-                    array.at[pl.ds(row, 2 * PAGE), :], held_ref.at[slot], sems.at[slot]
-                ).start()
-
-        return carry
-
-    lax.fori_loop(0, count, start, 0)
-    for pair in range(count // 2):
-        halves = []
-        for slot in (2 * pair, 2 * pair + 1):
-            pltpu.make_async_copy(
-                arrays[0].at[pl.ds(0, 2 * PAGE), :], held_ref.at[slot], sems.at[slot]
-            ).wait()
-            rows = held_ref[slot].astype(jnp.float32)
-            halves.append(jnp.where(odd_ref[slot] == 1, rows[PAGE:], rows[:PAGE]))
-        both = jnp.concatenate(halves, axis=0).astype(jnp.bfloat16)
-        out_ref = own_ref if 2 * pair < PAGES else pair_ref
-        place = (2 * pair % PAGES) * PAGE
-        out_ref[place : place + 2 * PAGE, :] = both
-
-
-def fetch_pages(code, row, odd, arrays):
+def page_kernel(place_ref, code_ref, *rest):
+    arrays, (own_ref, pair_ref, held_ref) = rest[:-3], rest[-3:]
+    held_ref[...] = jnp.zeros_like(held_ref)
+    y, z, core = place_ref[0], place_ref[1], place_ref[2]
+    for by_y in range(4):
+        for by_z in range(4):
+            if by_y == 0:
+                array, base = arrays[by_z], 0
+            else:
+                array, base = arrays[3 + by_y + by_z // 2 * 3], by_z % 2 * BLK
+            source = (((y - by_y) & 3) * 4 + ((z - by_z) & 3)) * 2 + core
+            for entry in range(2 * MOST):
+                code = code_ref[source * 2 * MOST + entry]
+
+                @pl.when(code >= 0)
+                def _():
+                    page = code >> 6
+                    slot = (code & 63) + entry // MOST * PAGES
+                    row = pl.multiple_of(base + (page >> 1) * 2 * PAGE, 2 * PAGE)
+                    rows = array[pl.ds(row, 2 * PAGE), :].astype(jnp.float32)
+                    rows = jnp.where((page & 1) == 1, rows[PAGE:], rows[:PAGE])
+                    held_ref[pl.ds(pl.multiple_of(slot * PAGE, PAGE), PAGE), :] = rows
+
+    own_ref[...] = held_ref[: PAGES * PAGE].astype(jnp.bfloat16)
+    pair_ref[...] = held_ref[PAGES * PAGE :].astype(jnp.bfloat16)
+
+
+def fetch_pages(place, codes, arrays):
     out = jax.ShapeDtypeStruct((PAGES * PAGE, 2 * HD), jnp.bfloat16)
     return pl.pallas_call(
         page_kernel,
-        in_specs=[pl.BlockSpec(memory_space=pltpu.SMEM)] * 3
-        + [pl.BlockSpec(memory_space=pl.ANY)] * len(arrays),
+        in_specs=[pl.BlockSpec(memory_space=pltpu.SMEM)] * 2
+        + [pl.BlockSpec(memory_space=pltpu.VMEM)] * len(arrays),
         out_shape=(out, out),
-        scratch_shapes=[
-            pltpu.VMEM((2 * PAGES, 2 * PAGE, 2 * HD), jnp.bfloat16),
-            pltpu.SemaphoreType.DMA((2 * PAGES,)),
-        ],
+        scratch_shapes=[pltpu.VMEM((2 * PAGES * PAGE, 2 * HD), jnp.float32)],
         compiler_params=params(),
         name="pages",
-    )(code, row, odd, *arrays)
+    )(place, codes, *arrays)
 
 
 def moves(step):
@@ -420,10 +408,25 @@
     return lax.ppermute(value, "seq", moves(lambda y, z, c: (y, z, 1 - c)))
 
 
-def pages_of(targets, owner):
-    mine = owner * PAGES + jnp.arange(PAGES, dtype=jnp.int32)
-    index = jnp.arange(SEQ * PAGES, dtype=jnp.int32)
-    return jnp.sum(jnp.where(targets[None, :] == mine[:, None], index[None, :], 0), axis=1)
+def page_codes(targets, me):
+    index = jnp.arange(PAGES, dtype=jnp.int32)
+    codes = []
+    for owner in (me, me ^ 1):
+        slot = targets - owner * PAGES
+        match = (slot >= 0) & (slot < PAGES)
+        before = match[:, None, :] & (index[None, :] < index[:, None])
+        rank = jnp.sum(before.astype(jnp.int32), axis=2)
+        code = index * 64 + slot + 1
+        for entry in range(MOST):
+            codes.append(jnp.sum(jnp.where(match & (rank == entry), code, 0), axis=1) - 1)
+    return jnp.stack(codes, axis=1).reshape(-1)
+
+
+def held_here(targets, me):
+    mine = me * PAGES + jnp.arange(PAGES, dtype=jnp.int32)
+    same_core = (jnp.arange(SEQ, dtype=jnp.int32) % 2 == me % 2)[:, None]
+    match = (targets[None] == mine[:, None, None]) & same_core[None]
+    return jnp.any(match, axis=(1, 2))
 
 
 def attention_and_pages(me, targets, qkv):
@@ -433,48 +436,32 @@
     by_z = {0: kv}
     for count in (1, 2, 3):
         by_z[count] = along_z(kv, count)
-    zero = {count: along_y(kv, count) for count in (1, 3, 2)}
-    one = {count: along_y(by_z[1], count) for count in (1, 3, 2)}
-    last = jnp.concatenate([by_z[2], by_z[3]], axis=0)
-    rest = {count: along_y(last, count) for count in (1, 3, 2)}
+    near = jnp.concatenate([kv, by_z[1]], axis=0)
+    near = {count: along_y(near, count) for count in (1, 3, 2)}
+    far = jnp.concatenate([by_z[2], by_z[3]], axis=0)
+    far = {count: along_y(far, count) for count in (1, 3, 2)}
 
     def flag(*conditions):
         return jnp.stack([jnp.asarray(value, jnp.int32) for value in conditions])
 
     state = attend_first(core, queries, pair, kv)
     state = attend_more(
-        flag(z >= 1, z >= 2, z >= 3, y >= 1, y >= 2, y >= 3),
-        queries,
-        pair,
-        state,
-        [by_z[1], by_z[2], by_z[3], zero[1], zero[2], zero[3]],
+        flag(z >= 1, z >= 2, z >= 3), queries, pair, state, [by_z[1], by_z[2], by_z[3]]
     )
     state = attend_more(
-        flag(y >= 1, y >= 2, y >= 3), queries, pair, state, [one[1], one[2], one[3]]
+        flag(y >= 1, y >= 3, y >= 2), queries, pair, state, [near[1], near[3], near[2]]
     )
-    state = attend_more(
-        flag(y >= 1, y >= 1, y >= 3, y >= 3), queries, pair, state, [rest[1], rest[3]]
-    )
-    own, sent = attend_more(
-        flag(y >= 2, y >= 2), queries, pair, state, [rest[2]], split=True
-    )
+    state = attend_more(flag(y >= 1, y >= 3), queries, pair, state, [far[1], far[3]])
+    own, sent = attend_more(flag(y >= 2), queries, pair, state, [far[2]], split=True)
     got = other_core(sent)
 
-    page = jnp.concatenate([pages_of(targets, me), pages_of(targets, me ^ 1)])
-    source = page // PAGES
-    by_y = (y - source // 8) % 4
-    by_zz = (z - (source // 2) % 4) % 4
-    held = source % 2 == core
-    code = jnp.where(by_y == 0, by_zz, jnp.minimum(by_zz, 2) * 3 + 3 + by_y)
-    offset = jnp.where((by_y > 0) & (by_zz == 3), BLK, 0)
-    row = offset + (page % PAGES) // 2 * 2 * PAGE
     arrays = [by_z[count] for count in range(4)]
-    for group in (zero, one, rest):
-        arrays += [group[count] for count in (1, 2, 3)]
-    own_pages, sent_pages = fetch_pages(code, row, page % 2, arrays)
+    arrays += [group[count] for group in (near, far) for count in (1, 2, 3)]
+    place = jnp.stack([y, z, core])
+    own_pages, sent_pages = fetch_pages(place, page_codes(targets, me), arrays)
     got_pages = other_core(sent_pages)
     attention = finish(own, got)
-    keep = held[:PAGES].reshape(PAGES, 1, 1, 1)
+    keep = held_here(targets, me).reshape(PAGES, 1, 1, 1)
     shape = (PAGES, PAGE, 2, HD)
     kv_cache = jnp.where(keep, own_pages.reshape(shape), got_pages.reshape(shape))
     return attention, kv_cache
@@ -503,7 +490,7 @@
     message = jnp.pad(message, ((0, 0), (0, 512 - message.shape[1])))
     message = jnp.broadcast_to(message[:, None], (FRAMES, SEQ // FRAMES, 512)).reshape(SEQ, 512)
     message = lax.all_to_all(message, "seq", split_axis=0, concat_axis=0, tiled=True)
-    targets = message[:, EXT * LAT : EXT * LAT + PAGES].astype(jnp.int32).reshape(-1)
+    targets = message[:, EXT * LAT : EXT * LAT + PAGES].astype(jnp.int32)
     offset = tensor - me % (SEQ // FRAMES)
     latent = place_latents(message[:, : EXT * LAT].reshape(SEQ * EXT, LAT), offset)
     for bit in (1, 2, 4):

time: 173 us -> 166 us (0.960)
  the two profiles are of different devices: /device:TPU:25 before, /device:TPU:89 now
where the time goes in v3:
time: 166 us
  waiting for transfers between devices  51.2 us (31%)
  Pallas kernels  36.5 us (22%)
  starting transfers between devices  29.1 us (18%)
  local copies, waits for them, and re-layouts  21 us (13%)
  between operations  14.5 us (9%)
  matrix products  6.92 us (4%)
  other arithmetic  6.37 us (4%)
    all_gather x1, waiting for transfers between devices, on_device(): weight = lax.all_gather(qkv_weight, 'seq', axis=0, tiled=True)  28.2 us
    pallas_call x4, Pallas kernels, attend_more(): pl.pallas_call(functools.partial(more_kernel, unit, count, split), in_spe...  25 us
    unnamed x60, local copies, waits for them, and re-layouts  16.3 us
    ppermute x3, waiting for transfers between devices, along_z(): lax.ppermute(value, 'seq', moves(lambda y, z, c: (y, (z + count) % 4, c)))  13.3 us
    all_to_all x1, starting transfers between devices, on_device(): lax.all_to_all(message, 'seq', split_axis=0, concat_axis=0, tiled=True)  8.39 us
    ppermute x3, starting transfers between devices, on_device(): latent = latent + lax.ppermute(latent, 'tensor', swap)  8.17 us
    ppermute x6, starting transfers between devices, along_y(): lax.ppermute(value, 'seq', moves(lambda y, z, c: ((y + count) % 4, z, c)))  7.31 us
    dot_general x1, matrix products, on_device(): jnp.dot(normed, weight, preferred_element_type=jnp.float32)  6.92 us
  transfers between devices with their start and end apart: 17, of which 7 were waited for; matrix products, arithmetic and copies ran while one was open for 6% of the time, Pallas kernels for 18%

profile of v3, /device:TPU:89, one launch (start us, length us, event | category | flops | bytes accessed | tf_op | source)
XLA Modules:
  0.0 165.5 jit_solution(8019224778973717303)
XLA Ops:
  7.2 0.7 all-gather.2.cloned.1.call-update
  7.9 1.2 copy-done.12
  9.2 0.8 copy-done.26
  9.9 0.5 conv.1
  10.6 0.7 add_convert_fusion.1
  11.4 0.7 all_to_all.8
  12.1 8.4 %all-to-all-start = ((f32[32,1,512]{2,1,0:T(1,128)}), f32[32,1,512]{2,1,0:T(1,128)S(1)}, u32[]{:S(2)}, u32[]{:S(2)}) async-start(f32[32,1,512]{2,1,0:T(1,128)} %all_to_all.8), calls=%async_computation | async-start | bytes 131072 | tf_op jit(solution)/shard_map/all_to_all | solution.py:492
  20.7 0.6 fusion.1
  21.3 0.5 iota_add_fusion
  21.9 0.7 fusion
  22.6 0.7 copy.28.bias_ref
  23.4 0.7 reshape.144.gain_ref
  24.1 1.1 copy.27.token_ref
  25.2 1.0 reshape.142.parts_ref
  26.2 1.0 copy-done.2
  27.2 1.0 copy-done.3
  28.2 0.6 place.1
  28.8 4.3 %collective-permute-start = (f32[16,384]{1,0:T(8,128)S(1)}, f32[16,384]{1,0:T(8,128)S(1)}, u32[]{:S(2)}, u32[]{:S(2)}) collective-permute-start(f32[16,384]{1,0:T(8,128)S(1)} %place.1), channel_id=1, source_target_pairs={{0,1},{1,0},{2,3},{3,2},{4,5},{5,4},{6,7},{7,6},{8,9},{9,8},{10,11... | collective-permute-start | bytes 73736 | tf_op jit(solution)/shard_map/ppermute | solution.py:498
  33.2 1.2 convert_reduce_fusion
  34.4 1.4 collective-permute-done
  35.8 1.2 collective-permute-start.1
  37.0 0.3 select_reduce_fusion
  37.3 1.6 collective-permute-done.1
  38.9 2.7 %collective-permute-start.2 = (f32[16,384]{1,0:T(8,128)S(1)}, f32[16,384]{1,0:T(8,128)S(1)}, u32[]{:S(2)}, u32[]{:S(2)}) collective-permute-start(f32[16,384]{1,0:T(8,128)S(1)} %add.132), channel_id=1, source_target_pairs={{0,4},{1,5},{2,6},{3,7},{4,0},{5,1},{6,2},{7,3},{8,12},{9,13},{10,... | collective-permute-start | bytes 73736 | tf_op jit(solution)/shard_map/ppermute | solution.py:498
  41.6 1.6 collective-permute-done.2
  43.3 0.9 copy-done.25
  44.2 4.8 %hidden.1 = bf16[320,5120]{1,0:T(8,128)(2,1)S(1)} custom-call(f32[16,384]{1,0:T(8,128)S(1)} %add.133.latent_ref, f32[16,1]{1,0:T(8,128)S(1)} %copy.28.bias_ref, bf16[16,5120]{1,0:T(8,128)(2,1)S(1)} %copy-done.25, bf16[320,5120]{1,0:T(8,128)(2,1)S(1)} %copy-done, bf16[1,5120]{1,0:T(2,128)(2,1)S(1)} %reshape.144.gain_ref), custom_call_target="tpu_custom_call" | custom-call | tf_op jit(solution)/shard_map/hidden/pallas_call | solution.py:169
  48.9 1.8 %copy-done.1 = bf16[320,5120]{1,0:T(8,128)(2,1)} copy-done((bf16[320,5120]{1,0:T(8,128)(2,1)}, bf16[320,5120]{1,0:T(8,128)(2,1)S(1)}, u32[]{:S(2)}) %copy-start.1) | copy-done | bytes 3276824
  50.7 28.2 %all-gather.2.cloned.1.call-done = bf16[5120,768]{1,0:T(8,128)(2,1)} async-done(((bf16[160,768]{1,0:T(8,128)(2,1)}), bf16[5120,768]{1,0:T(8,128)(2,1)}) %all-gather.2.cloned.1.call-update) | async-done | bytes 7864336 | tf_op jit(solution)/shard_map/all_gather | solution.py:484
  78.9 6.9 %convolution_convert_fusion = bf16[320,768]{1,0:T(8,128)(2,1)S(1)} fusion(bf16[320,5120]{1,0:T(8,128)(2,1)} %copy-done.1, bf16[5120,768]{1,0:T(8,128)(2,1)} %all-gather.2.cloned.1.call-done), kind=kOutput, calls=%fused_computation | convolution fusion | flops 2516828160 | bytes 11632640 | tf_op jit(solution)/shard_map/dot_general | solution.py:500
  85.9 1.2 collective-permute-start.5
  87.1 1.0 collective-permute-start.4
  88.1 0.6 collective-permute-start.6
  88.7 1.1 collective-permute-start.3
  89.8 13.3 %collective-permute-done.4.rest_0_.rest_1_ = bf16[320,256]{1,0:T(8,128)(2,1)S(1)} collective-permute-done((bf16[320,256]{1,0:T(8,128)(2,1)S(1)}, bf16[320,256]{1,0:T(8,128)(2,1)S(1)}, u32[]{:S(2)}, u32[]{:S(2)}) %collective-permute-start.4) | collective-permute-done | bytes 163872 | tf_op jit(solution)/shard_map/ppermute | solution.py:404
  103.1 1.6 collective-permute-start.9
  104.7 1.3 collective-permute-start.8
  105.9 1.4 collective-permute-start.7
  107.4 0.1 collective-permute-start.11
  107.5 2.6 %collective-permute-start.10 = (bf16[640,256]{1,0:T(8,128)(2,1)S(1)}, bf16[640,256]{1,0:T(8,128)(2,1)S(1)}, u32[]{:S(2)}, u32[]{:S(2)}) collective-permute-start(bf16[640,256]{1,0:T(8,128)(2,1)S(1)} %constant_dynamic-update-slice_fusion), channel_id=1, source_target_pairs={{0,64},{8,72},{16,80},{24,88},{32,96},{40,104},{48,112},{56,120},{... | collective-permute-start | bytes 983048 | tf_op jit(solution)/shard_map/ppermute | solution.py:400
  110.2 2.0 %first.1.state_ref = f32[136,2560]{1,0:T(8,128)S(1)} custom-call(s32[1]{0:T(128)} %bitcast.10.core_ref, bf16[320,512]{1,0:T(8,128)(2,1)S(1)} %slice.22.own_ref, bf16[320,512]{1,0:T(8,128)(2,1)S(1)} %collective-permute-done.3.pair_ref, bf16[320,256]{1,0:T(8,128)(2,1)S(1)} %slice.23.kv_ref.rest_0_), custom_call_target="tpu_custom_call" | custom-call | flops 419430400 | bytes 3145728 | tf_op jit(solution)/shard_map/first/pallas_call | solution.py:258
  112.2 4.8 %more.4.state_ref = f32[136,2560]{1,0:T(8,128)S(1)} custom-call(s32[3]{0:T(128)S(1)} %add_convert_fusion.flag_ref, bf16[320,512]{1,0:T(8,128)(2,1)S(1)} %slice.22.own_ref, bf16[320,512]{1,0:T(8,128)(2,1)S(1)} %collective-permute-done.3.pair_ref, f32[136,2560]{1,0:T(8,128)S(1)} %first.1.state_ref, ...), custom_call_target="tpu_custom_call" | custom-call | flops 1258291200 | bytes 3145728 | tf_op jit(solution)/shard_map/more/pallas_call | solution.py:310
  117.0 0.3 collective-permute-start.12
  117.3 4.0 %collective-permute-done.8.rest_1_.rest_6_ = bf16[640,256]{1,0:T(8,128)(2,1)S(1)} collective-permute-done((bf16[640,256]{1,0:T(8,128)(2,1)S(1)}, bf16[640,256]{1,0:T(8,128)(2,1)S(1)}, u32[]{:S(2)}, u32[]{:S(2)}) %collective-permute-start.8) | collective-permute-done | bytes 327712 | tf_op jit(solution)/shard_map/ppermute | solution.py:400
  121.3 9.6 %more.5.state_ref = f32[136,2560]{1,0:T(8,128)S(1)} custom-call(s32[3]{0:T(128)S(1)} %pad_add_fusion.1.flag_ref, bf16[320,512]{1,0:T(8,128)(2,1)S(1)} %slice.22.own_ref, bf16[320,512]{1,0:T(8,128)(2,1)S(1)} %collective-permute-done.3.pair_ref, f32[136,2560]{1,0:T(8,128)S(1)} %more.4.state_ref, bf16[640,256]{1,0:T(8,128)(2,1)S(1)} %collective-permute-done.7.rest_0_.rest_4_, ...), custom_call_target="tpu_custom_call" | custom-call | flops 2516582400 | bytes 3145728 | tf_op jit(solution)/shard_map/more/pallas_call | solution.py:310
  131.0 6.6 %more.6.state_ref = f32[136,2560]{1,0:T(8,128)S(1)} custom-call(s32[2]{0:T(128)S(1)} %pad_add_fusion.flag_ref, bf16[320,512]{1,0:T(8,128)(2,1)S(1)} %slice.22.own_ref, bf16[320,512]{1,0:T(8,128)(2,1)S(1)} %collective-permute-done.3.pair_ref, f32[136,2560]{1,0:T(8,128)S(1)} %more.5.state_ref, bf16[640,256]{1,0:T(8,128)(2,1)S(1)} %collective-permute-done.10.rest_0_.rest_7_, ...), custom_call_target="tpu_custom_call" | custom-call | flops 1677721600 | bytes 3145728 | tf_op jit(solution)/shard_map/more/pallas_call | solution.py:310
  137.7 4.0 %more.7 = (f32[136,1280]{1,0:T(8,128)S(1)}, f32[136,1280]{1,0:T(8,128)}) custom-call(s32[1]{0:T(128)} %bitcast.flag_ref, bf16[320,512]{1,0:T(8,128)(2,1)S(1)} %slice.22.own_ref, bf16[320,512]{1,0:T(8,128)(2,1)S(1)} %collective-permute-done.3.pair_ref, f32[136,2560]{1,0:T(8,128)S(1)} %more.6.state_ref, ...), custom_call_target="tpu_custom_call" | custom-call | flops 838860800 | bytes 3145728 | tf_op jit(solution)/shard_map/more/pallas_call | solution.py:310
  141.8 0.9 copy-done.4
  142.6 1.2 collective-permute-start.13
  144.0 0.1 reshape.146.code_ref
  144.1 0.9 copy-done.7
  145.0 0.9 copy-done.9
  145.9 0.9 copy-done.11
  146.8 1.0 copy-done.14
  147.8 1.0 copy-done.16
  148.8 1.0 copy-done.18
  149.8 1.0 copy-done.20
  150.7 1.0 copy-done.22
  151.7 1.0 copy-done.24
  152.7 1.6 pages.1
  154.4 1.0 and_reduce_fusion
  155.4 0.3 collective-permute-done.14
  155.7 0.9 broadcast_select_fusion
  156.7 2.0 %finish.1 = bf16[320,512]{1,0:T(8,128)(2,1)} custom-call(f32[136,1280]{1,0:T(8,128)S(1)} %copy-done.5, f32[136,1280]{1,0:T(8,128)} %collective-permute-done.13.got_ref), custom_call_target="tpu_custom_call" | custom-call | tf_op jit(solution)/shard_map/finish/pallas_call | solution.py:340
  (82 shorter events, 1.1 us)
Async XLA Ops:
  7.2 36.1 %copy-start = (bf16[320,5120]{1,0:T(8,128)(2,1)S(1)}, bf16[320,5120]{1,0:T(8,128)(2,1)}, u32[]{:S(2)}) copy-start(bf16[320,5120]{1,0:T(8,128)(2,1)} %table_ref.1) | copy-start | bytes 9830404
  7.2 71.8 %all-gather.2.cloned.1.call-start = ((), (), s32[]{:S(2)}) async-start(), calls=%async_computation.1 | async-start | bytes 8110080 | tf_op jit(solution)/shard_map/all_gather | solution.py:484
  7.9 1.3 copy-start.12
  9.2 0.8 copy-start.26
  12.1 13.1 %all-to-all-start = ((f32[32,1,512]{2,1,0:T(1,128)}), f32[32,1,512]{2,1,0:T(1,128)S(1)}, u32[]{:S(2)}, u32[]{:S(2)}) async-start(f32[32,1,512]{2,1,0:T(1,128)} %all_to_all.8), calls=%async_computation | async-start | bytes 131072 | tf_op jit(solution)/shard_map/all_to_all | solution.py:492
  26.2 1.0 copy-start.2
  27.2 1.0 copy-start.3
  28.8 7.0 %collective-permute-start = (f32[16,384]{1,0:T(8,128)S(1)}, f32[16,384]{1,0:T(8,128)S(1)}, u32[]{:S(2)}, u32[]{:S(2)}) collective-permute-start(f32[16,384]{1,0:T(8,128)S(1)} %place.1), channel_id=1, source_target_pairs={{0,1},{1,0},{2,3},{3,2},{4,5},{5,4},{6,7},{7,6},{8,9},{9,8},{10,11... | collective-permute-start | bytes 73736 | tf_op jit(solution)/shard_map/ppermute | solution.py:498
  35.8 3.1 %collective-permute-start.1 = (f32[16,384]{1,0:T(8,128)S(1)}, f32[16,384]{1,0:T(8,128)S(1)}, u32[]{:S(2)}, u32[]{:S(2)}) collective-permute-start(f32[16,384]{1,0:T(8,128)S(1)} %add.131), channel_id=1, source_target_pairs={{0,2},{1,3},{2,0},{3,1},{4,6},{5,7},{6,4},{7,5},{8,10},{9,11},{10,... | collective-permute-start | bytes 73736 | tf_op jit(solution)/shard_map/ppermute | solution.py:498
  38.9 4.3 %collective-permute-start.2 = (f32[16,384]{1,0:T(8,128)S(1)}, f32[16,384]{1,0:T(8,128)S(1)}, u32[]{:S(2)}, u32[]{:S(2)}) collective-permute-start(f32[16,384]{1,0:T(8,128)S(1)} %add.132), channel_id=1, source_target_pairs={{0,4},{1,5},{2,6},{3,7},{4,0},{5,1},{6,2},{7,3},{8,12},{9,13},{10,... | collective-permute-start | bytes 73736 | tf_op jit(solution)/shard_map/ppermute | solution.py:498
  43.2 0.9 copy-start.25
  48.9 1.8 %copy-start.1 = (bf16[320,5120]{1,0:T(8,128)(2,1)}, bf16[320,5120]{1,0:T(8,128)(2,1)S(1)}, u32[]{:S(2)}) copy-start(bf16[320,5120]{1,0:T(8,128)(2,1)S(1)} %hidden.1) | copy-start | bytes 9830404
  85.9 20.0 %collective-permute-start.5 = (bf16[320,256]{1,0:T(8,128)(2,1)S(1)}, bf16[320,256]{1,0:T(8,128)(2,1)S(1)}, u32[]{:S(2)}, u32[]{:S(2)}) collective-permute-start(bf16[320,256]{1,0:T(8,128)(2,1)S(1)} %slice.23.kv_ref.rest_0_), channel_id=1, source_target_pairs={{0,32},{8,40},{16,48},{24,56},{32,0},{40,8},{48,16},{56,24},{64,96... | collective-permute-start | bytes 491528 | tf_op jit(solution)/shard_map/ppermute | solution.py:404
  87.1 16.0 %collective-permute-start.4 = (bf16[320,256]{1,0:T(8,128)(2,1)S(1)}, bf16[320,256]{1,0:T(8,128)(2,1)S(1)}, u32[]{:S(2)}, u32[]{:S(2)}) collective-permute-start(bf16[320,256]{1,0:T(8,128)(2,1)S(1)} %slice.23.kv_ref.rest_0_), channel_id=1, source_target_pairs={{0,16},{8,24},{16,32},{24,40},{32,48},{40,56},{48,0},{56,8},{64,80... | collective-permute-start | bytes 491528 | tf_op jit(solution)/shard_map/ppermute | solution.py:404
  88.1 19.3 %collective-permute-start.6 = (bf16[320,256]{1,0:T(8,128)(2,1)S(1)}, bf16[320,256]{1,0:T(8,128)(2,1)S(1)}, u32[]{:S(2)}, u32[]{:S(2)}) collective-permute-start(bf16[320,256]{1,0:T(8,128)(2,1)S(1)} %slice.23.kv_ref.rest_0_), channel_id=1, source_target_pairs={{0,48},{8,56},{16,0},{24,8},{32,16},{40,24},{48,32},{56,40},{64,11... | collective-permute-start | bytes 491528 | tf_op jit(solution)/shard_map/ppermute | solution.py:404
  88.7 18.8 %collective-permute-start.3 = (bf16[320,512]{1,0:T(8,128)(2,1)S(1)}, bf16[320,512]{1,0:T(8,128)(2,1)S(1)}, u32[]{:S(2)}, u32[]{:S(2)}) collective-permute-start(bf16[320,512]{1,0:T(8,128)(2,1)S(1)} %slice.22.own_ref), channel_id=1, source_target_pairs={{0,8},{8,0},{16,24},{24,16},{32,40},{40,32},{48,56},{56,48},{64,72... | collective-permute-start | bytes 983048 | tf_op jit(solution)/shard_map/ppermute | solution.py:408
  103.1 13.9 %copy-start.6 = (bf16[320,256]{1,0:T(8,128)(2,1)}, bf16[320,256]{1,0:T(8,128)(2,1)S(1)}, u32[]{:S(2)}) copy-start(bf16[320,256]{1,0:T(8,128)(2,1)S(1)} %collective-permute-done.4.rest_0_.rest_1_) | copy-start | bytes 491524
  103.1 13.9 %collective-permute-start.9 = (bf16[640,256]{1,0:T(8,128)(2,1)S(1)}, bf16[640,256]{1,0:T(8,128)(2,1)S(1)}, u32[]{:S(2)}, u32[]{:S(2)}) collective-permute-start(bf16[640,256]{1,0:T(8,128)(2,1)S(1)} %pad_maximum_fusion), channel_id=1, source_target_pairs={{0,128},{8,136},{16,144},{24,152},{32,160},{40,168},{48,176},{56,1... | collective-permute-start | bytes 983048 | tf_op jit(solution)/shard_map/ppermute | solution.py:400
  104.7 16.7 %collective-permute-start.8 = (bf16[640,256]{1,0:T(8,128)(2,1)S(1)}, bf16[640,256]{1,0:T(8,128)(2,1)S(1)}, u32[]{:S(2)}, u32[]{:S(2)}) collective-permute-start(bf16[640,256]{1,0:T(8,128)(2,1)S(1)} %pad_maximum_fusion), channel_id=1, source_target_pairs={{0,192},{8,200},{16,208},{24,216},{32,224},{40,232},{48,240},{56,2... | collective-permute-start | bytes 983048 | tf_op jit(solution)/shard_map/ppermute | solution.py:400
  105.9 11.0 %copy-start.8 = (bf16[320,256]{1,0:T(8,128)(2,1)}, bf16[320,256]{1,0:T(8,128)(2,1)S(1)}, u32[]{:S(2)}) copy-start(bf16[320,256]{1,0:T(8,128)(2,1)S(1)} %collective-permute-done.5.rest_1_.rest_2_) | copy-start | bytes 491524
  105.9 15.4 %collective-permute-start.7 = (bf16[640,256]{1,0:T(8,128)(2,1)S(1)}, bf16[640,256]{1,0:T(8,128)(2,1)S(1)}, u32[]{:S(2)}, u32[]{:S(2)}) collective-permute-start(bf16[640,256]{1,0:T(8,128)(2,1)S(1)} %pad_maximum_fusion), channel_id=1, source_target_pairs={{0,64},{8,72},{16,80},{24,88},{32,96},{40,104},{48,112},{56,120},{... | collective-permute-start | bytes 983048 | tf_op jit(solution)/shard_map/ppermute | solution.py:400
  107.4 9.6 %copy-start.10 = (bf16[320,256]{1,0:T(8,128)(2,1)}, bf16[320,256]{1,0:T(8,128)(2,1)S(1)}, u32[]{:S(2)}) copy-start(bf16[320,256]{1,0:T(8,128)(2,1)S(1)} %collective-permute-done.6.rest_2_.rest_3_) | copy-start | bytes 491524
  107.4 23.6 %collective-permute-start.11 = (bf16[640,256]{1,0:T(8,128)(2,1)S(1)}, bf16[640,256]{1,0:T(8,128)(2,1)S(1)}, u32[]{:S(2)}, u32[]{:S(2)}) collective-permute-start(bf16[640,256]{1,0:T(8,128)(2,1)S(1)} %constant_dynamic-update-slice_fusion), channel_id=1, source_target_pairs={{0,192},{8,200},{16,208},{24,216},{32,224},{40,232},{48,240},{56,2... | collective-permute-start | bytes 983048 | tf_op jit(solution)/shard_map/ppermute | solution.py:400
  107.5 23.4 %collective-permute-start.10 = (bf16[640,256]{1,0:T(8,128)(2,1)S(1)}, bf16[640,256]{1,0:T(8,128)(2,1)S(1)}, u32[]{:S(2)}, u32[]{:S(2)}) collective-permute-start(bf16[640,256]{1,0:T(8,128)(2,1)S(1)} %constant_dynamic-update-slice_fusion), channel_id=1, source_target_pairs={{0,64},{8,72},{16,80},{24,88},{32,96},{40,104},{48,112},{56,120},{... | collective-permute-start | bytes 983048 | tf_op jit(solution)/shard_map/ppermute | solution.py:400
  117.0 13.9 %copy-start.13 = (bf16[640,256]{1,0:T(8,128)(2,1)}, bf16[640,256]{1,0:T(8,128)(2,1)S(1)}, u32[]{:S(2)}) copy-start(bf16[640,256]{1,0:T(8,128)(2,1)S(1)} %collective-permute-done.9.rest_2_.rest_5_) | copy-start | bytes 983044
  117.0 20.6 %collective-permute-start.12 = (bf16[640,256]{1,0:T(8,128)(2,1)S(1)}, bf16[640,256]{1,0:T(8,128)(2,1)S(1)}, u32[]{:S(2)}, u32[]{:S(2)}) collective-permute-start(bf16[640,256]{1,0:T(8,128)(2,1)S(1)} %constant_dynamic-update-slice_fusion), channel_id=1, source_target_pairs={{0,128},{8,136},{16,144},{24,152},{32,160},{40,168},{48,176},{56,1... | collective-permute-start | bytes 983048 | tf_op jit(solution)/shard_map/ppermute | solution.py:400
  121.3 9.6 %copy-start.15 = (bf16[640,256]{1,0:T(8,128)(2,1)}, bf16[640,256]{1,0:T(8,128)(2,1)S(1)}, u32[]{:S(2)}) copy-start(bf16[640,256]{1,0:T(8,128)(2,1)S(1)} %collective-permute-done.8.rest_1_.rest_6_) | copy-start | bytes 983044
  121.3 9.6 %copy-start.17 = (bf16[640,256]{1,0:T(8,128)(2,1)}, bf16[640,256]{1,0:T(8,128)(2,1)S(1)}, u32[]{:S(2)}) copy-start(bf16[640,256]{1,0:T(8,128)(2,1)S(1)} %collective-permute-done.7.rest_0_.rest_4_) | copy-start | bytes 983044
  131.0 10.8 %copy-start.19 = (bf16[640,256]{1,0:T(8,128)(2,1)}, bf16[640,256]{1,0:T(8,128)(2,1)S(1)}, u32[]{:S(2)}) copy-start(bf16[640,256]{1,0:T(8,128)(2,1)S(1)} %collective-permute-done.11.rest_1_.rest_9_) | copy-start | bytes 983044
  131.0 10.8 %copy-start.21 = (bf16[640,256]{1,0:T(8,128)(2,1)}, bf16[640,256]{1,0:T(8,128)(2,1)S(1)}, u32[]{:S(2)}) copy-start(bf16[640,256]{1,0:T(8,128)(2,1)S(1)} %collective-permute-done.10.rest_0_.rest_7_) | copy-start | bytes 983044
  137.6 16.8 %copy-start.27 = (pred[32]{0:T(512)(128)(4,1)S(1)}, pred[32]{0:T(512)(128)(4,1)}, u32[]{:S(2)}) copy-start(pred[32]{0:T(512)(128)(4,1)} %fusion.1) | copy-start | bytes 100
  137.6 16.8 %copy-start.28 = (s32[40]{0:T(128)S(1)}, s32[40]{0:T(128)}, u32[]{:S(2)}) copy-start(s32[40]{0:T(128)} %iota_add_fusion) | copy-start | bytes 484
  137.7 6.3 %copy-start.23 = (bf16[640,256]{1,0:T(8,128)(2,1)}, bf16[640,256]{1,0:T(8,128)(2,1)S(1)}, u32[]{:S(2)}) copy-start(bf16[640,256]{1,0:T(8,128)(2,1)S(1)} %collective-permute-done.12.rest_0_.rest_8_) | copy-start | bytes 983044
  141.7 0.9 copy-start.4
  142.6 14.0 %collective-permute-start.13 = (f32[136,1280]{1,0:T(8,128)}, f32[136,1280]{1,0:T(8,128)}, u32[]{:S(2)}, u32[]{:S(2)}) collective-permute-start(f32[136,1280]{1,0:T(8,128)} %get-tuple-element.7), channel_id=1, source_target_pairs={{0,8},{8,0},{16,24},{24,16},{32,40},{40,32},{48,56},{56,48},{64,72... | collective-permute-start | bytes 2088968 | tf_op jit(solution)/shard_map/ppermute | solution.py:408
  144.1 0.9 copy-start.7
  145.0 0.9 copy-start.9
  145.9 0.9 copy-start.11
  146.8 1.0 copy-start.14
  147.8 1.0 copy-start.16
  148.8 1.0 copy-start.18
  149.8 1.0 copy-start.20
  150.7 1.0 copy-start.22
  151.7 1.0 copy-start.24
  152.7 4.0 %copy-start.5 = (f32[136,1280]{1,0:T(8,128)S(1)}, f32[136,1280]{1,0:T(8,128)}, u32[]{:S(2)}) copy-start(f32[136,1280]{1,0:T(8,128)} %copy-done.4) | copy-start | bytes 2088964
  154.2 1.5 collective-permute-start.14
Sparse Core Ops, SparseCore 0:
  9.9 69.0 all-gather.1

commit v4 on v3

--- a/solution.py
+++ b/solution.py
@@ -24,6 +24,8 @@
 TILE = 256
 QROWS = GROUP * BLK
 STATE = HD + 8
+RBLK = 160
+PIECES = 4
 VMEM = 24 * 1024 * 1024
 
 
@@ -157,9 +159,11 @@
         mean = jnp.sum(sq_ref[...], axis=1, keepdims=True) / (count * width)
         factor = lax.rsqrt(mean + 1e-05)
         for tile in range(count):
-            cut = slice(tile * width, (tile + 1) * width)
-            gain = gain_ref[:, cut].astype(jnp.float32)
-            out_ref[:, cut] = (hid_ref[tile] * factor * gain).astype(jnp.bfloat16)
+            gain = gain_ref[:, tile * width : (tile + 1) * width].astype(jnp.float32)
+            normed = hid_ref[tile] * factor * gain
+            for part in range(width // RBLK):
+                piece = normed[:, part * RBLK : (part + 1) * RBLK]
+                out_ref[tile * (width // RBLK) + part] = piece.astype(jnp.bfloat16)
 
 
 def normed_hidden(latent, conv_bias, embed_weight, position_table, norm_gain):
@@ -176,8 +180,8 @@
             pl.BlockSpec((BLK, width), lambda i: (0, i)),
             pl.BlockSpec((1, depth), lambda i: (0, 0)),
         ],
-        out_specs=pl.BlockSpec((BLK, depth), lambda i: (0, 0)),
-        out_shape=jax.ShapeDtypeStruct((BLK, depth), jnp.bfloat16),
+        out_specs=pl.BlockSpec((depth // RBLK, BLK, RBLK), lambda i: (0, 0, 0)),
+        out_shape=jax.ShapeDtypeStruct((depth // RBLK, BLK, RBLK), jnp.bfloat16),
         scratch_shapes=[
             pltpu.VMEM((steps, BLK, width), jnp.float32),
             pltpu.VMEM((BLK, 128), jnp.float32),
@@ -185,6 +189,54 @@
         compiler_params=params(dimension_semantics=("arbitrary",)),
         name="hidden",
     )(latent, conv_bias.reshape(LAT, 1), embed_weight, position_table, norm_gain.reshape(1, depth))
+
+
+def project_kernel(index_ref, normed_ref, weight_ref, out_ref, held_ref, sum_ref, sems):
+    rows = weight_ref.shape[0] // PIECES
+    copies = []
+    for piece in range(PIECES):
+        cut = pl.ds(piece * rows, rows)
+        copies.append(
+            pltpu.make_async_copy(weight_ref.at[cut, :], held_ref.at[cut, :], sems.at[piece])
+        )
+        copies[-1].start()
+    sum_ref[...] = jnp.zeros_like(sum_ref)
+    for piece in range(PIECES):
+        copies[piece].wait()
+
+        def body(step, carry, first=piece * rows // RBLK):
+            block = first + step
+            weight = held_ref[pl.ds(pl.multiple_of(block * RBLK, RBLK), RBLK), :]
+            sum_ref[...] += jnp.dot(
+                normed_ref[index_ref[block]], weight, preferred_element_type=jnp.float32
+            )
+            return carry
+
+        lax.fori_loop(0, rows // RBLK, body, 0)
+    out_ref[...] = sum_ref[...].astype(jnp.bfloat16)
+
+
+def project(index, normed, weight):
+    depth, width = weight.shape
+    return pl.pallas_call(
+        project_kernel,
+        in_specs=[
+            pl.BlockSpec(memory_space=pltpu.SMEM),
+            pl.BlockSpec(memory_space=pltpu.VMEM),
+            pl.BlockSpec(memory_space=pl.ANY),
+        ],
+        out_shape=jax.ShapeDtypeStruct((BLK, width), jnp.bfloat16),
+        scratch_shapes=[
+            pltpu.VMEM((depth, width), jnp.bfloat16),
+            pltpu.VMEM((BLK, width), jnp.float32),
+            pltpu.SemaphoreType.DMA((PIECES,)),
+        ],
+        compiler_params=params(),
+        cost_estimate=pl.CostEstimate(
+            flops=2 * BLK * depth * width, bytes_accessed=2 * depth * width, transcendentals=0
+        ),
+        name="project",
+    )(index, normed, weight)
 
 
 def attend_block(masked, partner_full, keys, values, q_ref, state_ref):
@@ -241,15 +293,11 @@
         state_ref[:HD, cut] = summed
 
 
-def set_queries(own_ref, pair_ref, q_ref):
+def first_kernel(core_ref, own_ref, pair_ref, kv_ref, state_ref, q_ref):
     for index, ref in enumerate((own_ref, pair_ref)):
         for head in range(GROUP):
             start = (index * GROUP + head) * BLK
             q_ref[start : start + BLK, :] = ref[:, head * HD : (head + 1) * HD]
-
-
-def first_kernel(core_ref, own_ref, pair_ref, kv_ref, state_ref, q_ref):
-    set_queries(own_ref, pair_ref, q_ref)
     state_ref[HD + 2 :, :] = jnp.zeros((STATE - HD - 2, 2 * QROWS), jnp.float32)
     attend_block(True, core_ref[0] == 0, kv_ref[:, :HD], kv_ref[:, HD:], q_ref, state_ref)
 
@@ -259,25 +307,26 @@
         first_kernel,
         in_specs=[pl.BlockSpec(memory_space=pltpu.SMEM)]
         + [pl.BlockSpec(memory_space=pltpu.VMEM)] * 3,
-        out_shape=jax.ShapeDtypeStruct((STATE, 2 * QROWS), jnp.float32),
-        scratch_shapes=[pltpu.VMEM((2 * QROWS, HD), jnp.bfloat16)],
+        out_shape=(
+            jax.ShapeDtypeStruct((STATE, 2 * QROWS), jnp.float32),
+            jax.ShapeDtypeStruct((2 * QROWS, HD), jnp.bfloat16),
+        ),
         compiler_params=params(),
         cost_estimate=cost(1),
         name="first",
     )(core.reshape(1), own, pair, kv)
 
 
-def more_kernel(unit, count, split, flag_ref, own_ref, pair_ref, state_ref, *rest):
+def more_kernel(count, split, flag_ref, q_ref, state_ref, *rest):
     arrays, rest = rest[:count], rest[count:]
     if split:
-        own_out_ref, pair_out_ref, q_ref, held_ref, sems, work_ref = rest
+        own_out_ref, pair_out_ref, held_ref, sems, work_ref = rest
     else:
-        work_ref, q_ref, held_ref, sems = rest
+        work_ref, held_ref, sems = rest
     copies = []
     for index, array in enumerate(arrays):
         copies.append(pltpu.make_async_copy(array, held_ref.at[index], sems.at[index]))
         copies[-1].start()
-    set_queries(own_ref, pair_ref, q_ref)
     work_ref[...] = state_ref[...]
     for copy in copies:
         copy.wait()
@@ -296,28 +345,27 @@
         pair_out_ref[...] = work_ref[:, QROWS:]
 
 
-def attend_more(flags, own, pair, state, arrays, split=False):
+def attend_more(flags, queries, state, arrays, split=False):
     unit, count = arrays[0].shape[0], len(arrays)
     half = jax.ShapeDtypeStruct((STATE, QROWS), jnp.float32)
     whole = jax.ShapeDtypeStruct((STATE, 2 * QROWS), jnp.float32)
     scratch = [
-        pltpu.VMEM((2 * QROWS, HD), jnp.bfloat16),
         pltpu.VMEM((count, unit, 2 * HD), jnp.bfloat16),
         pltpu.SemaphoreType.DMA((count,)),
     ]
     if split:
         scratch.append(pltpu.VMEM((STATE, 2 * QROWS), jnp.float32))
     return pl.pallas_call(
-        functools.partial(more_kernel, unit, count, split),
+        functools.partial(more_kernel, count, split),
         in_specs=[pl.BlockSpec(memory_space=pltpu.SMEM)]
-        + [pl.BlockSpec(memory_space=pltpu.VMEM)] * 3
+        + [pl.BlockSpec(memory_space=pltpu.VMEM)] * 2
         + [pl.BlockSpec(memory_space=pl.ANY)] * count,
         out_shape=(half, half) if split else whole,
         scratch_shapes=scratch,
         compiler_params=params(),
         cost_estimate=cost(count * unit // BLK),
         name="more",
-    )(flags, own, pair, state, *arrays)
+    )(flags, queries, state, *arrays)
 
 
 def finish_kernel(own_ref, got_ref, out_ref, row_ref):
@@ -347,8 +395,18 @@
 
 
 def page_kernel(place_ref, code_ref, *rest):
-    arrays, (own_ref, pair_ref, held_ref) = rest[:-3], rest[-3:]
+    count = (len(rest) - 4) // 2
+    remote, own_ref, pair_ref = rest[:count], rest[count], rest[count + 1]
+    held_ref, sems, arrays = rest[count + 2], rest[count + 3], rest[count + 4 :]
+    copies = [
+        pltpu.make_async_copy(remote[index], arrays[index], sems.at[index])
+        for index in range(count)
+    ]
+    for copy in copies:
+        copy.start()
     held_ref[...] = jnp.zeros_like(held_ref)
+    for copy in copies:
+        copy.wait()
     y, z, core = place_ref[0], place_ref[1], place_ref[2]
     for by_y in range(4):
         for by_z in range(4):
@@ -378,9 +436,13 @@
     return pl.pallas_call(
         page_kernel,
         in_specs=[pl.BlockSpec(memory_space=pltpu.SMEM)] * 2
-        + [pl.BlockSpec(memory_space=pltpu.VMEM)] * len(arrays),
+        + [pl.BlockSpec(memory_space=pl.ANY)] * len(arrays),
         out_shape=(out, out),
-        scratch_shapes=[pltpu.VMEM((2 * PAGES * PAGE, 2 * HD), jnp.float32)],
+        scratch_shapes=[
+            pltpu.VMEM((2 * PAGES * PAGE, 2 * HD), jnp.float32),
+            pltpu.SemaphoreType.DMA((len(arrays),)),
+        ]
+        + [pltpu.VMEM(array.shape, array.dtype) for array in arrays],
         compiler_params=params(),
         name="pages",
     )(place, codes, *arrays)
@@ -429,30 +491,57 @@
     return jnp.any(match, axis=(1, 2))
 
 
-def attention_and_pages(me, targets, qkv):
+def spread(value, groups):
+    by_z = {0: value}
+    for count in (1, 2, 3):
+        by_z[count] = along_z(value, count)
+    by_y = []
+    for group in groups:
+        parts = [by_z[count] for count in group]
+        parts = jnp.concatenate(parts, axis=0) if len(parts) > 1 else parts[0]
+        by_y.append({count: along_y(parts, count) for count in (1, 3, 2)})
+    return by_z, by_y
+
+
+def gather_rows(stacked):
+    groups = [[(y * 4 + z) * 2 + c for y in range(4) for c in range(2)] for z in range(4)]
+    return lax.all_gather(stacked, "seq", axis=0, tiled=True, axis_index_groups=groups)
+
+
+def stack_z(value):
+    parts = [value] + [along_z(value, count) for count in (1, 2, 3)]
+    return jnp.concatenate(parts, axis=0)
+
+
+def row_order(me):
+    z = (me // 2) % 4
+    order = [(y * 4 + ((z - k) & 3)) * 2 + c for y in range(4) for c in range(2) for k in range(4)]
+    return jnp.stack(order)
+
+
+def attention_and_pages(me, targets, normed, kv_weight, query_weight):
     core, z, y = me % 2, (me // 2) % 4, me // 8
-    queries, kv = qkv[:, : GROUP * HD], qkv[:, GROUP * HD :]
-    pair = other_core(queries)
-    by_z = {0: kv}
-    for count in (1, 2, 3):
-        by_z[count] = along_z(kv, count)
-    near = jnp.concatenate([kv, by_z[1]], axis=0)
-    near = {count: along_y(near, count) for count in (1, 3, 2)}
-    far = jnp.concatenate([by_z[2], by_z[3]], axis=0)
-    far = {count: along_y(far, count) for count in (1, 3, 2)}
+    order = row_order(me)
+    kv = project(order, normed, kv_weight)
+    by_z, (near, far) = spread(kv, ((0, 1), (2, 3)))
+    order, near[1], near[2], near[3] = lax.optimization_barrier(
+        (order, near[1], near[2], near[3])
+    )
+    own_queries = project(order, normed, query_weight)
+    pair_queries = other_core(own_queries)
 
     def flag(*conditions):
         return jnp.stack([jnp.asarray(value, jnp.int32) for value in conditions])
 
-    state = attend_first(core, queries, pair, kv)
+    state, queries = attend_first(core, own_queries, pair_queries, kv)
     state = attend_more(
-        flag(z >= 1, z >= 2, z >= 3), queries, pair, state, [by_z[1], by_z[2], by_z[3]]
+        flag(z >= 1, z >= 2, z >= 3), queries, state, [by_z[1], by_z[2], by_z[3]]
     )
     state = attend_more(
-        flag(y >= 1, y >= 3, y >= 2), queries, pair, state, [near[1], near[3], near[2]]
+        flag(y >= 1, y >= 3, y >= 2), queries, state, [near[1], near[3], near[2]]
     )
-    state = attend_more(flag(y >= 1, y >= 3), queries, pair, state, [far[1], far[3]])
-    own, sent = attend_more(flag(y >= 2), queries, pair, state, [far[2]], split=True)
+    state = attend_more(flag(y >= 1, y >= 3), queries, state, [far[1], far[3]])
+    own, sent = attend_more(flag(y >= 2), queries, state, [far[2]], split=True)
     got = other_core(sent)
 
     arrays = [by_z[count] for count in range(4)]
@@ -481,8 +570,11 @@
     me = lax.axis_index("seq").astype(jnp.int32)
     tensor = lax.axis_index("tensor").astype(jnp.int32)
     tensor_count = lax.axis_size("tensor")
-    weight = lax.all_gather(qkv_weight, "seq", axis=0, tiled=True)
+    kv_weight = stack_z(qkv_weight[:, GROUP * HD :])
+    query_weight = stack_z(qkv_weight[:, : GROUP * HD])
     parts = partial_latents(features, conv_weight)
+    parts, kv_weight = lax.optimization_barrier((parts, kv_weight))
+    kv_weight = gather_rows(kv_weight)
     own = parts[: FRAMES * EXT].reshape(FRAMES, EXT * LAT)
     target = (page_owner * PAGES + page_slot).astype(jnp.float32)
     target = jnp.broadcast_to(target, (FRAMES, PAGES))
@@ -490,6 +582,8 @@
     message = jnp.pad(message, ((0, 0), (0, 512 - message.shape[1])))
     message = jnp.broadcast_to(message[:, None], (FRAMES, SEQ // FRAMES, 512)).reshape(SEQ, 512)
     message = lax.all_to_all(message, "seq", split_axis=0, concat_axis=0, tiled=True)
+    message, query_weight = lax.optimization_barrier((message, query_weight))
+    query_weight = gather_rows(query_weight)
     targets = message[:, EXT * LAT : EXT * LAT + PAGES].astype(jnp.int32)
     offset = tensor - me % (SEQ // FRAMES)
     latent = place_latents(message[:, : EXT * LAT].reshape(SEQ * EXT, LAT), offset)
@@ -497,8 +591,7 @@
         swap = [(i, i ^ bit) for i in range(tensor_count)]
         latent = latent + lax.ppermute(latent, "tensor", swap)
     normed = normed_hidden(latent, conv_bias, embed_weight, position_table, norm_gain)
-    qkv = jnp.dot(normed, weight, preferred_element_type=jnp.float32).astype(jnp.bfloat16)
-    return attention_and_pages(me, targets, qkv)
+    return attention_and_pages(me, targets, normed, kv_weight, query_weight)
 
 
 def solution(mesh):

time: 166 us -> 170 us (1.024)
  the two profiles are of different devices: /device:TPU:89 before, /device:TPU:25 now
where the time goes in v4:
time: 170 us; the launch traced here: 169 us
  Pallas kernels  49.6 us (29%)
  waiting for transfers between devices  35.6 us (21%)
  starting transfers between devices  35.5 us (21%)
  local copies, waits for them, and re-layouts  23.4 us (14%)
  between operations  14.4 us (8%)
  other arithmetic  10.6 us (6%)
    pallas_call x4, Pallas kernels, attend_more(): pl.pallas_call(functools.partial(more_kernel, count, split), in_specs=[pl...  21.3 us
    unnamed x48, local copies, waits for them, and re-layouts  18.6 us
    ppermute x6, waiting for transfers between devices, along_y(): lax.ppermute(value, 'seq', moves(lambda y, z, c: ((y + count) % 4, z, c)))  16.7 us
    pallas_call x2, Pallas kernels, project(): pl.pallas_call(project_kernel, in_specs=[pl.BlockSpec(memory_space=pltpu....  16 us
    ppermute x9, waiting for transfers between devices, along_z(): lax.ppermute(value, 'seq', moves(lambda y, z, c: (y, (z + count) % 4, c)))  13.1 us
    ppermute x3, starting transfers between devices, on_device(): latent = latent + lax.ppermute(latent, 'tensor', swap)  9.46 us
    ppermute x9, starting transfers between devices, along_z(): lax.ppermute(value, 'seq', moves(lambda y, z, c: (y, (z + count) % 4, c)))  8.85 us
    all_to_all x1, starting transfers between devices, on_device(): lax.all_to_all(message, 'seq', split_axis=0, concat_axis=0, tiled=True)  8.03 us
  transfers between devices with their start and end apart: 24, of which 11 were waited for; matrix products, arithmetic and copies ran while one was open for 8% of the time, Pallas kernels for 26%

profile of v4, /device:TPU:25, one launch (start us, length us, event | category | flops | bytes accessed | tf_op | source)
XLA Modules:
  0.0 169.1 jit_solution(9697388955299519323)
XLA Ops:
  7.2 0.9 slice.15
  8.1 4.3 %collective-permute-start.2 = (bf16[160,256]{1,0:T(8,128)(2,1)S(1)}, bf16[160,256]{1,0:T(8,128)(2,1)S(1)}, u32[]{:S(2)}, u32[]{:S(2)}) collective-permute-start(bf16[160,256]{1,0:T(8,128)(2,1)S(1)} %slice.15), channel_id=1, source_target_pairs={{0,48},{8,56},{16,0},{24,8},{32,16},{40,24},{48,32},{56,40},{64,11... | collective-permute-start | bytes 245768 | tf_op jit(solution)/shard_map/ppermute | solution.py:466
  12.8 1.0 copy-done.8
  13.9 0.8 copy-done.14
  15.2 5.1 %collective-permute-done.1 = bf16[160,256]{1,0:T(8,128)(2,1)S(1)} collective-permute-done((bf16[160,256]{1,0:T(8,128)(2,1)S(1)}, bf16[160,256]{1,0:T(8,128)(2,1)S(1)}, u32[]{:S(2)}, u32[]{:S(2)}) %collective-permute-start.1) | collective-permute-done | bytes 81952 | tf_op jit(solution)/shard_map/ppermute | solution.py:466
  20.3 0.7 pad_maximum_fusion.1
  21.2 1.2 collective-permute-start.4
  22.4 1.4 collective-permute-start.3
  24.0 0.7 all_to_all.8
  24.7 8.0 %all-to-all-start = ((f32[32,1,512]{2,1,0:T(1,128)}), f32[32,1,512]{2,1,0:T(1,128)}, u32[]{:S(2)}, u32[]{:S(2)}) async-start(f32[32,1,512]{2,1,0:T(1,128)} %all_to_all.8), calls=%async_computation | async-start | bytes 131072 | tf_op jit(solution)/shard_map/all_to_all | solution.py:584
  32.8 3.4 %collective-permute-done.4 = bf16[160,512]{1,0:T(8,128)(2,1)S(1)} collective-permute-done((bf16[160,512]{1,0:T(8,128)(2,1)S(1)}, bf16[160,512]{1,0:T(8,128)(2,1)S(1)}, u32[]{:S(2)}, u32[]{:S(2)}) %collective-permute-start.4) | collective-permute-done | bytes 163872 | tf_op jit(solution)/shard_map/ppermute | solution.py:466
  36.2 0.9 pad_maximum_fusion
  37.1 2.5 %all-to-all-done = f32[32,1,512]{2,1,0:T(1,128)} async-done(((f32[32,1,512]{2,1,0:T(1,128)}), f32[32,1,512]{2,1,0:T(1,128)}, u32[]{:S(2)}, u32[]{:S(2)}) %all-to-all-start) | async-done | bytes 65568 | tf_op jit(solution)/shard_map/all_to_all | solution.py:584
  39.6 1.0 copy.36
  40.7 0.7 fusion
  41.4 1.0 copy.27.token_ref
  42.4 0.6 iota_multiply_fusion
  43.1 0.5 iota_add_fusion
  43.7 0.6 iota_compare_fusion
  44.3 0.9 reshape.143.parts_ref
  45.2 1.0 copy-done.6
  46.2 1.0 copy-done.7
  47.3 0.6 place.1
  47.8 5.5 %collective-permute-start.6 = (f32[16,384]{1,0:T(8,128)S(1)}, f32[16,384]{1,0:T(8,128)}, u32[]{:S(2)}, u32[]{:S(2)}) collective-permute-start(f32[16,384]{1,0:T(8,128)S(1)} %place.1), channel_id=1, source_target_pairs={{0,1},{1,0},{2,3},{3,2},{4,5},{5,4},{6,7},{7,6},{8,9},{9,8},{10,11... | collective-permute-start | bytes 73736 | tf_op jit(solution)/shard_map/ppermute | solution.py:592
  53.9 0.8 collective-permute-done.6
  54.7 0.7 add.261
  55.5 1.2 collective-permute-start.7
  56.7 1.4 collective-permute-done.7
  58.1 0.6 add.262
  58.7 2.7 %collective-permute-start.8 = (f32[16,384]{1,0:T(8,128)}, f32[16,384]{1,0:T(8,128)}, u32[]{:S(2)}, u32[]{:S(2)}) collective-permute-start(f32[16,384]{1,0:T(8,128)} %add.262), channel_id=1, source_target_pairs={{0,4},{1,5},{2,6},{3,7},{4,0},{5,1},{6,2},{7,3},{8,12},{9,13},{10,... | collective-permute-start | bytes 73736 | tf_op jit(solution)/shard_map/ppermute | solution.py:592
  61.6 0.7 reshape.145.gain_ref
  62.5 0.8 collective-permute-done.8
  63.2 0.8 add.263.latent_ref
  64.0 4.8 %hidden.1.normed_ref = bf16[32,320,160]{2,1,0:T(8,128)(2,1)S(1)} custom-call(f32[16,384]{1,0:T(8,128)S(1)} %add.263.latent_ref, f32[16,1]{1,0:T(8,128)S(1)} %copy.28.bias_ref, bf16[16,5120]{1,0:T(8,128)(2,1)S(1)} %copy-done.13, bf16[320,5120]{1,0:T(8,128)(2,1)S(1)} %copy-done.4, bf16[1,5120]{1,0:T(2,128)(2,1)S(1)} %reshape.145.gain_ref), custom_call_target="tpu_custom_call" | custom-call | tf_op jit(solution)/shard_map/hidden/pallas_call | solution.py:173
  68.8 2.4 %copy-done = bf16[32,320,160]{2,1,0:T(8,128)(2,1)} copy-done((bf16[32,320,160]{2,1,0:T(8,128)(2,1)}, bf16[32,320,160]{2,1,0:T(8,128)(2,1)S(1)}, u32[]{:S(2)}) %copy-start) | copy-done | bytes 3276824
  71.2 2.6 %copy-done.1 = bf16[32,320,160]{2,1,0:T(8,128)(2,1)S(1)} copy-done((bf16[32,320,160]{2,1,0:T(8,128)(2,1)S(1)}, bf16[32,320,160]{2,1,0:T(8,128)(2,1)}, u32[]{:S(2)}) %copy-start.1) | copy-done | bytes 3276824
  73.8 1.8 %copy-done.5 = bf16[5120,256]{1,0:T(8,128)(2,1)S(1)} copy-done((bf16[5120,256]{1,0:T(8,128)(2,1)S(1)}, bf16[5120,256]{1,0:T(8,128)(2,1)}, u32[]{:S(2)}) %copy-start.5) | copy-done | bytes 2621464
  75.6 7.6 %project.2.kv_ref.rest_0_ = bf16[320,256]{1,0:T(8,128)(2,1)S(1)} custom-call(s32[32]{0:T(128)S(1)} %stack.195.index_ref, bf16[32,320,160]{2,1,0:T(8,128)(2,1)S(1)} %copy-done.1, bf16[5120,256]{1,0:T(8,128)(2,1)S(1)} %copy-done.5), custom_call_target="tpu_custom_call" | custom-call | flops 838860800 | bytes 2621440 | tf_op jit(solution)/shard_map/project/pallas_call | solution.py:221
  83.7 1.2 convert_reduce_fusion
  84.9 4.5 %collective-permute-done.9.rest_0_.rest_1_ = bf16[320,256]{1,0:T(8,128)(2,1)S(1)} collective-permute-done((bf16[320,256]{1,0:T(8,128)(2,1)S(1)}, bf16[320,256]{1,0:T(8,128)(2,1)S(1)}, u32[]{:S(2)}, u32[]{:S(2)}) %collective-permute-start.9) | collective-permute-done | bytes 163872 | tf_op jit(solution)/shard_map/ppermute | solution.py:466
  89.4 2.3 %collective-permute-start.10 = (bf16[640,256]{1,0:T(8,128)(2,1)S(1)}, bf16[640,256]{1,0:T(8,128)(2,1)S(1)}, u32[]{:S(2)}, u32[]{:S(2)}) collective-permute-start(bf16[640,256]{1,0:T(8,128)(2,1)S(1)} %pad_maximum_fusion.2), channel_id=1, source_target_pairs={{0,64},{8,72},{16,80},{24,88},{32,96},{40,104},{48,112},{56,120},{... | collective-permute-start | bytes 983048 | tf_op jit(solution)/shard_map/ppermute | solution.py:462
  91.8 0.6 collective-permute-start.12
  92.8 0.9 collective-permute-start.15
  93.7 5.7 %collective-permute-done.10.rest_0_.rest_4_ = bf16[640,256]{1,0:T(8,128)(2,1)S(1)} collective-permute-done((bf16[640,256]{1,0:T(8,128)(2,1)S(1)}, bf16[640,256]{1,0:T(8,128)(2,1)S(1)}, u32[]{:S(2)}, u32[]{:S(2)}) %collective-permute-start.10) | collective-permute-done | bytes 327712 | tf_op jit(solution)/shard_map/ppermute | solution.py:462
  99.4 8.0 %collective-permute-done.12.rest_1_.rest_6_ = bf16[640,256]{1,0:T(8,128)(2,1)S(1)} collective-permute-done((bf16[640,256]{1,0:T(8,128)(2,1)S(1)}, bf16[640,256]{1,0:T(8,128)(2,1)S(1)}, u32[]{:S(2)}, u32[]{:S(2)}) %collective-permute-start.12) | collective-permute-done | bytes 327712 | tf_op jit(solution)/shard_map/ppermute | solution.py:462
  107.4 2.5 %copy-done.2 = bf16[32,320,160]{2,1,0:T(8,128)(2,1)S(1)} copy-done((bf16[32,320,160]{2,1,0:T(8,128)(2,1)S(1)}, bf16[32,320,160]{2,1,0:T(8,128)(2,1)}, u32[]{:S(2)}) %copy-start.2) | copy-done | bytes 3276824
  109.9 2.5 %copy-done.3 = bf16[5120,512]{1,0:T(8,128)(2,1)S(1)} copy-done((bf16[5120,512]{1,0:T(8,128)(2,1)S(1)}, bf16[5120,512]{1,0:T(8,128)(2,1)}, u32[]{:S(2)}) %copy-start.3) | copy-done | bytes 5242904
  112.4 8.4 %project.3.own_ref = bf16[320,512]{1,0:T(8,128)(2,1)S(1)} custom-call(s32[32]{0:T(128)S(1)} %stack.195.index_ref, bf16[32,320,160]{2,1,0:T(8,128)(2,1)S(1)} %copy-done.2, bf16[5120,512]{1,0:T(8,128)(2,1)S(1)} %copy-done.3), custom_call_target="tpu_custom_call" | custom-call | flops 1677721600 | bytes 5242880 | tf_op jit(solution)/shard_map/project/pallas_call | solution.py:221
  120.8 2.9 %collective-permute-start.13 = (bf16[320,512]{1,0:T(8,128)(2,1)S(1)}, bf16[320,512]{1,0:T(8,128)(2,1)S(1)}, u32[]{:S(2)}, u32[]{:S(2)}) collective-permute-start(bf16[320,512]{1,0:T(8,128)(2,1)S(1)} %project.3.own_ref), channel_id=1, source_target_pairs={{0,8},{8,0},{16,24},{24,16},{32,40},{40,32},{48,56},{56,48},{64,72... | collective-permute-start | bytes 983048 | tf_op jit(solution)/shard_map/ppermute | solution.py:470
  123.7 0.6 collective-permute-start.16
  124.3 0.9 collective-permute-start.17
  125.6 2.0 %first.1 = (f32[136,2560]{1,0:T(8,128)S(1)}, bf16[2560,128]{1,0:T(8,128)(2,1)S(1)}) custom-call(s32[1]{0:T(128)} %bitcast.1.core_ref, bf16[320,512]{1,0:T(8,128)(2,1)S(1)} %project.3.own_ref, bf16[320,512]{1,0:T(8,128)(2,1)S(1)} %collective-permute-done.13.pair_ref, bf16[320,256]{1,0:T(8,128)(2,1)S(1)} %project.2.kv_ref.rest_0_), custom_call_target="tpu_custom_call" | custom-call | flops 419430400 | bytes 3145728 | tf_op jit(solution)/shard_map/first/pallas_call | solution.py:306
  127.6 1.3 more.4.state_ref
  129.0 9.5 %more.5.state_ref = f32[136,2560]{1,0:T(8,128)S(1)} custom-call(s32[3]{0:T(128)S(1)} %pad_add_fusion.1.flag_ref, bf16[2560,128]{1,0:T(8,128)(2,1)S(1)} %get-tuple-element.21.q_ref, f32[136,2560]{1,0:T(8,128)S(1)} %more.4.state_ref, bf16[640,256]{1,0:T(8,128)(2,1)S(1)} %collective-permute-done.10.rest_0_.rest_4_, ...), custom_call_target="tpu_custom_call" | custom-call | flops 2516582400 | bytes 3145728 | tf_op jit(solution)/shard_map/more/pallas_call | solution.py:358
  138.5 3.1 %collective-permute-done.17.rest_1_.rest_9_ = bf16[640,256]{1,0:T(8,128)(2,1)S(1)} collective-permute-done((bf16[640,256]{1,0:T(8,128)(2,1)S(1)}, bf16[640,256]{1,0:T(8,128)(2,1)S(1)}, u32[]{:S(2)}, u32[]{:S(2)}) %collective-permute-start.17) | collective-permute-done | bytes 327712 | tf_op jit(solution)/shard_map/ppermute | solution.py:462
  141.5 6.5 %more.6.state_ref = f32[136,2560]{1,0:T(8,128)S(1)} custom-call(s32[2]{0:T(128)S(1)} %pad_add_fusion.flag_ref, bf16[2560,128]{1,0:T(8,128)(2,1)S(1)} %get-tuple-element.21.q_ref, f32[136,2560]{1,0:T(8,128)S(1)} %more.5.state_ref, bf16[640,256]{1,0:T(8,128)(2,1)S(1)} %collective-permute-done.16.rest_0_.rest_7_, ...), custom_call_target="tpu_custom_call" | custom-call | flops 1677721600 | bytes 3145728 | tf_op jit(solution)/shard_map/more/pallas_call | solution.py:358
  148.1 4.0 %more.7 = (f32[136,1280]{1,0:T(8,128)S(1)}, f32[136,1280]{1,0:T(8,128)}) custom-call(s32[1]{0:T(128)} %bitcast.flag_ref, bf16[2560,128]{1,0:T(8,128)(2,1)S(1)} %get-tuple-element.21.q_ref, f32[136,2560]{1,0:T(8,128)S(1)} %more.6.state_ref, bf16[640,256]{1,0:T(8,128)(2,1)S(1)} %collective-permute-done.18.rest_0_.rest_8_), custom_call_target="tpu_custom_call" | custom-call | flops 838860800 | bytes 3145728 | tf_op jit(solution)/shard_map/more/pallas_call | solution.py:358
  152.1 1.2 collective-permute-start.19
  153.6 1.0 copy-done.10
  154.5 1.0 copy-done.12
  155.5 3.4 %pages.1 = (bf16[320,256]{1,0:T(8,128)(2,1)S(1)}, bf16[320,256]{1,0:T(8,128)(2,1)S(1)}) custom-call(s32[3]{0:T(128)S(1)} %pad_add_fusion.2.place_ref, s32[192]{0:T(256)S(1)} %reshape.146.code_ref, bf16[320,256]{1,0:T(8,128)(2,1)S(1)} %project.2.kv_ref.rest_0_, bf16[320,256]{1,0:T(8,128)(2,1)S(1)} %collective-permute-done.9.rest_0_.rest_1_, ...), custom_call_target="tpu_custom_call" | custom-call | tf_op jit(solution)/shard_map/pages/pallas_call | solution.py:436
  159.1 1.0 and_reduce_fusion
  160.4 0.9 broadcast_select_fusion
  161.3 1.0 finish.1
  (89 shorter events, 4.5 us)
Async XLA Ops:
  7.2 16.6 %copy-start.21 = (s32[40]{0:T(128)S(1)}, s32[40]{0:T(128)}, u32[]{:S(2)}) copy-start(s32[40]{0:T(128)} %param.18) | copy-start | bytes 484
  7.2 16.6 %copy-start.22 = (s32[40]{0:T(128)S(1)}, s32[40]{0:T(128)}, u32[]{:S(2)}) copy-start(s32[40]{0:T(128)} %param.17) | copy-start | bytes 484
  7.2 64.0 %all-gather.3.cloned.1.call-start = ((), (), s32[]{:S(2)}) async-start(), calls=%async_computation.1 | async-start | bytes 2949120 | tf_op jit(solution)/shard_map/all_gather | solution.py:508
  8.1 7.0 %collective-permute-start.2 = (bf16[160,256]{1,0:T(8,128)(2,1)S(1)}, bf16[160,256]{1,0:T(8,128)(2,1)S(1)}, u32[]{:S(2)}, u32[]{:S(2)}) collective-permute-start(bf16[160,256]{1,0:T(8,128)(2,1)S(1)} %slice.15), channel_id=1, source_target_pairs={{0,48},{8,56},{16,0},{24,8},{32,16},{40,24},{48,32},{56,40},{64,11... | collective-permute-start | bytes 245768 | tf_op jit(solution)/shard_map/ppermute | solution.py:466
  12.5 7.8 %collective-permute-start.1 = (bf16[160,256]{1,0:T(8,128)(2,1)S(1)}, bf16[160,256]{1,0:T(8,128)(2,1)S(1)}, u32[]{:S(2)}, u32[]{:S(2)}) collective-permute-start(bf16[160,256]{1,0:T(8,128)(2,1)S(1)} %slice.15), channel_id=1, source_target_pairs={{0,32},{8,40},{16,48},{24,56},{32,0},{40,8},{48,16},{56,24},{64,96... | collective-permute-start | bytes 245768 | tf_op jit(solution)/shard_map/ppermute | solution.py:466
  12.5 7.8 %collective-permute-start = (bf16[160,256]{1,0:T(8,128)(2,1)S(1)}, bf16[160,256]{1,0:T(8,128)(2,1)S(1)}, u32[]{:S(2)}, u32[]{:S(2)}) collective-permute-start(bf16[160,256]{1,0:T(8,128)(2,1)S(1)} %slice.15), channel_id=1, source_target_pairs={{0,16},{8,24},{16,32},{24,40},{32,48},{40,56},{48,0},{56,8},{64,80... | collective-permute-start | bytes 245768 | tf_op jit(solution)/shard_map/ppermute | solution.py:466
  12.8 1.0 copy-start.8
  13.9 0.8 copy-start.14
  14.6 6.4 %copy-start.15 = (bf16[160,768]{1,0:T(8,128)(2,1)S(1)}, bf16[160,768]{1,0:T(8,128)(2,1)}, u32[]{:S(2)}) copy-start(bf16[160,768]{1,0:T(8,128)(2,1)} %param.16) | copy-start | bytes 737284
  21.1 11.7 %collective-permute-start.5 = (bf16[160,512]{1,0:T(8,128)(2,1)S(1)}, bf16[160,512]{1,0:T(8,128)(2,1)S(1)}, u32[]{:S(2)}, u32[]{:S(2)}) collective-permute-start(bf16[160,512]{1,0:T(8,128)(2,1)S(1)} %slice.17), channel_id=1, source_target_pairs={{0,48},{8,56},{16,0},{24,8},{32,16},{40,24},{48,32},{56,40},{64,11... | collective-permute-start | bytes 491528 | tf_op jit(solution)/shard_map/ppermute | solution.py:466
  21.2 15.1 %collective-permute-start.4 = (bf16[160,512]{1,0:T(8,128)(2,1)S(1)}, bf16[160,512]{1,0:T(8,128)(2,1)S(1)}, u32[]{:S(2)}, u32[]{:S(2)}) collective-permute-start(bf16[160,512]{1,0:T(8,128)(2,1)S(1)} %slice.17), channel_id=1, source_target_pairs={{0,32},{8,40},{16,48},{24,56},{32,0},{40,8},{48,16},{56,24},{64,96... | collective-permute-start | bytes 491528 | tf_op jit(solution)/shard_map/ppermute | solution.py:466
  22.4 13.8 %collective-permute-start.3 = (bf16[160,512]{1,0:T(8,128)(2,1)S(1)}, bf16[160,512]{1,0:T(8,128)(2,1)S(1)}, u32[]{:S(2)}, u32[]{:S(2)}) collective-permute-start(bf16[160,512]{1,0:T(8,128)(2,1)S(1)} %slice.17), channel_id=1, source_target_pairs={{0,16},{8,24},{16,32},{24,40},{32,48},{40,56},{48,0},{56,8},{64,80... | collective-permute-start | bytes 491528 | tf_op jit(solution)/shard_map/ppermute | solution.py:466
  24.7 14.9 %all-to-all-start = ((f32[32,1,512]{2,1,0:T(1,128)}), f32[32,1,512]{2,1,0:T(1,128)}, u32[]{:S(2)}, u32[]{:S(2)}) async-start(f32[32,1,512]{2,1,0:T(1,128)} %all_to_all.8), calls=%async_computation | async-start | bytes 131072 | tf_op jit(solution)/shard_map/all_to_all | solution.py:584
  32.8 74.6 %all-gather.5.cloned.1.call-start = ((), (), s32[]{:S(2)}) async-start(), calls=%async_computation.2 | async-start | bytes 5898240 | tf_op jit(solution)/shard_map/all_gather | solution.py:508
  36.2 27.8 %copy-start.13 = (bf16[16,5120]{1,0:T(8,128)(2,1)S(1)}, bf16[16,5120]{1,0:T(8,128)(2,1)}, u32[]{:S(2)}) copy-start(bf16[16,5120]{1,0:T(8,128)(2,1)} %embed_ref.1) | copy-start | bytes 491524
  37.1 24.4 %copy-start.18 = (f32[16]{0:T(128)S(1)}, f32[16]{0:T(128)}, u32[]{:S(2)}) copy-start(f32[16]{0:T(128)} %param.12) | copy-start | bytes 196
  39.6 24.4 %copy-start.4 = (bf16[320,5120]{1,0:T(8,128)(2,1)S(1)}, bf16[320,5120]{1,0:T(8,128)(2,1)}, u32[]{:S(2)}) copy-start(bf16[320,5120]{1,0:T(8,128)(2,1)} %table_ref.1) | copy-start | bytes 9830404
  45.2 1.0 copy-start.6
  46.2 1.0 copy-start.7
  47.8 6.9 %collective-permute-start.6 = (f32[16,384]{1,0:T(8,128)S(1)}, f32[16,384]{1,0:T(8,128)}, u32[]{:S(2)}, u32[]{:S(2)}) collective-permute-start(f32[16,384]{1,0:T(8,128)S(1)} %place.1), channel_id=1, source_target_pairs={{0,1},{1,0},{2,3},{3,2},{4,5},{5,4},{6,7},{7,6},{8,9},{9,8},{10,11... | collective-permute-start | bytes 73736 | tf_op jit(solution)/shard_map/ppermute | solution.py:592
  55.5 2.7 %collective-permute-start.7 = (f32[16,384]{1,0:T(8,128)S(1)}, f32[16,384]{1,0:T(8,128)S(1)}, u32[]{:S(2)}, u32[]{:S(2)}) collective-permute-start(f32[16,384]{1,0:T(8,128)S(1)} %add.261), channel_id=1, source_target_pairs={{0,2},{1,3},{2,0},{3,1},{4,6},{5,7},{6,4},{7,5},{8,10},{9,11},{10,... | collective-permute-start | bytes 73736 | tf_op jit(solution)/shard_map/ppermute | solution.py:592
  58.7 4.5 %collective-permute-start.8 = (f32[16,384]{1,0:T(8,128)}, f32[16,384]{1,0:T(8,128)}, u32[]{:S(2)}, u32[]{:S(2)}) collective-permute-start(f32[16,384]{1,0:T(8,128)} %add.262), channel_id=1, source_target_pairs={{0,4},{1,5},{2,6},{3,7},{4,0},{5,1},{6,2},{7,3},{8,12},{9,13},{10,... | collective-permute-start | bytes 73736 | tf_op jit(solution)/shard_map/ppermute | solution.py:592
  68.8 2.4 %copy-start = (bf16[32,320,160]{2,1,0:T(8,128)(2,1)}, bf16[32,320,160]{2,1,0:T(8,128)(2,1)S(1)}, u32[]{:S(2)}) copy-start(bf16[32,320,160]{2,1,0:T(8,128)(2,1)S(1)} %hidden.1.normed_ref) | copy-start | bytes 9830404
  71.2 2.6 %copy-start.1 = (bf16[32,320,160]{2,1,0:T(8,128)(2,1)S(1)}, bf16[32,320,160]{2,1,0:T(8,128)(2,1)}, u32[]{:S(2)}) copy-start(bf16[32,320,160]{2,1,0:T(8,128)(2,1)} %copy-done) | copy-start | bytes 9830404
  73.8 1.8 %copy-start.5 = (bf16[5120,256]{1,0:T(8,128)(2,1)S(1)}, bf16[5120,256]{1,0:T(8,128)(2,1)}, u32[]{:S(2)}) copy-start(bf16[5120,256]{1,0:T(8,128)(2,1)} %all-gather.3.cloned.1.call-done.weight_ref) | copy-start | bytes 7864324
  75.6 8.1 %copy-start.16 = (pred[40,40]{1,0:T(8,128)(4,1)S(1)}, pred[40,40]{1,0:T(8,128)(4,1)}, u32[]{:S(2)}) copy-start(pred[40,40]{1,0:T(8,128)(4,1)} %iota_compare_fusion) | copy-start | bytes 4804
  75.6 16.8 %copy-start.17 = (s32[40]{0:T(128)S(1)}, s32[40]{0:T(128)}, u32[]{:S(2)}) copy-start(s32[40]{0:T(128)} %iota_multiply_fusion) | copy-start | bytes 484
  83.2 6.2 %collective-permute-start.9 = (bf16[320,256]{1,0:T(8,128)(2,1)S(1)}, bf16[320,256]{1,0:T(8,128)(2,1)S(1)}, u32[]{:S(2)}, u32[]{:S(2)}) collective-permute-start(bf16[320,256]{1,0:T(8,128)(2,1)S(1)} %project.2.kv_ref.rest_0_), channel_id=1, source_target_pairs={{0,16},{8,24},{16,32},{24,40},{32,48},{40,56},{48,0},{56,8},{64,80... | collective-permute-start | bytes 491528 | tf_op jit(solution)/shard_map/ppermute | solution.py:466
  89.4 10.0 %collective-permute-start.10 = (bf16[640,256]{1,0:T(8,128)(2,1)S(1)}, bf16[640,256]{1,0:T(8,128)(2,1)S(1)}, u32[]{:S(2)}, u32[]{:S(2)}) collective-permute-start(bf16[640,256]{1,0:T(8,128)(2,1)S(1)} %pad_maximum_fusion.2), channel_id=1, source_target_pairs={{0,64},{8,72},{16,80},{24,88},{32,96},{40,104},{48,112},{56,120},{... | collective-permute-start | bytes 983048 | tf_op jit(solution)/shard_map/ppermute | solution.py:462
  91.7 7.7 %collective-permute-start.11 = (bf16[640,256]{1,0:T(8,128)(2,1)S(1)}, bf16[640,256]{1,0:T(8,128)(2,1)S(1)}, u32[]{:S(2)}, u32[]{:S(2)}) collective-permute-start(bf16[640,256]{1,0:T(8,128)(2,1)S(1)} %pad_maximum_fusion.2), channel_id=1, source_target_pairs={{0,128},{8,136},{16,144},{24,152},{32,160},{40,168},{48,176},{56,1... | collective-permute-start | bytes 983048 | tf_op jit(solution)/shard_map/ppermute | solution.py:462
  91.8 15.6 %collective-permute-start.12 = (bf16[640,256]{1,0:T(8,128)(2,1)S(1)}, bf16[640,256]{1,0:T(8,128)(2,1)S(1)}, u32[]{:S(2)}, u32[]{:S(2)}) collective-permute-start(bf16[640,256]{1,0:T(8,128)(2,1)S(1)} %pad_maximum_fusion.2), channel_id=1, source_target_pairs={{0,192},{8,200},{16,208},{24,216},{32,224},{40,232},{48,240},{56,2... | collective-permute-start | bytes 983048 | tf_op jit(solution)/shard_map/ppermute | solution.py:462
  92.7 31.0 %collective-permute-start.14 = (bf16[320,256]{1,0:T(8,128)(2,1)S(1)}, bf16[320,256]{1,0:T(8,128)(2,1)S(1)}, u32[]{:S(2)}, u32[]{:S(2)}) collective-permute-start(bf16[320,256]{1,0:T(8,128)(2,1)S(1)} %project.2.kv_ref.rest_0_), channel_id=1, source_target_pairs={{0,32},{8,40},{16,48},{24,56},{32,0},{40,8},{48,16},{56,24},{64,96... | collective-permute-start | bytes 491528 | tf_op jit(solution)/shard_map/ppermute | solution.py:466
  92.8 30.9 %collective-permute-start.15 = (bf16[320,256]{1,0:T(8,128)(2,1)S(1)}, bf16[320,256]{1,0:T(8,128)(2,1)S(1)}, u32[]{:S(2)}, u32[]{:S(2)}) collective-permute-start(bf16[320,256]{1,0:T(8,128)(2,1)S(1)} %project.2.kv_ref.rest_0_), channel_id=1, source_target_pairs={{0,48},{8,56},{16,0},{24,8},{32,16},{40,24},{48,32},{56,40},{64,11... | collective-permute-start | bytes 491528 | tf_op jit(solution)/shard_map/ppermute | solution.py:466
  107.4 2.5 %copy-start.2 = (bf16[32,320,160]{2,1,0:T(8,128)(2,1)S(1)}, bf16[32,320,160]{2,1,0:T(8,128)(2,1)}, u32[]{:S(2)}) copy-start(bf16[32,320,160]{2,1,0:T(8,128)(2,1)} %copy-done) | copy-start | bytes 9830404
  109.9 2.5 %copy-start.3 = (bf16[5120,512]{1,0:T(8,128)(2,1)S(1)}, bf16[5120,512]{1,0:T(8,128)(2,1)}, u32[]{:S(2)}) copy-start(bf16[5120,512]{1,0:T(8,128)(2,1)} %all-gather.5.cloned.1.call-done.weight_ref) | copy-start | bytes 15728644
  120.8 4.8 %collective-permute-start.13 = (bf16[320,512]{1,0:T(8,128)(2,1)S(1)}, bf16[320,512]{1,0:T(8,128)(2,1)S(1)}, u32[]{:S(2)}, u32[]{:S(2)}) collective-permute-start(bf16[320,512]{1,0:T(8,128)(2,1)S(1)} %project.3.own_ref), channel_id=1, source_target_pairs={{0,8},{8,0},{16,24},{24,16},{32,40},{40,32},{48,56},{56,48},{64,72... | collective-permute-start | bytes 983048 | tf_op jit(solution)/shard_map/ppermute | solution.py:470
  123.7 14.7 %collective-permute-start.16 = (bf16[640,256]{1,0:T(8,128)(2,1)S(1)}, bf16[640,256]{1,0:T(8,128)(2,1)S(1)}, u32[]{:S(2)}, u32[]{:S(2)}) collective-permute-start(bf16[640,256]{1,0:T(8,128)(2,1)S(1)} %constant_dynamic-update-slice_fusion), channel_id=1, source_target_pairs={{0,64},{8,72},{16,80},{24,88},{32,96},{40,104},{48,112},{56,120},{... | collective-permute-start | bytes 983048 | tf_op jit(solution)/shard_map/ppermute | solution.py:462
  124.3 17.2 %collective-permute-start.17 = (bf16[640,256]{1,0:T(8,128)(2,1)S(1)}, bf16[640,256]{1,0:T(8,128)(2,1)S(1)}, u32[]{:S(2)}, u32[]{:S(2)}) collective-permute-start(bf16[640,256]{1,0:T(8,128)(2,1)S(1)} %constant_dynamic-update-slice_fusion), channel_id=1, source_target_pairs={{0,192},{8,200},{16,208},{24,216},{32,224},{40,232},{48,240},{56,2... | collective-permute-start | bytes 983048 | tf_op jit(solution)/shard_map/ppermute | solution.py:462
  125.3 22.8 %collective-permute-start.18 = (bf16[640,256]{1,0:T(8,128)(2,1)S(1)}, bf16[640,256]{1,0:T(8,128)(2,1)S(1)}, u32[]{:S(2)}, u32[]{:S(2)}) collective-permute-start(bf16[640,256]{1,0:T(8,128)(2,1)S(1)} %constant_dynamic-update-slice_fusion), channel_id=1, source_target_pairs={{0,128},{8,136},{16,144},{24,152},{32,160},{40,168},{48,176},{56,1... | collective-permute-start | bytes 983048 | tf_op jit(solution)/shard_map/ppermute | solution.py:462
  141.5 6.5 %copy-start.9 = (bf16[640,256]{1,0:T(8,128)(2,1)}, bf16[640,256]{1,0:T(8,128)(2,1)S(1)}, u32[]{:S(2)}) copy-start(bf16[640,256]{1,0:T(8,128)(2,1)S(1)} %collective-permute-done.17.rest_1_.rest_9_) | copy-start | bytes 983044
  148.1 4.0 %copy-start.11 = (bf16[640,256]{1,0:T(8,128)(2,1)}, bf16[640,256]{1,0:T(8,128)(2,1)S(1)}, u32[]{:S(2)}) copy-start(bf16[640,256]{1,0:T(8,128)(2,1)S(1)} %collective-permute-done.18.rest_0_.rest_8_) | copy-start | bytes 983044
  152.1 7.0 %copy-start.19 = (s32[40]{0:T(128)S(1)}, s32[40]{0:T(128)}, u32[]{:S(2)}) copy-start(s32[40]{0:T(128)} %iota_add_fusion) | copy-start | bytes 484
  152.1 7.0 %copy-start.20 = (pred[32]{0:T(512)(128)(4,1)S(1)}, pred[32]{0:T(512)(128)(4,1)}, u32[]{:S(2)}) copy-start(pred[32]{0:T(512)(128)(4,1)} %fusion.1) | copy-start | bytes 100
  152.1 9.2 %collective-permute-start.19 = (f32[136,1280]{1,0:T(8,128)}, f32[136,1280]{1,0:T(8,128)S(1)}, u32[]{:S(2)}, u32[]{:S(2)}) collective-permute-start(f32[136,1280]{1,0:T(8,128)} %get-tuple-element.27), channel_id=1, source_target_pairs={{0,8},{8,0},{16,24},{24,16},{32,40},{40,32},{48,56},{56,48},{64,72... | collective-permute-start | bytes 2088968 | tf_op jit(solution)/shard_map/ppermute | solution.py:470
  153.5 1.0 copy-start.10
  154.5 1.0 copy-start.12
  158.9 1.5 collective-permute-start.20
Sparse Core Ops, SparseCore 0:
  21.2 29.1 all-gather.2
  52.2 38.8 all-gather.4

commit v5 on v4

--- a/solution.py
+++ b/solution.py
@@ -25,7 +25,6 @@
 QROWS = GROUP * BLK
 STATE = HD + 8
 RBLK = 160
-PIECES = 4
 VMEM = 24 * 1024 * 1024
 
 
@@ -90,9 +89,9 @@
     return high, middle, low
 
 
-def place_kernel(parts_ref, token_ref, out_ref):
+def place_kernel(offset_ref, parts_ref, token_ref, out_ref):
     count = parts_ref.shape[0]
-    token = lax.broadcasted_iota(jnp.int32, (count, TOK), 1)
+    token = lax.broadcasted_iota(jnp.int32, (count, TOK), 1) - offset_ref[0] * BLK
     pick = jnp.where(token == token_ref[...], 1.0, 0.0).astype(jnp.bfloat16)
     total = jnp.zeros((LAT, TOK), jnp.float32)
     for part in reversed(split_three(parts_ref[...])):
@@ -103,28 +102,23 @@
 
 
 def place_table():
-    table = np.full((3, SEQ, ROWS + 2, COLS + 2), -1, np.int32)
-    for case in range(3):
-        for source in range(SEQ):
-            for row in range(ROWS + 2):
-                for col in range(COLS + 2):
-                    height = row - 1 + ROWS * (case - 1)
-                    width = source * COLS - 1 + col
-                    if 0 <= height < ROWS and 0 <= width < SEQ * COLS:
-                        table[case, source, row, col] = height * SEQ * COLS + width
-    return table.reshape(3, SEQ * EXT, 1)
+    row = np.arange(ROWS + 2).reshape(1, -1, 1) - 1
+    col = np.arange(COLS + 2).reshape(1, 1, -1) - 1
+    width = np.arange(SEQ).reshape(-1, 1, 1) * COLS + col
+    inside = (width >= 0) & (width < SEQ * COLS)
+    token = np.where(inside, row * SEQ * COLS + width, -(1 << 20))
+    return token.astype(np.int32).reshape(SEQ * EXT, 1)
 
 
 def place_latents(parts, offset):
-    table = jnp.asarray(place_table())
-    token = lax.dynamic_index_in_dim(table, jnp.clip(offset + 1, 0, 2), 0, keepdims=False)
-    token = jnp.where(jnp.abs(offset) <= 1, token, -1)
     return pl.pallas_call(
         place_kernel,
+        in_specs=[pl.BlockSpec(memory_space=pltpu.SMEM)]
+        + [pl.BlockSpec(memory_space=pltpu.VMEM)] * 2,
         out_shape=jax.ShapeDtypeStruct((LAT, TOK), jnp.float32),
         compiler_params=params(),
         name="place",
-    )(parts, token)
+    )(offset.reshape(1), parts, jnp.asarray(place_table()))
 
 
 def hidden_kernel(latent_ref, bias_ref, embed_ref, table_ref, gain_ref, out_ref, hid_ref, sq_ref):
@@ -163,7 +157,10 @@
             normed = hid_ref[tile] * factor * gain
             for part in range(width // RBLK):
                 piece = normed[:, part * RBLK : (part + 1) * RBLK]
-                out_ref[tile * (width // RBLK) + part] = piece.astype(jnp.bfloat16)
+                block = tile * (width // RBLK) + part
+                y, z, core = block // 8, block // 2 % 4, block % 2
+                start = ((y * 2 + core) * 4 + z) * RBLK
+                out_ref[:, start : start + RBLK] = piece.astype(jnp.bfloat16)
 
 
 def normed_hidden(latent, conv_bias, embed_weight, position_table, norm_gain):
@@ -180,8 +177,8 @@
             pl.BlockSpec((BLK, width), lambda i: (0, i)),
             pl.BlockSpec((1, depth), lambda i: (0, 0)),
         ],
-        out_specs=pl.BlockSpec((depth // RBLK, BLK, RBLK), lambda i: (0, 0, 0)),
-        out_shape=jax.ShapeDtypeStruct((depth // RBLK, BLK, RBLK), jnp.bfloat16),
+        out_specs=pl.BlockSpec((BLK, depth), lambda i: (0, 0)),
+        out_shape=jax.ShapeDtypeStruct((BLK, depth), jnp.bfloat16),
         scratch_shapes=[
             pltpu.VMEM((steps, BLK, width), jnp.float32),
             pltpu.VMEM((BLK, 128), jnp.float32),
@@ -189,54 +186,6 @@
         compiler_params=params(dimension_semantics=("arbitrary",)),
         name="hidden",
     )(latent, conv_bias.reshape(LAT, 1), embed_weight, position_table, norm_gain.reshape(1, depth))
-
-
-def project_kernel(index_ref, normed_ref, weight_ref, out_ref, held_ref, sum_ref, sems):
-    rows = weight_ref.shape[0] // PIECES
-    copies = []
-    for piece in range(PIECES):
-        cut = pl.ds(piece * rows, rows)
-        copies.append(
-            pltpu.make_async_copy(weight_ref.at[cut, :], held_ref.at[cut, :], sems.at[piece])
-        )
-        copies[-1].start()
-    sum_ref[...] = jnp.zeros_like(sum_ref)
-    for piece in range(PIECES):
-        copies[piece].wait()
-
-        def body(step, carry, first=piece * rows // RBLK):
-            block = first + step
-            weight = held_ref[pl.ds(pl.multiple_of(block * RBLK, RBLK), RBLK), :]
-            sum_ref[...] += jnp.dot(
-                normed_ref[index_ref[block]], weight, preferred_element_type=jnp.float32
-            )
-            return carry
-
-        lax.fori_loop(0, rows // RBLK, body, 0)
-    out_ref[...] = sum_ref[...].astype(jnp.bfloat16)
-
-
-def project(index, normed, weight):
-    depth, width = weight.shape
-    return pl.pallas_call(
-        project_kernel,
-        in_specs=[
-            pl.BlockSpec(memory_space=pltpu.SMEM),
-            pl.BlockSpec(memory_space=pltpu.VMEM),
-            pl.BlockSpec(memory_space=pl.ANY),
-        ],
-        out_shape=jax.ShapeDtypeStruct((BLK, width), jnp.bfloat16),
-        scratch_shapes=[
-            pltpu.VMEM((depth, width), jnp.bfloat16),
-            pltpu.VMEM((BLK, width), jnp.float32),
-            pltpu.SemaphoreType.DMA((PIECES,)),
-        ],
-        compiler_params=params(),
-        cost_estimate=pl.CostEstimate(
-            flops=2 * BLK * depth * width, bytes_accessed=2 * depth * width, transcendentals=0
-        ),
-        name="project",
-    )(index, normed, weight)
 
 
 def attend_block(masked, partner_full, keys, values, q_ref, state_ref):
@@ -413,7 +362,7 @@
             if by_y == 0:
                 array, base = arrays[by_z], 0
             else:
-                array, base = arrays[3 + by_y + by_z // 2 * 3], by_z % 2 * BLK
+                array, base = arrays[3 + by_y + by_z // 3 * 3], by_z % 3 * BLK
             source = (((y - by_y) & 3) * 4 + ((z - by_z) & 3)) * 2 + core
             for entry in range(2 * MOST):
                 code = code_ref[source * 2 * MOST + entry]
@@ -508,26 +457,25 @@
     return lax.all_gather(stacked, "seq", axis=0, tiled=True, axis_index_groups=groups)
 
 
-def stack_z(value):
-    parts = [value] + [along_z(value, count) for count in (1, 2, 3)]
-    return jnp.concatenate(parts, axis=0)
-
-
-def row_order(me):
+def stack_z(value, me):
     z = (me // 2) % 4
-    order = [(y * 4 + ((z - k) & 3)) * 2 + c for y in range(4) for c in range(2) for k in range(4)]
-    return jnp.stack(order)
+    by_z = [value] + [along_z(value, count) for count in (1, 2, 3)]
+    orders = [jnp.concatenate([by_z[(own - i) % 4] for i in range(4)], axis=0) for own in range(4)]
+    low = jnp.where(z == 0, orders[0], orders[1])
+    high = jnp.where(z == 2, orders[2], orders[3])
+    return jnp.where(z < 2, low, high)
+
+
+def project(normed, weight):
+    return jnp.dot(normed, weight, preferred_element_type=jnp.float32).astype(jnp.bfloat16)
 
 
 def attention_and_pages(me, targets, normed, kv_weight, query_weight):
     core, z, y = me % 2, (me // 2) % 4, me // 8
-    order = row_order(me)
-    kv = project(order, normed, kv_weight)
-    by_z, (near, far) = spread(kv, ((0, 1), (2, 3)))
-    order, near[1], near[2], near[3] = lax.optimization_barrier(
-        (order, near[1], near[2], near[3])
-    )
-    own_queries = project(order, normed, query_weight)
+    kv = project(normed, kv_weight)
+    by_z, (near, far) = spread(kv, ((0, 1, 2), (3,)))
+    normed, unused = lax.optimization_barrier((normed, near[1]))
+    own_queries = project(normed, query_weight)
     pair_queries = other_core(own_queries)
 
     def flag(*conditions):
@@ -540,8 +488,9 @@
     state = attend_more(
         flag(y >= 1, y >= 3, y >= 2), queries, state, [near[1], near[3], near[2]]
     )
-    state = attend_more(flag(y >= 1, y >= 3), queries, state, [far[1], far[3]])
-    own, sent = attend_more(flag(y >= 2), queries, state, [far[2]], split=True)
+    own, sent = attend_more(
+        flag(y >= 1, y >= 3, y >= 2), queries, state, [far[1], far[3], far[2]], split=True
+    )
     got = other_core(sent)
 
     arrays = [by_z[count] for count in range(4)]
@@ -570,8 +519,8 @@
     me = lax.axis_index("seq").astype(jnp.int32)
     tensor = lax.axis_index("tensor").astype(jnp.int32)
     tensor_count = lax.axis_size("tensor")
-    kv_weight = stack_z(qkv_weight[:, GROUP * HD :])
-    query_weight = stack_z(qkv_weight[:, : GROUP * HD])
+    kv_weight = stack_z(qkv_weight[:, GROUP * HD :], me)
+    query_weight = stack_z(qkv_weight[:, : GROUP * HD], me)
     parts = partial_latents(features, conv_weight)
     parts, kv_weight = lax.optimization_barrier((parts, kv_weight))
     kv_weight = gather_rows(kv_weight)
@@ -582,14 +531,15 @@
     message = jnp.pad(message, ((0, 0), (0, 512 - message.shape[1])))
     message = jnp.broadcast_to(message[:, None], (FRAMES, SEQ // FRAMES, 512)).reshape(SEQ, 512)
     message = lax.all_to_all(message, "seq", split_axis=0, concat_axis=0, tiled=True)
-    message, query_weight = lax.optimization_barrier((message, query_weight))
-    query_weight = gather_rows(query_weight)
     targets = message[:, EXT * LAT : EXT * LAT + PAGES].astype(jnp.int32)
     offset = tensor - me % (SEQ // FRAMES)
     latent = place_latents(message[:, : EXT * LAT].reshape(SEQ * EXT, LAT), offset)
     for bit in (1, 2, 4):
         swap = [(i, i ^ bit) for i in range(tensor_count)]
         latent = latent + lax.ppermute(latent, "tensor", swap)
+        if bit == 1:
+            latent, query_weight = lax.optimization_barrier((latent, query_weight))
+    query_weight = gather_rows(query_weight)
     normed = normed_hidden(latent, conv_bias, embed_weight, position_table, norm_gain)
     return attention_and_pages(me, targets, normed, kv_weight, query_weight)
 

time: 170 us -> 172 us (1.012); the launches traced: 169 us -> 169 us
  Pallas kernels: 49.6 us -> 34.5 us
  starting transfers between devices: 35.5 us -> 48.9 us
  local copies, waits for them, and re-layouts: 23.4 us -> 11.6 us
  matrix products: 0 us -> 8.31 us
  waiting for transfers between devices: 35.6 us -> 38.8 us
    pallas_call x3 -> x1, Pallas kernels: 16.6 us -> 0.57 us  [place_latents(): pl.pallas_call(place_kernel, in_specs=[pl.BlockSpec(memory_space=pltpu.SM...]
    unnamed x48 -> x37, local copies, waits for them, and re-layouts: 18.6 us -> 6.57 us
    ppermute x3, starting transfers between devices: 4.22 us -> 13.2 us  [other_core(): return lax.ppermute(value, 'seq', moves(lambda y, z, c: (y, z, 1 - c)))]
    ppermute x6, waiting for transfers between devices: 16.7 us -> 7.82 us  [along_y(): lax.ppermute(value, 'seq', moves(lambda y, z, c: ((y + count) % 4, z, c)))]
    dot_general x0 -> x2, matrix products: none -> 8.31 us  [project(): jnp.dot(normed, weight, preferred_element_type=jnp.float32)]
    ppermute x9, waiting for transfers between devices: 13.1 us -> 21.3 us  [along_z(): lax.ppermute(value, 'seq', moves(lambda y, z, c: (y, (z + count) % 4, c)))]
    all_to_all x1, waiting for transfers between devices: 2.46 us -> 8.38 us  [on_device(): lax.all_to_all(message, 'seq', split_axis=0, concat_axis=0, tiled=True)]
    ppermute x6, starting transfers between devices: 4.86 us -> 7.96 us  [along_y(): lax.ppermute(value, 'seq', moves(lambda y, z, c: ((y + count) % 4, z, c)))]
  transfers between devices with their start and end apart: 24 -> 24, of which waited for: 11 -> 8; matrix products, arithmetic and copies ran while one was open for 8% -> 14% of each run, Pallas kernels for 26% -> 16%
where the time goes in v5:
time: 172 us; the launch traced here: 169 us
  starting transfers between devices  48.9 us (28%)
  waiting for transfers between devices  38.8 us (23%)
  Pallas kernels  34.5 us (20%)
  between operations  14.4 us (8%)
  other arithmetic  12 us (7%)
  local copies, waits for them, and re-layouts  11.6 us (7%)
  matrix products  8.31 us (5%)
    pallas_call x3, Pallas kernels, attend_more(): pl.pallas_call(functools.partial(more_kernel, count, split), in_specs=[pl...  21.8 us
    ppermute x9, waiting for transfers between devices, along_z(): lax.ppermute(value, 'seq', moves(lambda y, z, c: (y, (z + count) % 4, c)))  21.3 us
    ppermute x3, starting transfers between devices, other_core(): return lax.ppermute(value, 'seq', moves(lambda y, z, c: (y, z, 1 - c)))  13.2 us
    ppermute x9, starting transfers between devices, along_z(): lax.ppermute(value, 'seq', moves(lambda y, z, c: (y, (z + count) % 4, c)))  11.1 us
    ppermute x3, starting transfers between devices, on_device(): latent = latent + lax.ppermute(latent, 'tensor', swap)  9.54 us
    all_to_all x1, waiting for transfers between devices, on_device(): lax.all_to_all(message, 'seq', split_axis=0, concat_axis=0, tiled=True)  8.38 us
    dot_general x2, matrix products, project(): jnp.dot(normed, weight, preferred_element_type=jnp.float32)  8.31 us
    ppermute x6, starting transfers between devices, along_y(): lax.ppermute(value, 'seq', moves(lambda y, z, c: ((y + count) % 4, z, c)))  7.96 us
  transfers between devices with their start and end apart: 24, of which 8 were waited for; matrix products, arithmetic and copies ran while one was open for 14% of the time, Pallas kernels for 16%

profile of v5, /device:TPU:25, one launch (start us, length us, event | category | flops | bytes accessed | tf_op | source)
XLA Modules:
  0.0 168.5 jit_solution(14941222925846734849)
XLA Ops:
  7.2 0.9 slice.15
  8.1 1.6 collective-permute-start.2
  9.8 3.0 %collective-permute-start.1 = (bf16[160,256]{1,0:T(8,128)(2,1)S(1)}, bf16[160,256]{1,0:T(8,128)(2,1)S(1)}, u32[]{:S(2)}, u32[]{:S(2)}) collective-permute-start(bf16[160,256]{1,0:T(8,128)(2,1)S(1)} %slice.15), channel_id=1, source_target_pairs={{0,32},{8,40},{16,48},{24,56},{32,0},{40,8},{48,16},{56,24},{64,96... | collective-permute-start | bytes 245768 | tf_op jit(solution)/shard_map/ppermute | solution.py:415
  12.8 0.7 collective-permute-start
  13.5 1.0 copy-done.9
  14.5 0.8 copy-done.11
  15.3 0.5 conv.1
  15.8 3.1 %collective-permute-done.1 = bf16[160,256]{1,0:T(8,128)(2,1)S(1)} collective-permute-done((bf16[160,256]{1,0:T(8,128)(2,1)S(1)}, bf16[160,256]{1,0:T(8,128)(2,1)S(1)}, u32[]{:S(2)}, u32[]{:S(2)}) %collective-permute-start.1) | collective-permute-done | bytes 81952 | tf_op jit(solution)/shard_map/ppermute | solution.py:415
  18.9 0.9 fusion.1
  19.8 0.7 slice.18
  20.5 2.0 %collective-permute-start.6 = (bf16[160,512]{1,0:T(8,128)(2,1)}, bf16[160,512]{1,0:T(8,128)(2,1)}, u32[]{:S(2)}, u32[]{:S(2)}) collective-permute-start(bf16[160,512]{1,0:T(8,128)(2,1)} %slice.18), channel_id=1, source_target_pairs={{0,16},{8,24},{16,32},{24,40},{32,48},{40,56},{48,0},{56,8},{64,80... | collective-permute-start | bytes 491528 | tf_op jit(solution)/shard_map/ppermute | solution.py:415
  22.5 0.8 collective-permute-start.5
  23.3 1.3 collective-permute-start.4
  24.8 0.7 all_to_all.8
  25.5 7.0 %all-to-all-start = ((f32[32,1,512]{2,1,0:T(1,128)}), f32[32,1,512]{2,1,0:T(1,128)S(1)}, u32[]{:S(2)}, u32[]{:S(2)}) async-start(f32[32,1,512]{2,1,0:T(1,128)} %all_to_all.8), calls=%async_computation | async-start | bytes 131072 | tf_op jit(solution)/shard_map/all_to_all | solution.py:533
  32.6 8.4 %all-to-all-done = f32[32,1,512]{2,1,0:T(1,128)S(1)} async-done(((f32[32,1,512]{2,1,0:T(1,128)}), f32[32,1,512]{2,1,0:T(1,128)S(1)}, u32[]{:S(2)}, u32[]{:S(2)}) %all-to-all-start) | async-done | bytes 65568 | tf_op jit(solution)/shard_map/all_to_all | solution.py:533
  41.0 0.9 reshape.132.parts_ref
  42.0 1.3 copy-done.3
  43.3 1.0 copy-done.8
  44.3 0.6 place.1
  44.9 5.6 %collective-permute-start.3 = (f32[16,384]{1,0:T(8,128)S(1)}, f32[16,384]{1,0:T(8,128)}, u32[]{:S(2)}, u32[]{:S(2)}) collective-permute-start(f32[16,384]{1,0:T(8,128)S(1)} %place.1), channel_id=1, source_target_pairs={{0,1},{1,0},{2,3},{3,2},{4,5},{5,4},{6,7},{7,6},{8,9},{9,8},{10,11... | collective-permute-start | bytes 73736 | tf_op jit(solution)/shard_map/ppermute | solution.py:539
  50.5 2.7 %fusion = bf16[640,512]{1,0:T(8,128)(2,1)} fusion(bf16[160,512]{1,0:T(8,128)(2,1)} %collective-permute-done.6, bf16[160,512]{1,0:T(8,128)(2,1)} %collective-permute-done.5, bf16[160,512]{1,0:T(8,128)(2,1)} %collective-permute-done.4, bf16[160,512]{1,0:T(8,128)(2,1)} %slice.18, pred[]{:T(512)S(6)} %eq.59, pred[]{:T(512)S(6)} %eq.58, pred[]{:T(512)S(6)} %lt.69), kind=kLoop, calls=%fused_computation.3 | loop fusion | flops 11468800 | bytes 1310723 | tf_op jit(solution)/shard_map/jit(_where)/select_n | solution.py:466
  53.2 0.7 add.129
  54.0 0.5 iota_multiply_fusion
  54.5 0.5 iota_add_fusion
  55.1 1.2 collective-permute-start.7
  56.3 0.6 fusion.2
  56.9 0.9 collective-permute-done.7
  57.7 0.6 add.130
  58.3 2.7 %collective-permute-start.8 = (f32[16,384]{1,0:T(8,128)}, f32[16,384]{1,0:T(8,128)S(1)}, u32[]{:S(2)}, u32[]{:S(2)}) collective-permute-start(f32[16,384]{1,0:T(8,128)} %add.130), channel_id=1, source_target_pairs={{0,4},{1,5},{2,6},{3,7},{4,0},{5,1},{6,2},{7,3},{8,12},{9,13},{10,... | collective-permute-start | bytes 73736 | tf_op jit(solution)/shard_map/ppermute | solution.py:539
  61.2 0.7 copy.23.bias_ref
  61.9 0.7 reshape.134.gain_ref
  62.6 0.1 collective-permute-done.8
  62.7 0.7 add.131.latent_ref
  63.5 4.9 %hidden.1 = bf16[320,5120]{1,0:T(8,128)(2,1)S(1)} custom-call(f32[16,384]{1,0:T(8,128)S(1)} %add.131.latent_ref, f32[16,1]{1,0:T(8,128)S(1)} %copy.23.bias_ref, bf16[16,5120]{1,0:T(8,128)(2,1)S(1)} %copy-done.10, bf16[320,5120]{1,0:T(8,128)(2,1)S(1)} %copy-done, bf16[1,5120]{1,0:T(2,128)(2,1)S(1)} %reshape.134.gain_ref), custom_call_target="tpu_custom_call" | custom-call | tf_op jit(solution)/shard_map/hidden/pallas_call | solution.py:170
  68.4 1.7 %copy-done.1 = bf16[320,5120]{1,0:T(8,128)(2,1)} copy-done((bf16[320,5120]{1,0:T(8,128)(2,1)}, bf16[320,5120]{1,0:T(8,128)(2,1)S(1)}, u32[]{:S(2)}) %copy-start.1) | copy-done | bytes 3276824
  70.1 4.0 %convolution_convert_fusion.1.kv_ref.rest_0_ = bf16[320,256]{1,0:T(8,128)(2,1)S(1)} fusion(bf16[320,5120]{1,0:T(8,128)(2,1)} %copy-done.1, bf16[5120,256]{1,0:T(8,128)(2,1)} %all-gather.3.cloned.1.call-done), kind=kOutput, calls=%fused_computation.1 | convolution fusion | flops 838942720 | bytes 6062080 | tf_op jit(solution)/shard_map/dot_general | solution.py:470
  74.1 0.2 collective-permute-start.10
  74.4 1.4 collective-permute-start.9
  75.8 12.5 %collective-permute-done.10.rest_1_.rest_2_ = bf16[320,256]{1,0:T(8,128)(2,1)S(1)} collective-permute-done((bf16[320,256]{1,0:T(8,128)(2,1)S(1)}, bf16[320,256]{1,0:T(8,128)(2,1)S(1)}, u32[]{:S(2)}, u32[]{:S(2)}) %collective-permute-start.10) | collective-permute-done | bytes 163872 | tf_op jit(solution)/shard_map/ppermute | solution.py:415
  88.3 0.9 pad_maximum_fusion
  89.2 0.7 copy-done.4
  89.9 2.0 %collective-permute-start.11 = (bf16[960,256]{1,0:T(8,128)(2,1)}, bf16[960,256]{1,0:T(8,128)(2,1)}, u32[]{:S(2)}, u32[]{:S(2)}) collective-permute-start(bf16[960,256]{1,0:T(8,128)(2,1)} %pad_maximum_fusion), channel_id=1, source_target_pairs={{0,64},{8,72},{16,80},{24,88},{32,96},{40,104},{48,112},{56,120},{... | collective-permute-start | bytes 1474568 | tf_op jit(solution)/shard_map/ppermute | solution.py:411
  92.0 1.2 convert_reduce_fusion
  93.2 0.3 select_reduce_fusion
  93.5 1.3 collective-permute-start.15
  94.9 7.8 %collective-permute-done.11.rest_0_.rest_4_ = bf16[960,256]{1,0:T(8,128)(2,1)} collective-permute-done((bf16[960,256]{1,0:T(8,128)(2,1)}, bf16[960,256]{1,0:T(8,128)(2,1)}, u32[]{:S(2)}, u32[]{:S(2)}) %collective-permute-start.11) | collective-permute-done | bytes 491552 | tf_op jit(solution)/shard_map/ppermute | solution.py:411
  102.7 4.3 %convolution_convert_fusion.own_ref = bf16[320,512]{1,0:T(8,128)(2,1)S(1)} fusion(bf16[320,5120]{1,0:T(8,128)(2,1)S(1)} %copy-done.2, bf16[5120,512]{1,0:T(8,128)(2,1)} %all-gather.5.cloned.1.call-done), kind=kOutput, calls=%fused_computation | convolution fusion | flops 1677885440 | bytes 8847360 | tf_op jit(solution)/shard_map/dot_general | solution.py:470
  107.0 11.6 %collective-permute-start.12 = (bf16[320,512]{1,0:T(8,128)(2,1)S(1)}, bf16[320,512]{1,0:T(8,128)(2,1)S(1)}, u32[]{:S(2)}, u32[]{:S(2)}) collective-permute-start(bf16[320,512]{1,0:T(8,128)(2,1)S(1)} %convolution_convert_fusion.own_ref), channel_id=1, source_target_pairs={{0,8},{8,0},{16,24},{24,16},{32,40},{40,32},{48,56},{56,48},{64,72... | collective-permute-start | bytes 983048 | tf_op jit(solution)/shard_map/ppermute | solution.py:419
  118.6 5.8 %collective-permute-done.13.rest_2_.rest_3_ = bf16[320,256]{1,0:T(8,128)(2,1)S(1)} collective-permute-done((bf16[320,256]{1,0:T(8,128)(2,1)S(1)}, bf16[320,256]{1,0:T(8,128)(2,1)S(1)}, u32[]{:S(2)}, u32[]{:S(2)}) %collective-permute-start.13) | collective-permute-done | bytes 163872 | tf_op jit(solution)/shard_map/ppermute | solution.py:415
  124.4 3.4 %collective-permute-start.16 = (bf16[320,256]{1,0:T(8,128)(2,1)S(1)}, bf16[320,256]{1,0:T(8,128)(2,1)S(1)}, u32[]{:S(2)}, u32[]{:S(2)}) collective-permute-start(bf16[320,256]{1,0:T(8,128)(2,1)S(1)} %collective-permute-done.13.rest_2_.rest_3_), channel_id=1, source_target_pairs={{0,64},{8,72},{16,80},{24,88},{32,96},{40,104},{48,112},{56,120},{... | collective-permute-start | bytes 491528 | tf_op jit(solution)/shard_map/ppermute | solution.py:411
  127.8 1.2 collective-permute-start.18
  128.9 2.0 %first.1 = (f32[136,2560]{1,0:T(8,128)S(1)}, bf16[2560,128]{1,0:T(8,128)(2,1)S(1)}) custom-call(s32[1]{0:T(128)} %bitcast.3.core_ref, bf16[320,512]{1,0:T(8,128)(2,1)S(1)} %convolution_convert_fusion.own_ref, bf16[320,512]{1,0:T(8,128)(2,1)S(1)} %collective-permute-done.12.pair_ref, bf16[320,256]{1,0:T(8,128)(2,1)S(1)} %convolution_convert_fusion.1.kv_ref.rest_0_), custom_call_target="tpu_custom_call" | custom-call | flops 419430400 | bytes 3145728 | tf_op jit(solution)/shard_map/first/pallas_call | solution.py:255
  131.0 1.3 more.3.state_ref
  132.4 14.0 %more.4.state_ref = f32[136,2560]{1,0:T(8,128)S(1)} custom-call(s32[3]{0:T(128)S(1)} %add_convert_fusion.flag_ref, bf16[2560,128]{1,0:T(8,128)(2,1)S(1)} %get-tuple-element.18.q_ref, f32[136,2560]{1,0:T(8,128)S(1)} %more.3.state_ref, bf16[960,256]{1,0:T(8,128)(2,1)} %collective-permute-done.11.rest_0_.rest_4_, ...), custom_call_target="tpu_custom_call" | custom-call | flops 3774873600 | bytes 3145728 | tf_op jit(solution)/shard_map/more/pallas_call | solution.py:307
  146.4 6.4 %more.5 = (f32[136,1280]{1,0:T(8,128)S(1)}, f32[136,1280]{1,0:T(8,128)S(1)}) custom-call(s32[3]{0:T(128)S(1)} %add_convert_fusion.flag_ref, bf16[2560,128]{1,0:T(8,128)(2,1)S(1)} %get-tuple-element.18.q_ref, f32[136,2560]{1,0:T(8,128)S(1)} %more.4.state_ref, bf16[320,256]{1,0:T(8,128)(2,1)S(1)} %collective-permute-done.16.rest_0_.rest_7_, ...), custom_call_target="tpu_custom_call" | custom-call | flops 1258291200 | bytes 3145728 | tf_op jit(solution)/shard_map/more/pallas_call | solution.py:307
  152.8 1.5 collective-permute-start.19
  154.5 0.1 reshape.135.code_ref
  154.6 3.8 %pages.1 = (bf16[320,256]{1,0:T(8,128)(2,1)S(1)}, bf16[320,256]{1,0:T(8,128)(2,1)S(1)}) custom-call(s32[3]{0:T(128)S(1)} %pad_add_fusion.place_ref, s32[192]{0:T(256)S(1)} %reshape.135.code_ref, bf16[320,256]{1,0:T(8,128)(2,1)S(1)} %convolution_convert_fusion.1.kv_ref.rest_0_, bf16[320,256]{1,0:T(8,128)(2,1)S(1)} %copy-done.7, ...), custom_call_target="tpu_custom_call" | custom-call | tf_op jit(solution)/shard_map/pages/pallas_call | solution.py:385
  158.3 0.1 collective-permute-start.20
  158.5 1.0 and_reduce_fusion
  159.5 0.3 collective-permute-done.20
  159.8 0.9 broadcast_select_fusion
  160.7 1.0 finish.1
  (72 shorter events, 1.0 us)
Async XLA Ops:
  7.2 17.4 %copy-start.16 = (s32[40]{0:T(128)S(1)}, s32[40]{0:T(128)}, u32[]{:S(2)}) copy-start(s32[40]{0:T(128)} %param.18) | copy-start | bytes 484
  7.2 17.4 %copy-start.17 = (s32[40]{0:T(128)S(1)}, s32[40]{0:T(128)}, u32[]{:S(2)}) copy-start(s32[40]{0:T(128)} %param.17) | copy-start | bytes 484
  7.2 62.9 %all-gather.3.cloned.1.call-start = ((), (), s32[]{:S(2)}) async-start(), calls=%async_computation.1 | async-start | bytes 2949120 | tf_op jit(solution)/shard_map/all_gather | solution.py:457
  8.1 7.7 %collective-permute-start.2 = (bf16[160,256]{1,0:T(8,128)(2,1)S(1)}, bf16[160,256]{1,0:T(8,128)(2,1)S(1)}, u32[]{:S(2)}, u32[]{:S(2)}) collective-permute-start(bf16[160,256]{1,0:T(8,128)(2,1)S(1)} %slice.15), channel_id=1, source_target_pairs={{0,16},{8,24},{16,32},{24,40},{32,48},{40,56},{48,0},{56,8},{64,80... | collective-permute-start | bytes 245768 | tf_op jit(solution)/shard_map/ppermute | solution.py:415
  9.8 9.1 %collective-permute-start.1 = (bf16[160,256]{1,0:T(8,128)(2,1)S(1)}, bf16[160,256]{1,0:T(8,128)(2,1)S(1)}, u32[]{:S(2)}, u32[]{:S(2)}) collective-permute-start(bf16[160,256]{1,0:T(8,128)(2,1)S(1)} %slice.15), channel_id=1, source_target_pairs={{0,32},{8,40},{16,48},{24,56},{32,0},{40,8},{48,16},{56,24},{64,96... | collective-permute-start | bytes 245768 | tf_op jit(solution)/shard_map/ppermute | solution.py:415
  12.8 6.1 %collective-permute-start = (bf16[160,256]{1,0:T(8,128)(2,1)S(1)}, bf16[160,256]{1,0:T(8,128)(2,1)S(1)}, u32[]{:S(2)}, u32[]{:S(2)}) collective-permute-start(bf16[160,256]{1,0:T(8,128)(2,1)S(1)} %slice.15), channel_id=1, source_target_pairs={{0,48},{8,56},{16,0},{24,8},{32,16},{40,24},{48,32},{56,40},{64,11... | collective-permute-start | bytes 245768 | tf_op jit(solution)/shard_map/ppermute | solution.py:415
  13.5 1.0 copy-start.9
  14.5 0.8 copy-start.11
  15.3 4.5 %copy-start.12 = (bf16[160,768]{1,0:T(8,128)(2,1)S(1)}, bf16[160,768]{1,0:T(8,128)(2,1)}, u32[]{:S(2)}) copy-start(bf16[160,768]{1,0:T(8,128)(2,1)} %param.16) | copy-start | bytes 737284
  20.5 30.0 %collective-permute-start.6 = (bf16[160,512]{1,0:T(8,128)(2,1)}, bf16[160,512]{1,0:T(8,128)(2,1)}, u32[]{:S(2)}, u32[]{:S(2)}) collective-permute-start(bf16[160,512]{1,0:T(8,128)(2,1)} %slice.18), channel_id=1, source_target_pairs={{0,16},{8,24},{16,32},{24,40},{32,48},{40,56},{48,0},{56,8},{64,80... | collective-permute-start | bytes 491528 | tf_op jit(solution)/shard_map/ppermute | solution.py:415
  22.5 27.9 %collective-permute-start.5 = (bf16[160,512]{1,0:T(8,128)(2,1)}, bf16[160,512]{1,0:T(8,128)(2,1)}, u32[]{:S(2)}, u32[]{:S(2)}) collective-permute-start(bf16[160,512]{1,0:T(8,128)(2,1)} %slice.18), channel_id=1, source_target_pairs={{0,32},{8,40},{16,48},{24,56},{32,0},{40,8},{48,16},{56,24},{64,96... | collective-permute-start | bytes 491528 | tf_op jit(solution)/shard_map/ppermute | solution.py:415
  23.3 27.2 %collective-permute-start.4 = (bf16[160,512]{1,0:T(8,128)(2,1)}, bf16[160,512]{1,0:T(8,128)(2,1)}, u32[]{:S(2)}, u32[]{:S(2)}) collective-permute-start(bf16[160,512]{1,0:T(8,128)(2,1)} %slice.18), channel_id=1, source_target_pairs={{0,48},{8,56},{16,0},{24,8},{32,16},{40,24},{48,32},{56,40},{64,11... | collective-permute-start | bytes 491528 | tf_op jit(solution)/shard_map/ppermute | solution.py:415
  25.5 15.5 %all-to-all-start = ((f32[32,1,512]{2,1,0:T(1,128)}), f32[32,1,512]{2,1,0:T(1,128)S(1)}, u32[]{:S(2)}, u32[]{:S(2)}) async-start(f32[32,1,512]{2,1,0:T(1,128)} %all_to_all.8), calls=%async_computation | async-start | bytes 131072 | tf_op jit(solution)/shard_map/all_to_all | solution.py:533
  32.6 70.1 %all-gather.5.cloned.1.call-start = ((), (), s32[]{:S(2)}) async-start(), calls=%async_computation.2 | async-start | bytes 5898240 | tf_op jit(solution)/shard_map/all_gather | solution.py:457
  41.0 22.5 %copy-start = (bf16[320,5120]{1,0:T(8,128)(2,1)S(1)}, bf16[320,5120]{1,0:T(8,128)(2,1)}, u32[]{:S(2)}) copy-start(bf16[320,5120]{1,0:T(8,128)(2,1)} %table_ref.1) | copy-start | bytes 9830404
  42.0 1.3 copy-start.3
  43.3 1.0 copy-start.8
  44.9 18.6 %copy-start.10 = (bf16[16,5120]{1,0:T(8,128)(2,1)S(1)}, bf16[16,5120]{1,0:T(8,128)(2,1)}, u32[]{:S(2)}) copy-start(bf16[16,5120]{1,0:T(8,128)(2,1)} %embed_ref.1) | copy-start | bytes 491524
  44.9 8.3 %collective-permute-start.3 = (f32[16,384]{1,0:T(8,128)S(1)}, f32[16,384]{1,0:T(8,128)}, u32[]{:S(2)}, u32[]{:S(2)}) collective-permute-start(f32[16,384]{1,0:T(8,128)S(1)} %place.1), channel_id=1, source_target_pairs={{0,1},{1,0},{2,3},{3,2},{4,5},{5,4},{6,7},{7,6},{8,9},{9,8},{10,11... | collective-permute-start | bytes 73736 | tf_op jit(solution)/shard_map/ppermute | solution.py:539
  55.1 2.7 %collective-permute-start.7 = (f32[16,384]{1,0:T(8,128)S(1)}, f32[16,384]{1,0:T(8,128)S(1)}, u32[]{:S(2)}, u32[]{:S(2)}) collective-permute-start(f32[16,384]{1,0:T(8,128)S(1)} %add.129), channel_id=1, source_target_pairs={{0,2},{1,3},{2,0},{3,1},{4,6},{5,7},{6,4},{7,5},{8,10},{9,11},{10,... | collective-permute-start | bytes 73736 | tf_op jit(solution)/shard_map/ppermute | solution.py:539
  58.3 4.4 %collective-permute-start.8 = (f32[16,384]{1,0:T(8,128)}, f32[16,384]{1,0:T(8,128)S(1)}, u32[]{:S(2)}, u32[]{:S(2)}) collective-permute-start(f32[16,384]{1,0:T(8,128)} %add.130), channel_id=1, source_target_pairs={{0,4},{1,5},{2,6},{3,7},{4,0},{5,1},{6,2},{7,3},{8,12},{9,13},{10,... | collective-permute-start | bytes 73736 | tf_op jit(solution)/shard_map/ppermute | solution.py:539
  68.4 1.8 %copy-start.1 = (bf16[320,5120]{1,0:T(8,128)(2,1)}, bf16[320,5120]{1,0:T(8,128)(2,1)S(1)}, u32[]{:S(2)}) copy-start(bf16[320,5120]{1,0:T(8,128)(2,1)S(1)} %hidden.1) | copy-start | bytes 9830404
  70.1 23.0 %copy-start.13 = (s32[40]{0:T(128)S(1)}, s32[40]{0:T(128)}, u32[]{:S(2)}) copy-start(s32[40]{0:T(128)} %iota_multiply_fusion) | copy-start | bytes 484
  70.1 32.6 %copy-start.2 = (bf16[320,5120]{1,0:T(8,128)(2,1)S(1)}, bf16[320,5120]{1,0:T(8,128)(2,1)}, u32[]{:S(2)}) copy-start(bf16[320,5120]{1,0:T(8,128)(2,1)} %copy-done.1) | copy-start | bytes 9830404
  74.1 14.2 %collective-permute-start.10 = (bf16[320,256]{1,0:T(8,128)(2,1)S(1)}, bf16[320,256]{1,0:T(8,128)(2,1)S(1)}, u32[]{:S(2)}, u32[]{:S(2)}) collective-permute-start(bf16[320,256]{1,0:T(8,128)(2,1)S(1)} %convolution_convert_fusion.1.kv_ref.rest_0_), channel_id=1, source_target_pairs={{0,32},{8,40},{16,48},{24,56},{32,0},{40,8},{48,16},{56,24},{64,96... | collective-permute-start | bytes 491528 | tf_op jit(solution)/shard_map/ppermute | solution.py:415
  74.4 13.9 %collective-permute-start.9 = (bf16[320,256]{1,0:T(8,128)(2,1)S(1)}, bf16[320,256]{1,0:T(8,128)(2,1)S(1)}, u32[]{:S(2)}, u32[]{:S(2)}) collective-permute-start(bf16[320,256]{1,0:T(8,128)(2,1)S(1)} %convolution_convert_fusion.1.kv_ref.rest_0_), channel_id=1, source_target_pairs={{0,16},{8,24},{16,32},{24,40},{32,48},{40,56},{48,0},{56,8},{64,80... | collective-permute-start | bytes 491528 | tf_op jit(solution)/shard_map/ppermute | solution.py:415
  88.3 0.9 copy-start.6
  89.2 0.7 copy-start.4
  89.9 12.8 %collective-permute-start.11 = (bf16[960,256]{1,0:T(8,128)(2,1)}, bf16[960,256]{1,0:T(8,128)(2,1)}, u32[]{:S(2)}, u32[]{:S(2)}) collective-permute-start(bf16[960,256]{1,0:T(8,128)(2,1)} %pad_maximum_fusion), channel_id=1, source_target_pairs={{0,64},{8,72},{16,80},{24,88},{32,96},{40,104},{48,112},{56,120},{... | collective-permute-start | bytes 1474568 | tf_op jit(solution)/shard_map/ppermute | solution.py:411
  93.4 38.9 %collective-permute-start.14 = (bf16[960,256]{1,0:T(8,128)(2,1)}, bf16[960,256]{1,0:T(8,128)(2,1)}, u32[]{:S(2)}, u32[]{:S(2)}) collective-permute-start(bf16[960,256]{1,0:T(8,128)(2,1)} %pad_maximum_fusion), channel_id=1, source_target_pairs={{0,192},{8,200},{16,208},{24,216},{32,224},{40,232},{48,240},{56,2... | collective-permute-start | bytes 1474568 | tf_op jit(solution)/shard_map/ppermute | solution.py:411
  93.5 38.8 %collective-permute-start.15 = (bf16[960,256]{1,0:T(8,128)(2,1)}, bf16[960,256]{1,0:T(8,128)(2,1)}, u32[]{:S(2)}, u32[]{:S(2)}) collective-permute-start(bf16[960,256]{1,0:T(8,128)(2,1)} %pad_maximum_fusion), channel_id=1, source_target_pairs={{0,128},{8,136},{16,144},{24,152},{32,160},{40,168},{48,176},{56,1... | collective-permute-start | bytes 1474568 | tf_op jit(solution)/shard_map/ppermute | solution.py:411
  107.0 24.0 %copy-start.5 = (bf16[320,256]{1,0:T(8,128)(2,1)S(1)}, bf16[320,256]{1,0:T(8,128)(2,1)}, u32[]{:S(2)}) copy-start(bf16[320,256]{1,0:T(8,128)(2,1)} %copy-done.4) | copy-start | bytes 491524
  107.0 24.0 %copy-start.7 = (bf16[320,256]{1,0:T(8,128)(2,1)S(1)}, bf16[320,256]{1,0:T(8,128)(2,1)}, u32[]{:S(2)}) copy-start(bf16[320,256]{1,0:T(8,128)(2,1)} %copy-done.6) | copy-start | bytes 491524
  107.0 20.7 %collective-permute-start.12 = (bf16[320,512]{1,0:T(8,128)(2,1)S(1)}, bf16[320,512]{1,0:T(8,128)(2,1)S(1)}, u32[]{:S(2)}, u32[]{:S(2)}) collective-permute-start(bf16[320,512]{1,0:T(8,128)(2,1)S(1)} %convolution_convert_fusion.own_ref), channel_id=1, source_target_pairs={{0,8},{8,0},{16,24},{24,16},{32,40},{40,32},{48,56},{56,48},{64,72... | collective-permute-start | bytes 983048 | tf_op jit(solution)/shard_map/ppermute | solution.py:419
  118.6 5.8 %collective-permute-start.13 = (bf16[320,256]{1,0:T(8,128)(2,1)S(1)}, bf16[320,256]{1,0:T(8,128)(2,1)S(1)}, u32[]{:S(2)}, u32[]{:S(2)}) collective-permute-start(bf16[320,256]{1,0:T(8,128)(2,1)S(1)} %convolution_convert_fusion.1.kv_ref.rest_0_), channel_id=1, source_target_pairs={{0,48},{8,56},{16,0},{24,8},{32,16},{40,24},{48,32},{56,40},{64,11... | collective-permute-start | bytes 491528 | tf_op jit(solution)/shard_map/ppermute | solution.py:415
  124.4 22.0 %collective-permute-start.16 = (bf16[320,256]{1,0:T(8,128)(2,1)S(1)}, bf16[320,256]{1,0:T(8,128)(2,1)S(1)}, u32[]{:S(2)}, u32[]{:S(2)}) collective-permute-start(bf16[320,256]{1,0:T(8,128)(2,1)S(1)} %collective-permute-done.13.rest_2_.rest_3_), channel_id=1, source_target_pairs={{0,64},{8,72},{16,80},{24,88},{32,96},{40,104},{48,112},{56,120},{... | collective-permute-start | bytes 491528 | tf_op jit(solution)/shard_map/ppermute | solution.py:411
  127.7 18.6 %collective-permute-start.17 = (bf16[320,256]{1,0:T(8,128)(2,1)S(1)}, bf16[320,256]{1,0:T(8,128)(2,1)S(1)}, u32[]{:S(2)}, u32[]{:S(2)}) collective-permute-start(bf16[320,256]{1,0:T(8,128)(2,1)S(1)} %collective-permute-done.13.rest_2_.rest_3_), channel_id=1, source_target_pairs={{0,192},{8,200},{16,208},{24,216},{32,224},{40,232},{48,240},{56,2... | collective-permute-start | bytes 491528 | tf_op jit(solution)/shard_map/ppermute | solution.py:411
  127.8 18.6 %collective-permute-start.18 = (bf16[320,256]{1,0:T(8,128)(2,1)S(1)}, bf16[320,256]{1,0:T(8,128)(2,1)S(1)}, u32[]{:S(2)}, u32[]{:S(2)}) collective-permute-start(bf16[320,256]{1,0:T(8,128)(2,1)S(1)} %collective-permute-done.13.rest_2_.rest_3_), channel_id=1, source_target_pairs={{0,128},{8,136},{16,144},{24,152},{32,160},{40,168},{48,176},{56,1... | collective-permute-start | bytes 491528 | tf_op jit(solution)/shard_map/ppermute | solution.py:411
  152.8 7.9 %collective-permute-start.19 = (f32[136,1280]{1,0:T(8,128)S(1)}, f32[136,1280]{1,0:T(8,128)S(1)}, u32[]{:S(2)}, u32[]{:S(2)}) collective-permute-start(f32[136,1280]{1,0:T(8,128)S(1)} %get-tuple-element.21), channel_id=1, source_target_pairs={{0,8},{8,0},{16,24},{24,16},{32,40},{40,32},{48,56},{56,48},{64,72... | collective-permute-start | bytes 2088968 | tf_op jit(solution)/shard_map/ppermute | solution.py:419
  154.6 4.0 %copy-start.14 = (s32[40]{0:T(128)S(1)}, s32[40]{0:T(128)}, u32[]{:S(2)}) copy-start(s32[40]{0:T(128)} %iota_add_fusion) | copy-start | bytes 484
  154.6 4.0 %copy-start.15 = (pred[32]{0:T(512)(128)(4,1)S(1)}, pred[32]{0:T(512)(128)(4,1)}, u32[]{:S(2)}) copy-start(pred[32]{0:T(512)(128)(4,1)} %fusion.2) | copy-start | bytes 100
  158.3 1.5 collective-permute-start.20
Sparse Core Ops, SparseCore 0:
  19.9 30.4 all-gather.2
  54.1 38.3 all-gather.4

commit v6 on v5

--- a/solution.py
+++ b/solution.py
@@ -91,12 +91,12 @@
 
 def place_kernel(offset_ref, parts_ref, token_ref, out_ref):
     count = parts_ref.shape[0]
-    token = lax.broadcasted_iota(jnp.int32, (count, TOK), 1) - offset_ref[0] * BLK
+    token = lax.broadcasted_iota(jnp.int32, (TOK, count), 0) - offset_ref[0] * BLK
     pick = jnp.where(token == token_ref[...], 1.0, 0.0).astype(jnp.bfloat16)
     total = jnp.zeros((LAT, TOK), jnp.float32)
     for part in reversed(split_three(parts_ref[...])):
         total = total + lax.dot_general(
-            part, pick, (((0,), (0,)), ((), ())), preferred_element_type=jnp.float32
+            part, pick, (((0,), (1,)), ((), ())), preferred_element_type=jnp.float32
         )
     out_ref[...] = total
 
@@ -107,7 +107,7 @@
     width = np.arange(SEQ).reshape(-1, 1, 1) * COLS + col
     inside = (width >= 0) & (width < SEQ * COLS)
     token = np.where(inside, row * SEQ * COLS + width, -(1 << 20))
-    return token.astype(np.int32).reshape(SEQ * EXT, 1)
+    return token.astype(np.int32).reshape(1, SEQ * EXT)
 
 
 def place_latents(parts, offset):
@@ -121,10 +121,10 @@
     )(offset.reshape(1), parts, jnp.asarray(place_table()))
 
 
-def hidden_kernel(latent_ref, bias_ref, embed_ref, table_ref, gain_ref, out_ref, hid_ref, sq_ref):
+def hidden_kernel(latent_ref, embed_ref, table_ref, gain_ref, out_ref, hid_ref, sq_ref):
     step = pl.program_id(0)
     width = table_ref.shape[1]
-    latent = latent_ref[...][:, :BLK] + bias_ref[...]
+    latent = latent_ref[...][:, :BLK]
     latent = jnp.concatenate(split_three(latent), axis=0)
     embed = embed_ref[...]
     hidden = lax.dot_general(
@@ -163,7 +163,7 @@
                 out_ref[:, start : start + RBLK] = piece.astype(jnp.bfloat16)
 
 
-def normed_hidden(latent, conv_bias, embed_weight, position_table, norm_gain):
+def normed_hidden(latent, embed_weight, position_table, gain):
     depth = position_table.shape[1]
     steps = 8
     width = depth // steps
@@ -172,7 +172,6 @@
         grid=(steps,),
         in_specs=[
             pl.BlockSpec((LAT, TOK), lambda i: (0, 0)),
-            pl.BlockSpec((LAT, 1), lambda i: (0, 0)),
             pl.BlockSpec((LAT, width), lambda i: (0, i)),
             pl.BlockSpec((BLK, width), lambda i: (0, i)),
             pl.BlockSpec((1, depth), lambda i: (0, 0)),
@@ -185,7 +184,7 @@
         ],
         compiler_params=params(dimension_semantics=("arbitrary",)),
         name="hidden",
-    )(latent, conv_bias.reshape(LAT, 1), embed_weight, position_table, norm_gain.reshape(1, depth))
+    )(latent, embed_weight, position_table, gain)
 
 
 def attend_block(masked, partner_full, keys, values, q_ref, state_ref):
@@ -470,11 +469,11 @@
     return jnp.dot(normed, weight, preferred_element_type=jnp.float32).astype(jnp.bfloat16)
 
 
-def attention_and_pages(me, targets, normed, kv_weight, query_weight):
+def attention_and_pages(me, codes, keep, normed, kv_weight, query_weight):
     core, z, y = me % 2, (me // 2) % 4, me // 8
     kv = project(normed, kv_weight)
     by_z, (near, far) = spread(kv, ((0, 1, 2), (3,)))
-    normed, unused = lax.optimization_barrier((normed, near[1]))
+    normed, unused, unused = lax.optimization_barrier((normed, near[1], by_z[3]))
     own_queries = project(normed, query_weight)
     pair_queries = other_core(own_queries)
 
@@ -485,9 +484,11 @@
     state = attend_more(
         flag(z >= 1, z >= 2, z >= 3), queries, state, [by_z[1], by_z[2], by_z[3]]
     )
+    state, near[3], near[2] = lax.optimization_barrier((state, near[3], near[2]))
     state = attend_more(
         flag(y >= 1, y >= 3, y >= 2), queries, state, [near[1], near[3], near[2]]
     )
+    state, far[1], far[3], far[2] = lax.optimization_barrier((state, far[1], far[3], far[2]))
     own, sent = attend_more(
         flag(y >= 1, y >= 3, y >= 2), queries, state, [far[1], far[3], far[2]], split=True
     )
@@ -496,10 +497,10 @@
     arrays = [by_z[count] for count in range(4)]
     arrays += [group[count] for group in (near, far) for count in (1, 2, 3)]
     place = jnp.stack([y, z, core])
-    own_pages, sent_pages = fetch_pages(place, page_codes(targets, me), arrays)
+    own_pages, sent_pages = fetch_pages(place, codes, arrays)
     got_pages = other_core(sent_pages)
     attention = finish(own, got)
-    keep = held_here(targets, me).reshape(PAGES, 1, 1, 1)
+    keep = keep.reshape(PAGES, 1, 1, 1)
     shape = (PAGES, PAGE, 2, HD)
     kv_cache = jnp.where(keep, own_pages.reshape(shape), got_pages.reshape(shape))
     return attention, kv_cache
@@ -522,8 +523,6 @@
     kv_weight = stack_z(qkv_weight[:, GROUP * HD :], me)
     query_weight = stack_z(qkv_weight[:, : GROUP * HD], me)
     parts = partial_latents(features, conv_weight)
-    parts, kv_weight = lax.optimization_barrier((parts, kv_weight))
-    kv_weight = gather_rows(kv_weight)
     own = parts[: FRAMES * EXT].reshape(FRAMES, EXT * LAT)
     target = (page_owner * PAGES + page_slot).astype(jnp.float32)
     target = jnp.broadcast_to(target, (FRAMES, PAGES))
@@ -531,6 +530,9 @@
     message = jnp.pad(message, ((0, 0), (0, 512 - message.shape[1])))
     message = jnp.broadcast_to(message[:, None], (FRAMES, SEQ // FRAMES, 512)).reshape(SEQ, 512)
     message = lax.all_to_all(message, "seq", split_axis=0, concat_axis=0, tiled=True)
+    gain = norm_gain.reshape(1, -1)
+    message, kv_weight, gain = lax.optimization_barrier((message, kv_weight, gain))
+    kv_weight = gather_rows(kv_weight)
     targets = message[:, EXT * LAT : EXT * LAT + PAGES].astype(jnp.int32)
     offset = tensor - me % (SEQ // FRAMES)
     latent = place_latents(message[:, : EXT * LAT].reshape(SEQ * EXT, LAT), offset)
@@ -540,8 +542,11 @@
         if bit == 1:
             latent, query_weight = lax.optimization_barrier((latent, query_weight))
     query_weight = gather_rows(query_weight)
-    normed = normed_hidden(latent, conv_bias, embed_weight, position_table, norm_gain)
-    return attention_and_pages(me, targets, normed, kv_weight, query_weight)
+    latent = latent + conv_bias[:, None]
+    normed = normed_hidden(latent, embed_weight, position_table, gain)
+    codes, keep = page_codes(targets, me), held_here(targets, me)
+    normed, codes, keep = lax.optimization_barrier((normed, codes, keep))
+    return attention_and_pages(me, codes, keep, normed, kv_weight, query_weight)
 
 
 def solution(mesh):

time: 172 us -> 168 us (0.977); the launches traced: 169 us -> 167 us
  starting transfers between devices: 48.9 us -> 44 us
  waiting for transfers between devices: 38.8 us -> 42.9 us
    ppermute x9, waiting for transfers between devices: 21.3 us -> 9.02 us  [along_z(): lax.ppermute(value, 'seq', moves(lambda y, z, c: (y, (z + count) % 4, c)))]
    ppermute x3, starting transfers between devices: 13.2 us -> 1.9 us  [other_core(): return lax.ppermute(value, 'seq', moves(lambda y, z, c: (y, z, 1 - c)))]
    ppermute x6, waiting for transfers between devices: 7.82 us -> 15.7 us  [along_y(): lax.ppermute(value, 'seq', moves(lambda y, z, c: ((y + count) % 4, z, c)))]
    ppermute x3, waiting for transfers between devices: 1.01 us -> 7.39 us  [on_device(): latent = latent + lax.ppermute(latent, 'tensor', swap)]
    ppermute x6, starting transfers between devices: 7.96 us -> 13.2 us  [along_y(): lax.ppermute(value, 'seq', moves(lambda y, z, c: ((y + count) % 4, z, c)))]
    all_gather x2, waiting for transfers between devices: 0.01 us -> 4.77 us  [gather_rows(): lax.all_gather(stacked, 'seq', axis=0, tiled=True, axis_index_groups=groups)]
    all_to_all x1, waiting for transfers between devices: 8.38 us -> 4.62 us  [on_device(): lax.all_to_all(message, 'seq', split_axis=0, concat_axis=0, tiled=True)]
    add x3 -> x2, other arithmetic: 2.1 us -> 0.01 us  [on_device(): latent = latent + lax.ppermute(latent, 'tensor', swap)]
  transfers between devices with their start and end apart: 24 -> 24, of which waited for: 8 -> 9; matrix products, arithmetic and copies ran while one was open for 14% -> 14% of each run, Pallas kernels for 16% -> 17%
where the time goes in v6:
time: 168 us; the launch traced here: 167 us
  starting transfers between devices  44 us (26%)
  waiting for transfers between devices  42.9 us (26%)
  Pallas kernels  35.2 us (21%)
  between operations  14.4 us (9%)
  other arithmetic  11.3 us (7%)
  local copies, waits for them, and re-layouts  10.6 us (6%)
  matrix products  8.94 us (5%)
    pallas_call x3, Pallas kernels, attend_more(): pl.pallas_call(functools.partial(more_kernel, count, split), in_specs=[pl...  21.9 us
    ppermute x6, waiting for transfers between devices, along_y(): lax.ppermute(value, 'seq', moves(lambda y, z, c: ((y + count) % 4, z, c)))  15.7 us
    ppermute x6, starting transfers between devices, along_y(): lax.ppermute(value, 'seq', moves(lambda y, z, c: ((y + count) % 4, z, c)))  13.2 us
    ppermute x9, starting transfers between devices, along_z(): lax.ppermute(value, 'seq', moves(lambda y, z, c: (y, (z + count) % 4, c)))  12.8 us
    ppermute x3, starting transfers between devices, on_device(): latent = latent + lax.ppermute(latent, 'tensor', swap)  9.56 us
    ppermute x9, waiting for transfers between devices, along_z(): lax.ppermute(value, 'seq', moves(lambda y, z, c: (y, (z + count) % 4, c)))  9.02 us
    dot_general x2, matrix products, project(): jnp.dot(normed, weight, preferred_element_type=jnp.float32)  8.94 us
    ppermute x3, waiting for transfers between devices, on_device(): latent = latent + lax.ppermute(latent, 'tensor', swap)  7.39 us
  transfers between devices with their start and end apart: 24, of which 9 were waited for; matrix products, arithmetic and copies ran while one was open for 14% of the time, Pallas kernels for 17%

profile of v6, /device:TPU:25, one launch (start us, length us, event | category | flops | bytes accessed | tf_op | source)
XLA Modules:
  0.0 167.4 jit_solution(3445867507268707043)
XLA Ops:
  7.2 0.9 slice.16
  8.1 1.6 collective-permute-start.2
  9.7 3.0 %collective-permute-start.1 = (bf16[160,256]{1,0:T(8,128)(2,1)S(1)}, bf16[160,256]{1,0:T(8,128)(2,1)S(1)}, u32[]{:S(2)}, u32[]{:S(2)}) collective-permute-start(bf16[160,256]{1,0:T(8,128)(2,1)S(1)} %slice.16), channel_id=1, source_target_pairs={{0,32},{8,40},{16,48},{24,56},{32,0},{40,8},{48,16},{56,24},{64,96... | collective-permute-start | bytes 245768 | tf_op jit(solution)/shard_map/ppermute | solution.py:414
  12.7 0.7 collective-permute-start
  13.4 1.0 copy-done.10
  14.4 0.8 copy-done.14
  15.2 0.5 conv.1
  15.9 0.7 add_convert_fusion.2
  16.7 0.7 all_to_all.8
  17.4 6.5 %all-to-all-start = ((f32[32,1,512]{2,1,0:T(1,128)}), f32[32,1,512]{2,1,0:T(1,128)S(1)}, u32[]{:S(2)}, u32[]{:S(2)}) async-start(f32[32,1,512]{2,1,0:T(1,128)} %all_to_all.8), calls=%async_computation | async-start | bytes 131072 | tf_op jit(solution)/shard_map/all_to_all | solution.py:532
  24.0 0.9 fusion.1
  24.9 4.6 %all-to-all-done = f32[32,1,512]{2,1,0:T(1,128)S(1)} async-done(((f32[32,1,512]{2,1,0:T(1,128)}), f32[32,1,512]{2,1,0:T(1,128)S(1)}, u32[]{:S(2)}, u32[]{:S(2)}) %all-to-all-start) | async-done | bytes 65568 | tf_op jit(solution)/shard_map/all_to_all | solution.py:532
  29.6 0.7 slice.18
  30.3 0.6 collective-permute-start.6
  30.9 0.7 collective-permute-start.5
  31.6 2.0 %collective-permute-start.4 = (bf16[160,512]{1,0:T(8,128)(2,1)}, bf16[160,512]{1,0:T(8,128)(2,1)}, u32[]{:S(2)}, u32[]{:S(2)}) collective-permute-start(bf16[160,512]{1,0:T(8,128)(2,1)} %slice.18), channel_id=1, source_target_pairs={{0,48},{8,56},{16,0},{24,8},{32,16},{40,24},{48,32},{56,40},{64,11... | collective-permute-start | bytes 491528 | tf_op jit(solution)/shard_map/ppermute | solution.py:414
  33.6 0.9 reshape.131.parts_ref
  34.5 1.2 copy-done.3
  35.7 0.7 place.1
  36.4 5.6 %collective-permute-start.3 = (f32[16,384]{1,0:T(8,128)S(1)}, f32[16,384]{1,0:T(8,128)S(1)}, u32[]{:S(2)}, u32[]{:S(2)}) collective-permute-start(f32[16,384]{1,0:T(8,128)S(1)} %place.1), channel_id=1, source_target_pairs={{0,1},{1,0},{2,3},{3,2},{4,5},{5,4},{6,7},{7,6},{8,9},{9,8},{10,11... | collective-permute-start | bytes 73736 | tf_op jit(solution)/shard_map/ppermute | solution.py:541
  42.0 6.1 %collective-permute-done.3 = f32[16,384]{1,0:T(8,128)S(1)} collective-permute-done((f32[16,384]{1,0:T(8,128)S(1)}, f32[16,384]{1,0:T(8,128)S(1)}, u32[]{:S(2)}, u32[]{:S(2)}) %collective-permute-start.3) | collective-permute-done | bytes 24608 | tf_op jit(solution)/shard_map/ppermute | solution.py:541
  48.2 2.7 %fusion = bf16[640,512]{1,0:T(8,128)(2,1)} fusion(bf16[160,512]{1,0:T(8,128)(2,1)} %collective-permute-done.6, bf16[160,512]{1,0:T(8,128)(2,1)} %collective-permute-done.5, bf16[160,512]{1,0:T(8,128)(2,1)} %collective-permute-done.4, bf16[160,512]{1,0:T(8,128)(2,1)} %slice.18, pred[]{:T(512)S(6)} %eq.59, pred[]{:T(512)S(6)} %eq.58, pred[]{:T(512)S(6)} %lt.69), kind=kLoop, calls=%fused_computation.3 | loop fusion | flops 11468800 | bytes 1310723 | tf_op jit(solution)/shard_map/jit(_where)/select_n | solution.py:465
  51.1 1.2 convert_reduce_fusion
  52.2 0.3 select_reduce_fusion
  52.5 0.5 add_bitcast_fusion.4
  53.0 0.5 add_bitcast_fusion.2
  53.7 1.2 collective-permute-start.7
  54.9 0.6 add_bitcast_fusion
  55.5 1.3 collective-permute-done.7
  56.8 2.7 %collective-permute-start.8 = (f32[16,384]{1,0:T(8,128)S(1)}, f32[16,384]{1,0:T(8,128)S(1)}, u32[]{:S(2)}, u32[]{:S(2)}) collective-permute-start(f32[16,384]{1,0:T(8,128)S(1)} %add.138), channel_id=1, source_target_pairs={{0,4},{1,5},{2,6},{3,7},{4,0},{5,1},{6,2},{7,3},{8,12},{9,13},{10,... | collective-permute-start | bytes 73736 | tf_op jit(solution)/shard_map/ppermute | solution.py:541
  59.5 1.0 and_reduce_fusion
  60.5 0.7 stack.62
  61.3 0.1 reshape.132.code_ref
  61.5 0.7 add_add_fusion.latent_ref
  62.2 4.3 %hidden.1 = bf16[320,5120]{1,0:T(8,128)(2,1)S(1)} custom-call(f32[16,384]{1,0:T(8,128)S(1)} %add_add_fusion.latent_ref, bf16[16,5120]{1,0:T(8,128)(2,1)S(1)} %copy-done.11, bf16[320,5120]{1,0:T(8,128)(2,1)S(1)} %copy-done, bf16[1,5120]{1,0:T(2,128)(2,1)S(1)} %reshape.130.gain_ref), custom_call_target="tpu_custom_call" | custom-call | tf_op jit(solution)/shard_map/hidden/pallas_call | solution.py:170
  66.5 1.7 %copy-done.1 = bf16[320,5120]{1,0:T(8,128)(2,1)} copy-done((bf16[320,5120]{1,0:T(8,128)(2,1)}, bf16[320,5120]{1,0:T(8,128)(2,1)S(1)}, u32[]{:S(2)}) %copy-start.1) | copy-done | bytes 3276824
  68.3 3.9 %convolution_convert_fusion.1.kv_ref.rest_0_ = bf16[320,256]{1,0:T(8,128)(2,1)S(1)} fusion(bf16[320,5120]{1,0:T(8,128)(2,1)} %copy-done.1, bf16[5120,256]{1,0:T(8,128)(2,1)} %all-gather.3.cloned.1.call-done), kind=kOutput, calls=%fused_computation.1 | convolution fusion | flops 838942720 | bytes 6062080 | tf_op jit(solution)/shard_map/dot_general | solution.py:469
  72.2 2.6 %collective-permute-start.9 = (bf16[320,256]{1,0:T(8,128)(2,1)S(1)}, bf16[320,256]{1,0:T(8,128)(2,1)S(1)}, u32[]{:S(2)}, u32[]{:S(2)}) collective-permute-start(bf16[320,256]{1,0:T(8,128)(2,1)S(1)} %convolution_convert_fusion.1.kv_ref.rest_0_), channel_id=1, source_target_pairs={{0,16},{8,24},{16,32},{24,40},{32,48},{40,56},{48,0},{56,8},{64,80... | collective-permute-start | bytes 491528 | tf_op jit(solution)/shard_map/ppermute | solution.py:414
  74.9 2.4 %collective-permute-done.10.rest_1_.rest_2_ = bf16[320,256]{1,0:T(8,128)(2,1)S(1)} collective-permute-done((bf16[320,256]{1,0:T(8,128)(2,1)S(1)}, bf16[320,256]{1,0:T(8,128)(2,1)S(1)}, u32[]{:S(2)}, u32[]{:S(2)}) %collective-permute-start.10) | collective-permute-done | bytes 163872 | tf_op jit(solution)/shard_map/ppermute | solution.py:414
  77.3 4.6 %collective-permute-done.9.rest_0_.rest_1_ = bf16[320,256]{1,0:T(8,128)(2,1)S(1)} collective-permute-done((bf16[320,256]{1,0:T(8,128)(2,1)S(1)}, bf16[320,256]{1,0:T(8,128)(2,1)S(1)}, u32[]{:S(2)}, u32[]{:S(2)}) %collective-permute-start.9) | collective-permute-done | bytes 163872 | tf_op jit(solution)/shard_map/ppermute | solution.py:414
  81.9 0.8 pad_maximum_fusion
  82.8 1.1 collective-permute-start.11
  83.8 1.4 collective-permute-start.12
  85.2 1.4 collective-permute-start.15
  86.6 1.9 %collective-permute-done.12.rest_2_.rest_3_ = bf16[320,256]{1,0:T(8,128)(2,1)S(1)} collective-permute-done((bf16[320,256]{1,0:T(8,128)(2,1)S(1)}, bf16[320,256]{1,0:T(8,128)(2,1)S(1)}, u32[]{:S(2)}, u32[]{:S(2)}) %collective-permute-start.12) | collective-permute-done | bytes 163872 | tf_op jit(solution)/shard_map/ppermute | solution.py:414
  88.6 0.7 copy-done.12
  89.2 15.7 %collective-permute-done.11.rest_0_.rest_4_ = bf16[960,256]{1,0:T(8,128)(2,1)S(1)} collective-permute-done((bf16[960,256]{1,0:T(8,128)(2,1)}, bf16[960,256]{1,0:T(8,128)(2,1)S(1)}, u32[]{:S(2)}, u32[]{:S(2)}) %collective-permute-start.11) | collective-permute-done | bytes 491552 | tf_op jit(solution)/shard_map/ppermute | solution.py:410
  104.9 0.8 copy-done.8
  105.7 4.8 %all-gather.5.cloned.1.call-done = bf16[5120,512]{1,0:T(8,128)(2,1)} async-done(((bf16[640,512]{1,0:T(8,128)(2,1)}), bf16[5120,512]{1,0:T(8,128)(2,1)}) %all-gather.5.cloned.1.call-update) | async-done | bytes 5242896 | tf_op jit(solution)/shard_map/all_gather | solution.py:456
  110.5 5.1 %convolution_convert_fusion.own_ref = bf16[320,512]{1,0:T(8,128)(2,1)} fusion(bf16[320,5120]{1,0:T(8,128)(2,1)S(1)} %copy-done.2, bf16[5120,512]{1,0:T(8,128)(2,1)} %all-gather.5.cloned.1.call-done), kind=kOutput, calls=%fused_computation | convolution fusion | flops 1677885440 | bytes 8847360 | tf_op jit(solution)/shard_map/dot_general | solution.py:469
  115.6 1.1 collective-permute-start.13
  116.9 1.9 %collective-permute-start.16 = (bf16[320,256]{1,0:T(8,128)(2,1)}, bf16[320,256]{1,0:T(8,128)(2,1)S(1)}, u32[]{:S(2)}, u32[]{:S(2)}) collective-permute-start(bf16[320,256]{1,0:T(8,128)(2,1)} %copy-done.12), channel_id=1, source_target_pairs={{0,64},{8,72},{16,80},{24,88},{32,96},{40,104},{48,112},{56,120},{... | collective-permute-start | bytes 491528 | tf_op jit(solution)/shard_map/ppermute | solution.py:410
  118.7 7.1 %collective-permute-start.17 = (bf16[320,256]{1,0:T(8,128)(2,1)}, bf16[320,256]{1,0:T(8,128)(2,1)S(1)}, u32[]{:S(2)}, u32[]{:S(2)}) collective-permute-start(bf16[320,256]{1,0:T(8,128)(2,1)} %copy-done.12), channel_id=1, source_target_pairs={{0,192},{8,200},{16,208},{24,216},{32,224},{40,232},{48,240},{56,2... | collective-permute-start | bytes 491528 | tf_op jit(solution)/shard_map/ppermute | solution.py:410
  125.9 1.7 %collective-permute-start.18 = (bf16[320,256]{1,0:T(8,128)(2,1)}, bf16[320,256]{1,0:T(8,128)(2,1)S(1)}, u32[]{:S(2)}, u32[]{:S(2)}) collective-permute-start(bf16[320,256]{1,0:T(8,128)(2,1)} %copy-done.12), channel_id=1, source_target_pairs={{0,128},{8,136},{16,144},{24,152},{32,160},{40,168},{48,176},{56,1... | collective-permute-start | bytes 491528 | tf_op jit(solution)/shard_map/ppermute | solution.py:410
  127.6 3.0 %first.1 = (f32[136,2560]{1,0:T(8,128)S(1)}, bf16[2560,128]{1,0:T(8,128)(2,1)S(1)}) custom-call(s32[1]{0:T(128)} %bitcast.3.core_ref, bf16[320,512]{1,0:T(8,128)(2,1)} %convolution_convert_fusion.own_ref, bf16[320,512]{1,0:T(8,128)(2,1)S(1)} %collective-permute-done.13.pair_ref, bf16[320,256]{1,0:T(8,128)(2,1)S(1)} %convolution_convert_fusion.1.kv_ref.rest_0_), custom_call_target="tpu_custom_call" | custom-call | flops 419430400 | bytes 3145728 | tf_op jit(solution)/shard_map/first/pallas_call | solution.py:254
  130.6 1.3 more.3.state_ref
  132.0 14.1 %more.4.state_ref = f32[136,2560]{1,0:T(8,128)S(1)} custom-call(s32[3]{0:T(128)S(1)} %add_convert_fusion.flag_ref, bf16[2560,128]{1,0:T(8,128)(2,1)S(1)} %get-tuple-element.31.q_ref, f32[136,2560]{1,0:T(8,128)S(1)} %more.3.state_ref, bf16[960,256]{1,0:T(8,128)(2,1)S(1)} %copy-done.9, bf16[960,256]{1,0:T(8,128)(2,1)} %collective-permute-done.14.rest_1_.rest_6_, ...), custom_call_target="tpu_custom_call" | custom-call | flops 3774873600 | bytes 3145728 | tf_op jit(solution)/shard_map/more/pallas_call | solution.py:306
  146.2 6.4 %more.5 = (f32[136,1280]{1,0:T(8,128)S(1)}, f32[136,1280]{1,0:T(8,128)S(1)}) custom-call(s32[3]{0:T(128)S(1)} %add_convert_fusion.flag_ref, bf16[2560,128]{1,0:T(8,128)(2,1)S(1)} %get-tuple-element.31.q_ref, f32[136,2560]{1,0:T(8,128)S(1)} %more.4.state_ref, bf16[320,256]{1,0:T(8,128)(2,1)S(1)} %collective-permute-done.16.rest_0_.rest_7_, ...), custom_call_target="tpu_custom_call" | custom-call | flops 1258291200 | bytes 3145728 | tf_op jit(solution)/shard_map/more/pallas_call | solution.py:306
  152.6 0.7 collective-permute-start.19
  153.3 3.9 %pages.1 = (bf16[320,256]{1,0:T(8,128)(2,1)S(1)}, bf16[320,256]{1,0:T(8,128)(2,1)S(1)}) custom-call(s32[3]{0:T(128)S(1)} %pad_add_fusion.place_ref, s32[192]{0:T(256)S(1)} %reshape.132.code_ref, bf16[320,256]{1,0:T(8,128)(2,1)S(1)} %convolution_convert_fusion.1.kv_ref.rest_0_, bf16[320,256]{1,0:T(8,128)(2,1)S(1)} %copy-done.7, ...), custom_call_target="tpu_custom_call" | custom-call | tf_op jit(solution)/shard_map/pages/pallas_call | solution.py:384
  157.2 0.1 collective-permute-start.20
  157.3 1.4 collective-permute-done.20
  158.7 0.9 broadcast_select_fusion
  159.6 1.0 finish.1
  (71 shorter events, 1.0 us)
Async XLA Ops:
  7.2 16.8 %copy-start.17 = (bf16[5120]{0:T(1024)(128)(2,1)S(1)}, bf16[5120]{0:T(1024)(128)(2,1)}, u32[]{:S(2)}) copy-start(bf16[5120]{0:T(1024)(128)(2,1)} %param.15) | copy-start | bytes 30724
  8.1 15.9 %collective-permute-start.2 = (bf16[160,256]{1,0:T(8,128)(2,1)S(1)}, bf16[160,256]{1,0:T(8,128)(2,1)S(1)}, u32[]{:S(2)}, u32[]{:S(2)}) collective-permute-start(bf16[160,256]{1,0:T(8,128)(2,1)S(1)} %slice.16), channel_id=1, source_target_pairs={{0,16},{8,24},{16,32},{24,40},{32,48},{40,56},{48,0},{56,8},{64,80... | collective-permute-start | bytes 245768 | tf_op jit(solution)/shard_map/ppermute | solution.py:414
  9.7 14.3 %collective-permute-start.1 = (bf16[160,256]{1,0:T(8,128)(2,1)S(1)}, bf16[160,256]{1,0:T(8,128)(2,1)S(1)}, u32[]{:S(2)}, u32[]{:S(2)}) collective-permute-start(bf16[160,256]{1,0:T(8,128)(2,1)S(1)} %slice.16), channel_id=1, source_target_pairs={{0,32},{8,40},{16,48},{24,56},{32,0},{40,8},{48,16},{56,24},{64,96... | collective-permute-start | bytes 245768 | tf_op jit(solution)/shard_map/ppermute | solution.py:414
  12.7 11.3 %collective-permute-start = (bf16[160,256]{1,0:T(8,128)(2,1)S(1)}, bf16[160,256]{1,0:T(8,128)(2,1)S(1)}, u32[]{:S(2)}, u32[]{:S(2)}) collective-permute-start(bf16[160,256]{1,0:T(8,128)(2,1)S(1)} %slice.16), channel_id=1, source_target_pairs={{0,48},{8,56},{16,0},{24,8},{32,16},{40,24},{48,32},{56,40},{64,11... | collective-permute-start | bytes 245768 | tf_op jit(solution)/shard_map/ppermute | solution.py:414
  13.4 1.0 copy-start.10
  14.4 0.8 copy-start.14
  15.2 14.4 %copy-start.16 = (bf16[160,768]{1,0:T(8,128)(2,1)S(1)}, bf16[160,768]{1,0:T(8,128)(2,1)}, u32[]{:S(2)}) copy-start(bf16[160,768]{1,0:T(8,128)(2,1)} %param.16) | copy-start | bytes 737284
  15.8 18.8 %copy-start.15 = (s32[1,896]{1,0:T(1,128)S(1)}, s32[1,896]{1,0:T(1,128)}, u32[]{:S(2)}) copy-start(s32[1,896]{1,0:T(1,128)} %constant.105.clone.token_ref) | copy-start | bytes 10756
  17.4 12.2 %all-to-all-start = ((f32[32,1,512]{2,1,0:T(1,128)}), f32[32,1,512]{2,1,0:T(1,128)S(1)}, u32[]{:S(2)}, u32[]{:S(2)}) async-start(f32[32,1,512]{2,1,0:T(1,128)} %all_to_all.8), calls=%async_computation | async-start | bytes 131072 | tf_op jit(solution)/shard_map/all_to_all | solution.py:532
  23.9 44.4 %all-gather.3.cloned.1.call-start = ((), (), s32[]{:S(2)}) async-start(), calls=%async_computation.1 | async-start | bytes 2949120 | tf_op jit(solution)/shard_map/all_gather | solution.py:456
  29.6 80.9 %all-gather.5.cloned.1.call-start = ((), (), s32[]{:S(2)}) async-start(), calls=%async_computation.2 | async-start | bytes 5898240 | tf_op jit(solution)/shard_map/all_gather | solution.py:456
  30.3 17.8 %collective-permute-start.6 = (bf16[160,512]{1,0:T(8,128)(2,1)}, bf16[160,512]{1,0:T(8,128)(2,1)}, u32[]{:S(2)}, u32[]{:S(2)}) collective-permute-start(bf16[160,512]{1,0:T(8,128)(2,1)} %slice.18), channel_id=1, source_target_pairs={{0,16},{8,24},{16,32},{24,40},{32,48},{40,56},{48,0},{56,8},{64,80... | collective-permute-start | bytes 491528 | tf_op jit(solution)/shard_map/ppermute | solution.py:414
  30.9 17.3 %collective-permute-start.5 = (bf16[160,512]{1,0:T(8,128)(2,1)}, bf16[160,512]{1,0:T(8,128)(2,1)}, u32[]{:S(2)}, u32[]{:S(2)}) collective-permute-start(bf16[160,512]{1,0:T(8,128)(2,1)} %slice.18), channel_id=1, source_target_pairs={{0,32},{8,40},{16,48},{24,56},{32,0},{40,8},{48,16},{56,24},{64,96... | collective-permute-start | bytes 491528 | tf_op jit(solution)/shard_map/ppermute | solution.py:414
  31.6 16.6 %collective-permute-start.4 = (bf16[160,512]{1,0:T(8,128)(2,1)}, bf16[160,512]{1,0:T(8,128)(2,1)}, u32[]{:S(2)}, u32[]{:S(2)}) collective-permute-start(bf16[160,512]{1,0:T(8,128)(2,1)} %slice.18), channel_id=1, source_target_pairs={{0,48},{8,56},{16,0},{24,8},{32,16},{40,24},{48,32},{56,40},{64,11... | collective-permute-start | bytes 491528 | tf_op jit(solution)/shard_map/ppermute | solution.py:414
  33.6 28.6 %copy-start = (bf16[320,5120]{1,0:T(8,128)(2,1)S(1)}, bf16[320,5120]{1,0:T(8,128)(2,1)}, u32[]{:S(2)}) copy-start(bf16[320,5120]{1,0:T(8,128)(2,1)} %table_ref.1) | copy-start | bytes 9830404
  34.5 1.2 copy-start.3
  36.4 25.8 %copy-start.11 = (bf16[16,5120]{1,0:T(8,128)(2,1)S(1)}, bf16[16,5120]{1,0:T(8,128)(2,1)}, u32[]{:S(2)}) copy-start(bf16[16,5120]{1,0:T(8,128)(2,1)} %embed_ref.1) | copy-start | bytes 491524
  36.4 11.7 %collective-permute-start.3 = (f32[16,384]{1,0:T(8,128)S(1)}, f32[16,384]{1,0:T(8,128)S(1)}, u32[]{:S(2)}, u32[]{:S(2)}) collective-permute-start(f32[16,384]{1,0:T(8,128)S(1)} %place.1), channel_id=1, source_target_pairs={{0,1},{1,0},{2,3},{3,2},{4,5},{5,4},{6,7},{7,6},{8,9},{9,8},{10,11... | collective-permute-start | bytes 73736 | tf_op jit(solution)/shard_map/ppermute | solution.py:541
  53.7 3.1 %collective-permute-start.7 = (f32[16,384]{1,0:T(8,128)S(1)}, f32[16,384]{1,0:T(8,128)S(1)}, u32[]{:S(2)}, u32[]{:S(2)}) collective-permute-start(f32[16,384]{1,0:T(8,128)S(1)} %add.137), channel_id=1, source_target_pairs={{0,2},{1,3},{2,0},{3,1},{4,6},{5,7},{6,4},{7,5},{8,10},{9,11},{10,... | collective-permute-start | bytes 73736 | tf_op jit(solution)/shard_map/ppermute | solution.py:541
  56.8 4.7 %collective-permute-start.8 = (f32[16,384]{1,0:T(8,128)S(1)}, f32[16,384]{1,0:T(8,128)S(1)}, u32[]{:S(2)}, u32[]{:S(2)}) collective-permute-start(f32[16,384]{1,0:T(8,128)S(1)} %add.138), channel_id=1, source_target_pairs={{0,4},{1,5},{2,6},{3,7},{4,0},{5,1},{6,2},{7,3},{8,12},{9,13},{10,... | collective-permute-start | bytes 73736 | tf_op jit(solution)/shard_map/ppermute | solution.py:541
  66.5 1.8 %copy-start.1 = (bf16[320,5120]{1,0:T(8,128)(2,1)}, bf16[320,5120]{1,0:T(8,128)(2,1)S(1)}, u32[]{:S(2)}) copy-start(bf16[320,5120]{1,0:T(8,128)(2,1)S(1)} %hidden.1) | copy-start | bytes 9830404
  68.2 42.3 %copy-start.2 = (bf16[320,5120]{1,0:T(8,128)(2,1)S(1)}, bf16[320,5120]{1,0:T(8,128)(2,1)}, u32[]{:S(2)}) copy-start(bf16[320,5120]{1,0:T(8,128)(2,1)} %copy-done.1) | copy-start | bytes 9830404
  72.1 5.2 %collective-permute-start.10 = (bf16[320,256]{1,0:T(8,128)(2,1)S(1)}, bf16[320,256]{1,0:T(8,128)(2,1)S(1)}, u32[]{:S(2)}, u32[]{:S(2)}) collective-permute-start(bf16[320,256]{1,0:T(8,128)(2,1)S(1)} %convolution_convert_fusion.1.kv_ref.rest_0_), channel_id=1, source_target_pairs={{0,32},{8,40},{16,48},{24,56},{32,0},{40,8},{48,16},{56,24},{64,96... | collective-permute-start | bytes 491528 | tf_op jit(solution)/shard_map/ppermute | solution.py:414
  72.2 9.7 %collective-permute-start.9 = (bf16[320,256]{1,0:T(8,128)(2,1)S(1)}, bf16[320,256]{1,0:T(8,128)(2,1)S(1)}, u32[]{:S(2)}, u32[]{:S(2)}) collective-permute-start(bf16[320,256]{1,0:T(8,128)(2,1)S(1)} %convolution_convert_fusion.1.kv_ref.rest_0_), channel_id=1, source_target_pairs={{0,16},{8,24},{16,32},{24,40},{32,48},{40,56},{48,0},{56,8},{64,80... | collective-permute-start | bytes 491528 | tf_op jit(solution)/shard_map/ppermute | solution.py:414
  77.3 11.3 %copy-start.4 = (bf16[320,256]{1,0:T(8,128)(2,1)}, bf16[320,256]{1,0:T(8,128)(2,1)S(1)}, u32[]{:S(2)}) copy-start(bf16[320,256]{1,0:T(8,128)(2,1)S(1)} %collective-permute-done.10.rest_1_.rest_2_) | copy-start | bytes 491524
  81.9 6.6 %copy-start.6 = (bf16[320,256]{1,0:T(8,128)(2,1)}, bf16[320,256]{1,0:T(8,128)(2,1)S(1)}, u32[]{:S(2)}) copy-start(bf16[320,256]{1,0:T(8,128)(2,1)S(1)} %collective-permute-done.9.rest_0_.rest_1_) | copy-start | bytes 491524
  82.8 22.2 %collective-permute-start.11 = (bf16[960,256]{1,0:T(8,128)(2,1)}, bf16[960,256]{1,0:T(8,128)(2,1)S(1)}, u32[]{:S(2)}, u32[]{:S(2)}) collective-permute-start(bf16[960,256]{1,0:T(8,128)(2,1)} %pad_maximum_fusion), channel_id=1, source_target_pairs={{0,64},{8,72},{16,80},{24,88},{32,96},{40,104},{48,112},{56,120},{... | collective-permute-start | bytes 1474568 | tf_op jit(solution)/shard_map/ppermute | solution.py:410
  83.8 4.7 %collective-permute-start.12 = (bf16[320,256]{1,0:T(8,128)(2,1)S(1)}, bf16[320,256]{1,0:T(8,128)(2,1)S(1)}, u32[]{:S(2)}, u32[]{:S(2)}) collective-permute-start(bf16[320,256]{1,0:T(8,128)(2,1)S(1)} %convolution_convert_fusion.1.kv_ref.rest_0_), channel_id=1, source_target_pairs={{0,48},{8,56},{16,0},{24,8},{32,16},{40,24},{48,32},{56,40},{64,11... | collective-permute-start | bytes 491528 | tf_op jit(solution)/shard_map/ppermute | solution.py:414
  85.2 46.7 %collective-permute-start.14 = (bf16[960,256]{1,0:T(8,128)(2,1)}, bf16[960,256]{1,0:T(8,128)(2,1)}, u32[]{:S(2)}, u32[]{:S(2)}) collective-permute-start(bf16[960,256]{1,0:T(8,128)(2,1)} %pad_maximum_fusion), channel_id=1, source_target_pairs={{0,192},{8,200},{16,208},{24,216},{32,224},{40,232},{48,240},{56,2... | collective-permute-start | bytes 1474568 | tf_op jit(solution)/shard_map/ppermute | solution.py:410
  85.2 46.7 %collective-permute-start.15 = (bf16[960,256]{1,0:T(8,128)(2,1)}, bf16[960,256]{1,0:T(8,128)(2,1)}, u32[]{:S(2)}, u32[]{:S(2)}) collective-permute-start(bf16[960,256]{1,0:T(8,128)(2,1)} %pad_maximum_fusion), channel_id=1, source_target_pairs={{0,128},{8,136},{16,144},{24,152},{32,160},{40,168},{48,176},{56,1... | collective-permute-start | bytes 1474568 | tf_op jit(solution)/shard_map/ppermute | solution.py:410
  88.6 0.7 copy-start.12
  104.9 0.8 copy-start.8
  115.6 15.0 %copy-start.5 = (bf16[320,256]{1,0:T(8,128)(2,1)S(1)}, bf16[320,256]{1,0:T(8,128)(2,1)}, u32[]{:S(2)}) copy-start(bf16[320,256]{1,0:T(8,128)(2,1)} %copy-done.4) | copy-start | bytes 491524
  115.6 15.0 %copy-start.7 = (bf16[320,256]{1,0:T(8,128)(2,1)S(1)}, bf16[320,256]{1,0:T(8,128)(2,1)}, u32[]{:S(2)}) copy-start(bf16[320,256]{1,0:T(8,128)(2,1)} %copy-done.6) | copy-start | bytes 491524
  115.6 15.0 %copy-start.13 = (bf16[320,256]{1,0:T(8,128)(2,1)S(1)}, bf16[320,256]{1,0:T(8,128)(2,1)}, u32[]{:S(2)}) copy-start(bf16[320,256]{1,0:T(8,128)(2,1)} %copy-done.12) | copy-start | bytes 491524
  115.6 10.3 %collective-permute-start.13 = (bf16[320,512]{1,0:T(8,128)(2,1)}, bf16[320,512]{1,0:T(8,128)(2,1)S(1)}, u32[]{:S(2)}, u32[]{:S(2)}) collective-permute-start(bf16[320,512]{1,0:T(8,128)(2,1)} %convolution_convert_fusion.own_ref), channel_id=1, source_target_pairs={{0,8},{8,0},{16,24},{24,16},{32,40},{40,32},{48,56},{56,48},{64,72... | collective-permute-start | bytes 983048 | tf_op jit(solution)/shard_map/ppermute | solution.py:418
  116.9 29.3 %collective-permute-start.16 = (bf16[320,256]{1,0:T(8,128)(2,1)}, bf16[320,256]{1,0:T(8,128)(2,1)S(1)}, u32[]{:S(2)}, u32[]{:S(2)}) collective-permute-start(bf16[320,256]{1,0:T(8,128)(2,1)} %copy-done.12), channel_id=1, source_target_pairs={{0,64},{8,72},{16,80},{24,88},{32,96},{40,104},{48,112},{56,120},{... | collective-permute-start | bytes 491528 | tf_op jit(solution)/shard_map/ppermute | solution.py:410
  118.7 27.4 %collective-permute-start.17 = (bf16[320,256]{1,0:T(8,128)(2,1)}, bf16[320,256]{1,0:T(8,128)(2,1)S(1)}, u32[]{:S(2)}, u32[]{:S(2)}) collective-permute-start(bf16[320,256]{1,0:T(8,128)(2,1)} %copy-done.12), channel_id=1, source_target_pairs={{0,192},{8,200},{16,208},{24,216},{32,224},{40,232},{48,240},{56,2... | collective-permute-start | bytes 491528 | tf_op jit(solution)/shard_map/ppermute | solution.py:410
  125.9 20.3 %collective-permute-start.18 = (bf16[320,256]{1,0:T(8,128)(2,1)}, bf16[320,256]{1,0:T(8,128)(2,1)S(1)}, u32[]{:S(2)}, u32[]{:S(2)}) collective-permute-start(bf16[320,256]{1,0:T(8,128)(2,1)} %copy-done.12), channel_id=1, source_target_pairs={{0,128},{8,136},{16,144},{24,152},{32,160},{40,168},{48,176},{56,1... | collective-permute-start | bytes 491528 | tf_op jit(solution)/shard_map/ppermute | solution.py:410
  130.6 1.4 copy-start.9
  152.6 7.1 %collective-permute-start.19 = (f32[136,1280]{1,0:T(8,128)S(1)}, f32[136,1280]{1,0:T(8,128)S(1)}, u32[]{:S(2)}, u32[]{:S(2)}) collective-permute-start(f32[136,1280]{1,0:T(8,128)S(1)} %get-tuple-element.41), channel_id=1, source_target_pairs={{0,8},{8,0},{16,24},{24,16},{32,40},{40,32},{48,56},{56,48},{64,72... | collective-permute-start | bytes 2088968 | tf_op jit(solution)/shard_map/ppermute | solution.py:418
  157.2 1.5 collective-permute-start.20
Sparse Core Ops, SparseCore 0:
  29.7 29.5 all-gather.2
  61.1 49.4 all-gather.4

commit v7 on v6

--- a/solution.py
+++ b/solution.py
@@ -24,7 +24,6 @@
 TILE = 256
 QROWS = GROUP * BLK
 STATE = HD + 8
-RBLK = 160
 VMEM = 24 * 1024 * 1024
 
 
@@ -155,12 +154,7 @@
         for tile in range(count):
             gain = gain_ref[:, tile * width : (tile + 1) * width].astype(jnp.float32)
             normed = hid_ref[tile] * factor * gain
-            for part in range(width // RBLK):
-                piece = normed[:, part * RBLK : (part + 1) * RBLK]
-                block = tile * (width // RBLK) + part
-                y, z, core = block // 8, block // 2 % 4, block % 2
-                start = ((y * 2 + core) * 4 + z) * RBLK
-                out_ref[:, start : start + RBLK] = piece.astype(jnp.bfloat16)
+            out_ref[:, tile * width : (tile + 1) * width] = normed.astype(jnp.bfloat16)
 
 
 def normed_hidden(latent, embed_weight, position_table, gain):
@@ -361,7 +355,7 @@
             if by_y == 0:
                 array, base = arrays[by_z], 0
             else:
-                array, base = arrays[3 + by_y + by_z // 3 * 3], by_z % 3 * BLK
+                array, base = arrays[3 + by_y + by_z // 2 * 3], by_z % 2 * BLK
             source = (((y - by_y) & 3) * 4 + ((z - by_z) & 3)) * 2 + core
             for entry in range(2 * MOST):
                 code = code_ref[source * 2 * MOST + entry]
@@ -451,30 +445,16 @@
     return by_z, by_y
 
 
-def gather_rows(stacked):
-    groups = [[(y * 4 + z) * 2 + c for y in range(4) for c in range(2)] for z in range(4)]
-    return lax.all_gather(stacked, "seq", axis=0, tiled=True, axis_index_groups=groups)
-
-
-def stack_z(value, me):
-    z = (me // 2) % 4
-    by_z = [value] + [along_z(value, count) for count in (1, 2, 3)]
-    orders = [jnp.concatenate([by_z[(own - i) % 4] for i in range(4)], axis=0) for own in range(4)]
-    low = jnp.where(z == 0, orders[0], orders[1])
-    high = jnp.where(z == 2, orders[2], orders[3])
-    return jnp.where(z < 2, low, high)
-
-
 def project(normed, weight):
     return jnp.dot(normed, weight, preferred_element_type=jnp.float32).astype(jnp.bfloat16)
 
 
-def attention_and_pages(me, codes, keep, normed, kv_weight, query_weight):
+def attention_and_pages(me, codes, keep, normed, weight):
     core, z, y = me % 2, (me // 2) % 4, me // 8
-    kv = project(normed, kv_weight)
-    by_z, (near, far) = spread(kv, ((0, 1, 2), (3,)))
-    normed, unused, unused = lax.optimization_barrier((normed, near[1], by_z[3]))
-    own_queries = project(normed, query_weight)
+    kv = project(normed, weight[:, GROUP * HD :])
+    normed, kv = lax.optimization_barrier((normed, kv))
+    by_z, (near, far) = spread(kv, ((0, 1), (2, 3)))
+    own_queries = project(normed, weight[:, : GROUP * HD])
     pair_queries = other_core(own_queries)
 
     def flag(*conditions):
@@ -488,10 +468,10 @@
     state = attend_more(
         flag(y >= 1, y >= 3, y >= 2), queries, state, [near[1], near[3], near[2]]
     )
-    state, far[1], far[3], far[2] = lax.optimization_barrier((state, far[1], far[3], far[2]))
-    own, sent = attend_more(
-        flag(y >= 1, y >= 3, y >= 2), queries, state, [far[1], far[3], far[2]], split=True
-    )
+    state, far[1], far[3] = lax.optimization_barrier((state, far[1], far[3]))
+    state = attend_more(flag(y >= 1, y >= 3), queries, state, [far[1], far[3]])
+    state, far[2] = lax.optimization_barrier((state, far[2]))
+    own, sent = attend_more(flag(y >= 2), queries, state, [far[2]], split=True)
     got = other_core(sent)
 
     arrays = [by_z[count] for count in range(4)]
@@ -520,8 +500,7 @@
     me = lax.axis_index("seq").astype(jnp.int32)
     tensor = lax.axis_index("tensor").astype(jnp.int32)
     tensor_count = lax.axis_size("tensor")
-    kv_weight = stack_z(qkv_weight[:, GROUP * HD :], me)
-    query_weight = stack_z(qkv_weight[:, : GROUP * HD], me)
+    weight = lax.all_gather(qkv_weight, "seq", axis=0, tiled=True)
     parts = partial_latents(features, conv_weight)
     own = parts[: FRAMES * EXT].reshape(FRAMES, EXT * LAT)
     target = (page_owner * PAGES + page_slot).astype(jnp.float32)
@@ -531,22 +510,18 @@
     message = jnp.broadcast_to(message[:, None], (FRAMES, SEQ // FRAMES, 512)).reshape(SEQ, 512)
     message = lax.all_to_all(message, "seq", split_axis=0, concat_axis=0, tiled=True)
     gain = norm_gain.reshape(1, -1)
-    message, kv_weight, gain = lax.optimization_barrier((message, kv_weight, gain))
-    kv_weight = gather_rows(kv_weight)
+    message, gain = lax.optimization_barrier((message, gain))
     targets = message[:, EXT * LAT : EXT * LAT + PAGES].astype(jnp.int32)
     offset = tensor - me % (SEQ // FRAMES)
     latent = place_latents(message[:, : EXT * LAT].reshape(SEQ * EXT, LAT), offset)
     for bit in (1, 2, 4):
         swap = [(i, i ^ bit) for i in range(tensor_count)]
         latent = latent + lax.ppermute(latent, "tensor", swap)
-        if bit == 1:
-            latent, query_weight = lax.optimization_barrier((latent, query_weight))
-    query_weight = gather_rows(query_weight)
     latent = latent + conv_bias[:, None]
     normed = normed_hidden(latent, embed_weight, position_table, gain)
     codes, keep = page_codes(targets, me), held_here(targets, me)
     normed, codes, keep = lax.optimization_barrier((normed, codes, keep))
-    return attention_and_pages(me, codes, keep, normed, kv_weight, query_weight)
+    return attention_and_pages(me, codes, keep, normed, weight)
 
 
 def solution(mesh):

time: 168 us -> 155 us (0.923); the launches traced: 167 us -> 152 us
  waiting for transfers between devices: 42.9 us -> 58 us
  starting transfers between devices: 44 us -> 30.9 us
  other arithmetic: 11.3 us -> 5.28 us
  matrix products: 8.94 us -> 4.76 us
  local copies, waits for them, and re-layouts: 10.6 us -> 6.47 us
  Pallas kernels: 35.2 us -> 32.2 us
    all_gather x2 -> x1, waiting for transfers between devices: 4.77 us -> 31.4 us  [on_device(): weight = lax.all_gather(qkv_weight, 'seq', axis=0, tiled=True)]
    ppermute x9 -> x3, starting transfers between devices: 12.8 us -> 2.94 us  [along_z(): lax.ppermute(value, 'seq', moves(lambda y, z, c: (y, (z + count) % 4, c)))]
    ppermute x6, waiting for transfers between devices: 15.7 us -> 9.11 us  [along_y(): lax.ppermute(value, 'seq', moves(lambda y, z, c: ((y + count) % 4, z, c)))]
    ppermute x6, starting transfers between devices: 13.2 us -> 7.54 us  [along_y(): lax.ppermute(value, 'seq', moves(lambda y, z, c: ((y + count) % 4, z, c)))]
    ppermute x3, waiting for transfers between devices: 7.39 us -> 2.61 us  [on_device(): latent = latent + lax.ppermute(latent, 'tensor', swap)]
    dot_general x2, matrix products: 8.94 us -> 4.76 us  [project(): jnp.dot(normed, weight, preferred_element_type=jnp.float32)]
    select_n x2 -> x0, other arithmetic: 3.64 us -> none  [stack_z(): return jnp.where(z < 2, low, high)]
    all_to_all x1, starting transfers between devices: 6.5 us -> 9.26 us  [on_device(): lax.all_to_all(message, 'seq', split_axis=0, concat_axis=0, tiled=True)]
  transfers between devices with their start and end apart: 24 -> 17, of which waited for: 9 -> 10; matrix products, arithmetic and copies ran while one was open for 14% -> 6% of each run, Pallas kernels for 17% -> 18%
where the time goes in v7:
time: 155 us; the launch traced here: 152 us
  waiting for transfers between devices  58 us (37%)
  Pallas kernels  32.2 us (21%)
  starting transfers between devices  30.9 us (20%)
  between operations  14.3 us (9%)
  local copies, waits for them, and re-layouts  6.47 us (4%)
  other arithmetic  5.28 us (3%)
  matrix products  4.76 us (3%)
    all_gather x1, waiting for transfers between devices, on_device(): weight = lax.all_gather(qkv_weight, 'seq', axis=0, tiled=True)  31.4 us
    pallas_call x4, Pallas kernels, attend_more(): pl.pallas_call(functools.partial(more_kernel, count, split), in_specs=[pl...  20.6 us
    all_to_all x1, starting transfers between devices, on_device(): lax.all_to_all(message, 'seq', split_axis=0, concat_axis=0, tiled=True)  9.26 us
    ppermute x6, waiting for transfers between devices, along_y(): lax.ppermute(value, 'seq', moves(lambda y, z, c: ((y + count) % 4, z, c)))  9.11 us
    ppermute x3, starting transfers between devices, on_device(): latent = latent + lax.ppermute(latent, 'tensor', swap)  8.71 us
    ppermute x3, waiting for transfers between devices, along_z(): lax.ppermute(value, 'seq', moves(lambda y, z, c: (y, (z + count) % 4, c)))  8.26 us
    ppermute x6, starting transfers between devices, along_y(): lax.ppermute(value, 'seq', moves(lambda y, z, c: ((y + count) % 4, z, c)))  7.54 us
    dot_general x2, matrix products, project(): jnp.dot(normed, weight, preferred_element_type=jnp.float32)  4.76 us
  transfers between devices with their start and end apart: 17, of which 10 were waited for; matrix products, arithmetic and copies ran while one was open for 6% of the time, Pallas kernels for 18%

profile of v7, /device:TPU:25, one launch (start us, length us, event | category | flops | bytes accessed | tf_op | source)
XLA Modules:
  0.0 151.9 jit_solution(14194032874271859590)
XLA Ops:
  7.2 0.0 all-gather.2.cloned.1.call-start
  7.2 0.7 all-gather.2.cloned.1.call-update
  7.9 1.0 copy-done.1
  8.9 0.8 copy-done.3
  9.7 0.5 conv.1
  10.2 0.1 reshape.129
  10.3 0.7 add_convert_fusion.1
  11.0 0.1 pad.17.clone
  11.1 0.7 all_to_all.8
  11.8 9.3 %all-to-all-start = ((f32[32,1,512]{2,1,0:T(1,128)}), f32[32,1,512]{2,1,0:T(1,128)S(1)}, u32[]{:S(2)}, u32[]{:S(2)}) async-start(f32[32,1,512]{2,1,0:T(1,128)} %all_to_all.8), calls=%async_computation | async-start | bytes 131072 | tf_op jit(solution)/shard_map/all_to_all | solution.py:511
  21.2 0.1 pad_add_fusion.flag_ref
  21.2 0.1 pad_add_fusion.1.flag_ref
  21.3 0.1 add_convert_fusion.flag_ref
  21.4 0.7 reshape.130.gain_ref
  22.2 4.6 %all-to-all-done = f32[32,1,512]{2,1,0:T(1,128)S(1)} async-done(((f32[32,1,512]{2,1,0:T(1,128)}), f32[32,1,512]{2,1,0:T(1,128)S(1)}, u32[]{:S(2)}, u32[]{:S(2)}) %all-to-all-start) | async-done | bytes 65568 | tf_op jit(solution)/shard_map/all_to_all | solution.py:511
  26.8 0.2 reshape.131.parts_ref
  26.9 0.0 copy-start.4
  26.9 0.7 copy-done.4
  27.6 0.7 place.1
  28.3 4.2 %collective-permute-start = (f32[16,384]{1,0:T(8,128)S(1)}, f32[16,384]{1,0:T(8,128)S(1)}, u32[]{:S(2)}, u32[]{:S(2)}) collective-permute-start(f32[16,384]{1,0:T(8,128)S(1)} %place.1), channel_id=1, source_target_pairs={{0,1},{1,0},{2,3},{3,2},{4,5},{5,4},{6,7},{7,6},{8,9},{9,8},{10,11... | collective-permute-start | bytes 73736 | tf_op jit(solution)/shard_map/ppermute | solution.py:519
  32.5 0.1 compare_and_fusion.1
  32.6 1.2 convert_reduce_fusion
  33.8 0.3 select_reduce_fusion
  34.1 0.1 slice_convert_fusion
  34.1 0.9 collective-permute-done
  35.0 1.5 collective-permute-start.1
  36.5 1.6 %collective-permute-done.1 = f32[16,384]{1,0:T(8,128)S(1)} collective-permute-done((f32[16,384]{1,0:T(8,128)S(1)}, f32[16,384]{1,0:T(8,128)S(1)}, u32[]{:S(2)}, u32[]{:S(2)}) %collective-permute-start.1) | collective-permute-done | bytes 24608 | tf_op jit(solution)/shard_map/ppermute | solution.py:519
  38.1 3.0 %collective-permute-start.2 = (f32[16,384]{1,0:T(8,128)S(1)}, f32[16,384]{1,0:T(8,128)S(1)}, u32[]{:S(2)}, u32[]{:S(2)}) collective-permute-start(f32[16,384]{1,0:T(8,128)S(1)} %add.135), channel_id=1, source_target_pairs={{0,4},{1,5},{2,6},{3,7},{4,0},{5,1},{6,2},{7,3},{8,12},{9,13},{10,... | collective-permute-start | bytes 73736 | tf_op jit(solution)/shard_map/ppermute | solution.py:519
  41.1 1.0 and_reduce_fusion
  42.2 0.1 copy.20
  42.3 0.1 reshape.132.code_ref
  42.4 0.1 collective-permute-done.2
  42.5 0.7 add_add_fusion.latent_ref
  43.2 2.0 %copy-done = bf16[320,5120]{1,0:T(8,128)(2,1)S(1)} copy-done((bf16[320,5120]{1,0:T(8,128)(2,1)S(1)}, bf16[320,5120]{1,0:T(8,128)(2,1)}, u32[]{:S(2)}) %copy-start) | copy-done | bytes 3276824
  45.2 4.2 %hidden.1 = bf16[320,5120]{1,0:T(8,128)(2,1)S(1)} custom-call(f32[16,384]{1,0:T(8,128)S(1)} %add_add_fusion.latent_ref, bf16[16,5120]{1,0:T(8,128)(2,1)S(1)} %copy-done.2, bf16[320,5120]{1,0:T(8,128)(2,1)S(1)} %copy-done, bf16[1,5120]{1,0:T(2,128)(2,1)S(1)} %reshape.130.gain_ref), custom_call_target="tpu_custom_call" | custom-call | tf_op jit(solution)/shard_map/hidden/pallas_call | solution.py:164
  49.4 31.4 %all-gather.2.cloned.1.call-done = bf16[5120,768]{1,0:T(8,128)(2,1)} async-done(((bf16[160,768]{1,0:T(8,128)(2,1)}), bf16[5120,768]{1,0:T(8,128)(2,1)}) %all-gather.2.cloned.1.call-update) | async-done | bytes 7864336 | tf_op jit(solution)/shard_map/all_gather | solution.py:503
  80.7 2.9 %fusion.7.kv_ref.rest_0_ = bf16[320,256]{1,0:T(8,128)(2,1)S(1)} fusion(bf16[320,5120]{1,0:T(8,128)(2,1)S(1)} %hidden.1, bf16[5120,768]{1,0:T(8,128)(2,1)} %all-gather.2.cloned.1.call-done), kind=kOutput, calls=%fused_computation.5 | convolution fusion | flops 838942720 | bytes 6062080 | tf_op jit(solution)/shard_map/dot_general | solution.py:449
  83.7 2.6 %collective-permute-start.6 = (bf16[320,256]{1,0:T(8,128)(2,1)S(1)}, bf16[320,256]{1,0:T(8,128)(2,1)S(1)}, u32[]{:S(2)}, u32[]{:S(2)}) collective-permute-start(bf16[320,256]{1,0:T(8,128)(2,1)S(1)} %fusion.7.kv_ref.rest_0_), channel_id=1, source_target_pairs={{0,48},{8,56},{16,0},{24,8},{32,16},{40,24},{48,32},{56,40},{64,11... | collective-permute-start | bytes 491528 | tf_op jit(solution)/shard_map/ppermute | solution.py:408
  86.2 0.3 collective-permute-start.5
  86.5 0.1 collective-permute-start.4
  86.6 1.8 %fusion.4.own_ref = bf16[320,512]{1,0:T(8,128)(2,1)S(1)} fusion(bf16[320,5120]{1,0:T(8,128)(2,1)S(1)} %hidden.1, bf16[5120,768]{1,0:T(8,128)(2,1)S(1)} %copy-done.5), kind=kOutput, calls=%fused_computation.4 | convolution fusion | flops 1677885440 | bytes 8847360 | tf_op jit(solution)/shard_map/dot_general | solution.py:449
  88.5 1.0 collective-permute-start.3
  89.5 8.1 %collective-permute-done.4.rest_0_.rest_1_ = bf16[320,256]{1,0:T(8,128)(2,1)S(1)} collective-permute-done((bf16[320,256]{1,0:T(8,128)(2,1)S(1)}, bf16[320,256]{1,0:T(8,128)(2,1)S(1)}, u32[]{:S(2)}, u32[]{:S(2)}) %collective-permute-start.4) | collective-permute-done | bytes 163872 | tf_op jit(solution)/shard_map/ppermute | solution.py:408
  97.5 2.1 %collective-permute-start.9 = (bf16[640,256]{1,0:T(8,128)(2,1)S(1)}, bf16[640,256]{1,0:T(8,128)(2,1)S(1)}, u32[]{:S(2)}, u32[]{:S(2)}) collective-permute-start(bf16[640,256]{1,0:T(8,128)(2,1)S(1)} %constant_dynamic-update-slice_fusion), channel_id=1, source_target_pairs={{0,64},{8,72},{16,80},{24,88},{32,96},{40,104},{48,112},{56,120},{... | collective-permute-start | bytes 983048 | tf_op jit(solution)/shard_map/ppermute | solution.py:404
  99.7 1.2 collective-permute-start.8
  100.9 0.2 collective-permute-done.5.rest_1_.rest_2_
  101.1 0.2 collective-permute-start.7
  101.3 1.4 collective-permute-start.11
  102.7 1.4 collective-permute-start.10
  104.1 2.0 %first.1 = (f32[136,2560]{1,0:T(8,128)S(1)}, bf16[2560,128]{1,0:T(8,128)(2,1)S(1)}) custom-call(s32[1]{0:T(128)} %bitcast.1.core_ref, bf16[320,512]{1,0:T(8,128)(2,1)S(1)} %fusion.4.own_ref, bf16[320,512]{1,0:T(8,128)(2,1)S(1)} %collective-permute-done.3.pair_ref, bf16[320,256]{1,0:T(8,128)(2,1)S(1)} %fusion.7.kv_ref.rest_0_), custom_call_target="tpu_custom_call" | custom-call | flops 419430400 | bytes 3145728 | tf_op jit(solution)/shard_map/first/pallas_call | solution.py:248
  106.2 1.3 more.4.state_ref
  107.5 1.5 collective-permute-done.8.rest_2_.rest_5_
  109.0 1.2 collective-permute-start.12
  110.2 7.6 %collective-permute-done.7.rest_1_.rest_6_ = bf16[640,256]{1,0:T(8,128)(2,1)S(1)} collective-permute-done((bf16[640,256]{1,0:T(8,128)(2,1)S(1)}, bf16[640,256]{1,0:T(8,128)(2,1)S(1)}, u32[]{:S(2)}, u32[]{:S(2)}) %collective-permute-start.7) | collective-permute-done | bytes 327712 | tf_op jit(solution)/shard_map/ppermute | solution.py:404
  117.8 9.6 %more.5.state_ref = f32[136,2560]{1,0:T(8,128)S(1)} custom-call(s32[3]{0:T(128)S(1)} %pad_add_fusion.1.flag_ref, bf16[2560,128]{1,0:T(8,128)(2,1)S(1)} %get-tuple-element.28.q_ref, f32[136,2560]{1,0:T(8,128)S(1)} %more.4.state_ref, bf16[640,256]{1,0:T(8,128)(2,1)S(1)} %collective-permute-done.9.rest_0_.rest_4_, ...), custom_call_target="tpu_custom_call" | custom-call | flops 2516582400 | bytes 3145728 | tf_op jit(solution)/shard_map/more/pallas_call | solution.py:300
  127.4 6.6 %more.6.state_ref = f32[136,2560]{1,0:T(8,128)S(1)} custom-call(s32[2]{0:T(128)S(1)} %pad_add_fusion.flag_ref, bf16[2560,128]{1,0:T(8,128)(2,1)S(1)} %get-tuple-element.28.q_ref, f32[136,2560]{1,0:T(8,128)S(1)} %more.5.state_ref, bf16[640,256]{1,0:T(8,128)(2,1)S(1)} %collective-permute-done.10.rest_0_.rest_7_, ...), custom_call_target="tpu_custom_call" | custom-call | flops 1677721600 | bytes 3145728 | tf_op jit(solution)/shard_map/more/pallas_call | solution.py:300
  134.1 3.1 %more.7 = (f32[136,1280]{1,0:T(8,128)S(1)}, f32[136,1280]{1,0:T(8,128)S(1)}) custom-call(s32[1]{0:T(128)} %bitcast.flag_ref, bf16[2560,128]{1,0:T(8,128)(2,1)S(1)} %get-tuple-element.28.q_ref, f32[136,2560]{1,0:T(8,128)S(1)} %more.6.state_ref, bf16[640,256]{1,0:T(8,128)(2,1)S(1)} %collective-permute-done.12.rest_0_.rest_8_), custom_call_target="tpu_custom_call" | custom-call | flops 838860800 | bytes 3145728 | tf_op jit(solution)/shard_map/more/pallas_call | solution.py:300
  137.2 1.3 collective-permute-start.13
  138.5 0.1 pad_add_fusion.2.place_ref
  138.6 3.1 %pages.1 = (bf16[320,256]{1,0:T(8,128)(2,1)S(1)}, bf16[320,256]{1,0:T(8,128)(2,1)S(1)}) custom-call(s32[3]{0:T(128)S(1)} %pad_add_fusion.2.place_ref, s32[192]{0:T(256)S(1)} %reshape.132.code_ref, bf16[320,256]{1,0:T(8,128)(2,1)S(1)} %fusion.7.kv_ref.rest_0_, bf16[320,256]{1,0:T(8,128)(2,1)S(1)} %collective-permute-done.4.rest_0_.rest_1_, ...), custom_call_target="tpu_custom_call" | custom-call | tf_op jit(solution)/shard_map/pages/pallas_call | solution.py:378
  141.7 0.1 collective-permute-start.14
  141.8 1.4 collective-permute-done.14
  143.2 0.9 broadcast_select_fusion
  144.1 1.0 finish.1
  (33 shorter events, 0.2 us)
Async XLA Ops:
  7.2 36.1 %copy-start.2 = (bf16[16,5120]{1,0:T(8,128)(2,1)S(1)}, bf16[16,5120]{1,0:T(8,128)(2,1)}, u32[]{:S(2)}) copy-start(bf16[16,5120]{1,0:T(8,128)(2,1)} %embed_ref.1) | copy-start | bytes 491524
  7.2 73.6 %all-gather.2.cloned.1.call-start = ((), (), s32[]{:S(2)}) async-start(), calls=%async_computation.1 | async-start | bytes 8110080 | tf_op jit(solution)/shard_map/all_gather | solution.py:503
  7.9 1.0 copy-start.1
  8.9 0.8 copy-start.3
  11.8 14.9 %all-to-all-start = ((f32[32,1,512]{2,1,0:T(1,128)}), f32[32,1,512]{2,1,0:T(1,128)S(1)}, u32[]{:S(2)}, u32[]{:S(2)}) async-start(f32[32,1,512]{2,1,0:T(1,128)} %all_to_all.8), calls=%async_computation | async-start | bytes 131072 | tf_op jit(solution)/shard_map/all_to_all | solution.py:511
  26.9 0.7 copy-start.4
  28.3 6.7 %collective-permute-start = (f32[16,384]{1,0:T(8,128)S(1)}, f32[16,384]{1,0:T(8,128)S(1)}, u32[]{:S(2)}, u32[]{:S(2)}) collective-permute-start(f32[16,384]{1,0:T(8,128)S(1)} %place.1), channel_id=1, source_target_pairs={{0,1},{1,0},{2,3},{3,2},{4,5},{5,4},{6,7},{7,6},{8,9},{9,8},{10,11... | collective-permute-start | bytes 73736 | tf_op jit(solution)/shard_map/ppermute | solution.py:519
  35.0 3.1 %collective-permute-start.1 = (f32[16,384]{1,0:T(8,128)S(1)}, f32[16,384]{1,0:T(8,128)S(1)}, u32[]{:S(2)}, u32[]{:S(2)}) collective-permute-start(f32[16,384]{1,0:T(8,128)S(1)} %add.134), channel_id=1, source_target_pairs={{0,2},{1,3},{2,0},{3,1},{4,6},{5,7},{6,4},{7,5},{8,10},{9,11},{10,... | collective-permute-start | bytes 73736 | tf_op jit(solution)/shard_map/ppermute | solution.py:519
  38.1 4.3 %collective-permute-start.2 = (f32[16,384]{1,0:T(8,128)S(1)}, f32[16,384]{1,0:T(8,128)S(1)}, u32[]{:S(2)}, u32[]{:S(2)}) collective-permute-start(f32[16,384]{1,0:T(8,128)S(1)} %add.135), channel_id=1, source_target_pairs={{0,4},{1,5},{2,6},{3,7},{4,0},{5,1},{6,2},{7,3},{8,12},{9,13},{10,... | collective-permute-start | bytes 73736 | tf_op jit(solution)/shard_map/ppermute | solution.py:519
  43.2 2.0 %copy-start = (bf16[320,5120]{1,0:T(8,128)(2,1)S(1)}, bf16[320,5120]{1,0:T(8,128)(2,1)}, u32[]{:S(2)}) copy-start(bf16[320,5120]{1,0:T(8,128)(2,1)} %table_ref.1) | copy-start | bytes 9830404
  80.7 5.9 %copy-start.5 = (bf16[5120,768]{1,0:T(8,128)(2,1)S(1)}, bf16[5120,768]{1,0:T(8,128)(2,1)}, u32[]{:S(2)}) copy-start(bf16[5120,768]{1,0:T(8,128)(2,1)} %all-gather.2.cloned.1.call-done) | copy-start | bytes 23592964
  83.7 17.7 %collective-permute-start.6 = (bf16[320,256]{1,0:T(8,128)(2,1)S(1)}, bf16[320,256]{1,0:T(8,128)(2,1)S(1)}, u32[]{:S(2)}, u32[]{:S(2)}) collective-permute-start(bf16[320,256]{1,0:T(8,128)(2,1)S(1)} %fusion.7.kv_ref.rest_0_), channel_id=1, source_target_pairs={{0,48},{8,56},{16,0},{24,8},{32,16},{40,24},{48,32},{56,40},{64,11... | collective-permute-start | bytes 491528 | tf_op jit(solution)/shard_map/ppermute | solution.py:408
  86.2 14.9 %collective-permute-start.5 = (bf16[320,256]{1,0:T(8,128)(2,1)S(1)}, bf16[320,256]{1,0:T(8,128)(2,1)S(1)}, u32[]{:S(2)}, u32[]{:S(2)}) collective-permute-start(bf16[320,256]{1,0:T(8,128)(2,1)S(1)} %fusion.7.kv_ref.rest_0_), channel_id=1, source_target_pairs={{0,32},{8,40},{16,48},{24,56},{32,0},{40,8},{48,16},{56,24},{64,96... | collective-permute-start | bytes 491528 | tf_op jit(solution)/shard_map/ppermute | solution.py:408
  86.5 11.0 %collective-permute-start.4 = (bf16[320,256]{1,0:T(8,128)(2,1)S(1)}, bf16[320,256]{1,0:T(8,128)(2,1)S(1)}, u32[]{:S(2)}, u32[]{:S(2)}) collective-permute-start(bf16[320,256]{1,0:T(8,128)(2,1)S(1)} %fusion.7.kv_ref.rest_0_), channel_id=1, source_target_pairs={{0,16},{8,24},{16,32},{24,40},{32,48},{40,56},{48,0},{56,8},{64,80... | collective-permute-start | bytes 491528 | tf_op jit(solution)/shard_map/ppermute | solution.py:408
  88.5 14.2 %collective-permute-start.3 = (bf16[320,512]{1,0:T(8,128)(2,1)S(1)}, bf16[320,512]{1,0:T(8,128)(2,1)S(1)}, u32[]{:S(2)}, u32[]{:S(2)}) collective-permute-start(bf16[320,512]{1,0:T(8,128)(2,1)S(1)} %fusion.4.own_ref), channel_id=1, source_target_pairs={{0,8},{8,0},{16,24},{24,16},{32,40},{40,32},{48,56},{56,48},{64,72... | collective-permute-start | bytes 983048 | tf_op jit(solution)/shard_map/ppermute | solution.py:412
  97.5 20.3 %collective-permute-start.9 = (bf16[640,256]{1,0:T(8,128)(2,1)S(1)}, bf16[640,256]{1,0:T(8,128)(2,1)S(1)}, u32[]{:S(2)}, u32[]{:S(2)}) collective-permute-start(bf16[640,256]{1,0:T(8,128)(2,1)S(1)} %constant_dynamic-update-slice_fusion), channel_id=1, source_target_pairs={{0,64},{8,72},{16,80},{24,88},{32,96},{40,104},{48,112},{56,120},{... | collective-permute-start | bytes 983048 | tf_op jit(solution)/shard_map/ppermute | solution.py:404
  99.7 9.3 %collective-permute-start.8 = (bf16[640,256]{1,0:T(8,128)(2,1)S(1)}, bf16[640,256]{1,0:T(8,128)(2,1)S(1)}, u32[]{:S(2)}, u32[]{:S(2)}) collective-permute-start(bf16[640,256]{1,0:T(8,128)(2,1)S(1)} %constant_dynamic-update-slice_fusion), channel_id=1, source_target_pairs={{0,128},{8,136},{16,144},{24,152},{32,160},{40,168},{48,176},{56,1... | collective-permute-start | bytes 983048 | tf_op jit(solution)/shard_map/ppermute | solution.py:404
  101.1 16.7 %collective-permute-start.7 = (bf16[640,256]{1,0:T(8,128)(2,1)S(1)}, bf16[640,256]{1,0:T(8,128)(2,1)S(1)}, u32[]{:S(2)}, u32[]{:S(2)}) collective-permute-start(bf16[640,256]{1,0:T(8,128)(2,1)S(1)} %constant_dynamic-update-slice_fusion), channel_id=1, source_target_pairs={{0,192},{8,200},{16,208},{24,216},{32,224},{40,232},{48,240},{56,2... | collective-permute-start | bytes 983048 | tf_op jit(solution)/shard_map/ppermute | solution.py:404
  101.3 26.1 %collective-permute-start.11 = (bf16[640,256]{1,0:T(8,128)(2,1)S(1)}, bf16[640,256]{1,0:T(8,128)(2,1)S(1)}, u32[]{:S(2)}, u32[]{:S(2)}) collective-permute-start(bf16[640,256]{1,0:T(8,128)(2,1)S(1)} %constant_dynamic-update-slice_fusion.2), channel_id=1, source_target_pairs={{0,192},{8,200},{16,208},{24,216},{32,224},{40,232},{48,240},{56,2... | collective-permute-start | bytes 983048 | tf_op jit(solution)/shard_map/ppermute | solution.py:404
  102.7 24.7 %collective-permute-start.10 = (bf16[640,256]{1,0:T(8,128)(2,1)S(1)}, bf16[640,256]{1,0:T(8,128)(2,1)S(1)}, u32[]{:S(2)}, u32[]{:S(2)}) collective-permute-start(bf16[640,256]{1,0:T(8,128)(2,1)S(1)} %constant_dynamic-update-slice_fusion.2), channel_id=1, source_target_pairs={{0,64},{8,72},{16,80},{24,88},{32,96},{40,104},{48,112},{56,120},{... | collective-permute-start | bytes 983048 | tf_op jit(solution)/shard_map/ppermute | solution.py:404
  109.0 25.1 %collective-permute-start.12 = (bf16[640,256]{1,0:T(8,128)(2,1)S(1)}, bf16[640,256]{1,0:T(8,128)(2,1)S(1)}, u32[]{:S(2)}, u32[]{:S(2)}) collective-permute-start(bf16[640,256]{1,0:T(8,128)(2,1)S(1)} %constant_dynamic-update-slice_fusion.2), channel_id=1, source_target_pairs={{0,128},{8,136},{16,144},{24,152},{32,160},{40,168},{48,176},{56,1... | collective-permute-start | bytes 983048 | tf_op jit(solution)/shard_map/ppermute | solution.py:404
  137.2 7.0 %collective-permute-start.13 = (f32[136,1280]{1,0:T(8,128)S(1)}, f32[136,1280]{1,0:T(8,128)S(1)}, u32[]{:S(2)}, u32[]{:S(2)}) collective-permute-start(f32[136,1280]{1,0:T(8,128)S(1)} %get-tuple-element.39), channel_id=1, source_target_pairs={{0,8},{8,0},{16,24},{24,16},{32,40},{40,32},{48,56},{56,48},{64,72... | collective-permute-start | bytes 2088968 | tf_op jit(solution)/shard_map/ppermute | solution.py:412
  141.7 1.5 collective-permute-start.14
Sparse Core Ops, SparseCore 0:
  9.9 70.8 all-gather.1

commit v8 on v7

--- a/solution.py
+++ b/solution.py
@@ -355,7 +355,7 @@
             if by_y == 0:
                 array, base = arrays[by_z], 0
             else:
-                array, base = arrays[3 + by_y + by_z // 2 * 3], by_z % 2 * BLK
+                array, base = arrays[3 + by_y + (0, 3, 6, 3)[by_z]], by_z // 3 * BLK
             source = (((y - by_y) & 3) * 4 + ((z - by_z) & 3)) * 2 + core
             for entry in range(2 * MOST):
                 code = code_ref[source * 2 * MOST + entry]
@@ -433,18 +433,6 @@
     return jnp.any(match, axis=(1, 2))
 
 
-def spread(value, groups):
-    by_z = {0: value}
-    for count in (1, 2, 3):
-        by_z[count] = along_z(value, count)
-    by_y = []
-    for group in groups:
-        parts = [by_z[count] for count in group]
-        parts = jnp.concatenate(parts, axis=0) if len(parts) > 1 else parts[0]
-        by_y.append({count: along_y(parts, count) for count in (1, 3, 2)})
-    return by_z, by_y
-
-
 def project(normed, weight):
     return jnp.dot(normed, weight, preferred_element_type=jnp.float32).astype(jnp.bfloat16)
 
@@ -453,7 +441,8 @@
     core, z, y = me % 2, (me // 2) % 4, me // 8
     kv = project(normed, weight[:, GROUP * HD :])
     normed, kv = lax.optimization_barrier((normed, kv))
-    by_z, (near, far) = spread(kv, ((0, 1), (2, 3)))
+    by_z = {0: kv, 1: along_z(kv, 1), 3: along_z(kv, 3)}
+    none = {count: along_y(kv, count) for count in (1, 3, 2)}
     own_queries = project(normed, weight[:, : GROUP * HD])
     pair_queries = other_core(own_queries)
 
@@ -461,21 +450,28 @@
         return jnp.stack([jnp.asarray(value, jnp.int32) for value in conditions])
 
     state, queries = attend_first(core, own_queries, pair_queries, kv)
+    state, by_z[1], by_z[3] = lax.optimization_barrier((state, by_z[1], by_z[3]))
+    kv, odd = lax.optimization_barrier((kv, jnp.concatenate([by_z[1], by_z[3]], axis=0)))
+    by_z[2] = along_z(kv, 2)
+    odd = {count: along_y(odd, count) for count in (1, 3, 2)}
     state = attend_more(
-        flag(z >= 1, z >= 2, z >= 3), queries, state, [by_z[1], by_z[2], by_z[3]]
+        flag(y >= 1, y >= 3, y >= 2), queries, state, [none[1], none[3], none[2]]
     )
-    state, near[3], near[2] = lax.optimization_barrier((state, near[3], near[2]))
+    state, by_z[2] = lax.optimization_barrier((state, by_z[2]))
+    two = {count: along_y(by_z[2], count) for count in (1, 3, 2)}
     state = attend_more(
-        flag(y >= 1, y >= 3, y >= 2), queries, state, [near[1], near[3], near[2]]
+        flag(z >= 1, z >= 3, z >= 2), queries, state, [by_z[1], by_z[3], by_z[2]]
     )
-    state, far[1], far[3] = lax.optimization_barrier((state, far[1], far[3]))
-    state = attend_more(flag(y >= 1, y >= 3), queries, state, [far[1], far[3]])
-    state, far[2] = lax.optimization_barrier((state, far[2]))
-    own, sent = attend_more(flag(y >= 2), queries, state, [far[2]], split=True)
+    state, odd[1], odd[3], odd[2] = lax.optimization_barrier((state, odd[1], odd[3], odd[2]))
+    state = attend_more(flag(y >= 1, y >= 3, y >= 2), queries, state, [odd[1], odd[3], odd[2]])
+    state, two[1], two[3], two[2] = lax.optimization_barrier((state, two[1], two[3], two[2]))
+    own, sent = attend_more(
+        flag(y >= 1, y >= 3, y >= 2), queries, state, [two[1], two[3], two[2]], split=True
+    )
     got = other_core(sent)
 
     arrays = [by_z[count] for count in range(4)]
-    arrays += [group[count] for group in (near, far) for count in (1, 2, 3)]
+    arrays += [group[count] for group in (none, odd, two) for count in (1, 2, 3)]
     place = jnp.stack([y, z, core])
     own_pages, sent_pages = fetch_pages(place, codes, arrays)
     got_pages = other_core(sent_pages)

time: 155 us -> 153 us (0.987)
  waiting for transfers between devices: 58 us -> 42 us
  starting transfers between devices: 30.9 us -> 37 us
  Pallas kernels: 32.2 us -> 37.1 us
  local copies, waits for them, and re-layouts: 6.47 us -> 8.44 us
    ppermute x6 -> x9, waiting for transfers between devices: 9.11 us -> 0.02 us  [along_y(): lax.ppermute(value, 'seq', moves(lambda y, z, c: ((y + count) % 4, z, c)))]
    ppermute x3, waiting for transfers between devices: 8.26 us -> 1.51 us  [along_z(): lax.ppermute(value, 'seq', moves(lambda y, z, c: (y, (z + count) % 4, c)))]
    ppermute x6 -> x9, starting transfers between devices: 7.54 us -> 12.1 us  [along_y(): lax.ppermute(value, 'seq', moves(lambda y, z, c: ((y + count) % 4, z, c)))]
    pallas_call x4, Pallas kernels: 20.6 us -> 23.7 us  [attend_more(): pl.pallas_call(functools.partial(more_kernel, count, split), in_specs=[pl...]
    unnamed x15 -> x13, local copies, waits for them, and re-layouts: 4.47 us -> 6.46 us
    ppermute x3, starting transfers between devices: 2.94 us -> 4.7 us  [along_z(): lax.ppermute(value, 'seq', moves(lambda y, z, c: (y, (z + count) % 4, c)))]
  transfers between devices with their start and end apart: 17 -> 20, of which waited for: 10 -> 8; matrix products, arithmetic and copies ran while one was open for 6% -> 4% of each run, Pallas kernels for 18% -> 20%
where the time goes in v8:
time: 153 us; the launch traced here: 150 us
  waiting for transfers between devices  42 us (27%)
  Pallas kernels  37.1 us (24%)
  starting transfers between devices  37 us (24%)
  between operations  14.3 us (9%)
  local copies, waits for them, and re-layouts  8.44 us (6%)
  matrix products  5.57 us (4%)
  other arithmetic  5.22 us (3%)
    all_gather x1, waiting for transfers between devices, on_device(): weight = lax.all_gather(qkv_weight, 'seq', axis=0, tiled=True)  30.2 us
    pallas_call x4, Pallas kernels, attend_more(): pl.pallas_call(functools.partial(more_kernel, count, split), in_specs=[pl...  23.7 us
    ppermute x9, starting transfers between devices, along_y(): lax.ppermute(value, 'seq', moves(lambda y, z, c: ((y + count) % 4, z, c)))  12.1 us
    all_to_all x1, starting transfers between devices, on_device(): lax.all_to_all(message, 'seq', split_axis=0, concat_axis=0, tiled=True)  9.26 us
    ppermute x3, starting transfers between devices, on_device(): latent = latent + lax.ppermute(latent, 'tensor', swap)  8.17 us
    unnamed x13, local copies, waits for them, and re-layouts  6.46 us
    dot_general x2, matrix products, project(): jnp.dot(normed, weight, preferred_element_type=jnp.float32)  5.57 us
    all_to_all x1, waiting for transfers between devices, on_device(): lax.all_to_all(message, 'seq', split_axis=0, concat_axis=0, tiled=True)  4.85 us
  transfers between devices with their start and end apart: 20, of which 8 were waited for; matrix products, arithmetic and copies ran while one was open for 4% of the time, Pallas kernels for 20%

profile of v8, /device:TPU:25, one launch (start us, length us, event | category | flops | bytes accessed | tf_op | source)
XLA Modules:
  0.0 149.7 jit_solution(10222770524563973676)
XLA Ops:
  7.2 0.0 all-gather.2.cloned.1.call-start
  7.2 0.7 all-gather.2.cloned.1.call-update
  7.9 1.0 copy-done.1
  8.9 0.8 copy-done.3
  9.7 0.5 conv.1
  10.2 0.1 reshape.129
  10.3 0.7 add_convert_fusion.2
  11.0 0.1 pad.14.clone
  11.1 0.7 all_to_all.8
  11.8 9.3 %all-to-all-start = ((f32[32,1,512]{2,1,0:T(1,128)}), f32[32,1,512]{2,1,0:T(1,128)S(1)}, u32[]{:S(2)}, u32[]{:S(2)}) async-start(f32[32,1,512]{2,1,0:T(1,128)} %all_to_all.8), calls=%async_computation | async-start | bytes 131072 | tf_op jit(solution)/shard_map/all_to_all | solution.py:507
  21.1 0.7 reshape.130.gain_ref
  21.9 4.9 %all-to-all-done = f32[32,1,512]{2,1,0:T(1,128)S(1)} async-done(((f32[32,1,512]{2,1,0:T(1,128)}), f32[32,1,512]{2,1,0:T(1,128)S(1)}, u32[]{:S(2)}, u32[]{:S(2)}) %all-to-all-start) | async-done | bytes 65568 | tf_op jit(solution)/shard_map/all_to_all | solution.py:507
  26.8 0.2 reshape.131.parts_ref
  26.9 0.7 copy-done.4
  27.6 0.7 place.1
  28.3 4.2 %collective-permute-start = (f32[16,384]{1,0:T(8,128)S(1)}, f32[16,384]{1,0:T(8,128)S(1)}, u32[]{:S(2)}, u32[]{:S(2)}) collective-permute-start(f32[16,384]{1,0:T(8,128)S(1)} %place.1), channel_id=1, source_target_pairs={{0,1},{1,0},{2,3},{3,2},{4,5},{5,4},{6,7},{7,6},{8,9},{9,8},{10,11... | collective-permute-start | bytes 73736 | tf_op jit(solution)/shard_map/ppermute | solution.py:515
  32.5 0.1 compare_and_fusion.1
  32.6 1.2 convert_reduce_fusion
  33.8 0.3 select_reduce_fusion
  34.0 0.1 slice_convert_fusion
  34.1 1.2 collective-permute-done
  35.3 1.2 collective-permute-start.1
  36.5 1.9 %collective-permute-done.1 = f32[16,384]{1,0:T(8,128)S(1)} collective-permute-done((f32[16,384]{1,0:T(8,128)S(1)}, f32[16,384]{1,0:T(8,128)S(1)}, u32[]{:S(2)}, u32[]{:S(2)}) %collective-permute-start.1) | collective-permute-done | bytes 24608 | tf_op jit(solution)/shard_map/ppermute | solution.py:515
  38.4 2.8 %collective-permute-start.2 = (f32[16,384]{1,0:T(8,128)S(1)}, f32[16,384]{1,0:T(8,128)S(1)}, u32[]{:S(2)}, u32[]{:S(2)}) collective-permute-start(f32[16,384]{1,0:T(8,128)S(1)} %add.135), channel_id=1, source_target_pairs={{0,4},{1,5},{2,6},{3,7},{4,0},{5,1},{6,2},{7,3},{8,12},{9,13},{10,... | collective-permute-start | bytes 73736 | tf_op jit(solution)/shard_map/ppermute | solution.py:515
  41.1 1.0 and_reduce_fusion
  42.2 0.1 copy.20
  42.3 0.1 reshape.132.code_ref
  42.4 0.4 collective-permute-done.2
  42.7 0.7 add_add_fusion.latent_ref
  43.5 2.0 %copy-done = bf16[320,5120]{1,0:T(8,128)(2,1)S(1)} copy-done((bf16[320,5120]{1,0:T(8,128)(2,1)S(1)}, bf16[320,5120]{1,0:T(8,128)(2,1)}, u32[]{:S(2)}) %copy-start) | copy-done | bytes 3276824
  45.5 0.9 copy-done.2
  46.4 4.2 %hidden.1 = bf16[320,5120]{1,0:T(8,128)(2,1)S(1)} custom-call(f32[16,384]{1,0:T(8,128)S(1)} %add_add_fusion.latent_ref, bf16[16,5120]{1,0:T(8,128)(2,1)S(1)} %copy-done.2, bf16[320,5120]{1,0:T(8,128)(2,1)S(1)} %copy-done, bf16[1,5120]{1,0:T(2,128)(2,1)S(1)} %reshape.130.gain_ref), custom_call_target="tpu_custom_call" | custom-call | tf_op jit(solution)/shard_map/hidden/pallas_call | solution.py:164
  50.6 30.2 %all-gather.2.cloned.1.call-done = bf16[5120,768]{1,0:T(8,128)(2,1)} async-done(((bf16[160,768]{1,0:T(8,128)(2,1)}), bf16[5120,768]{1,0:T(8,128)(2,1)}) %all-gather.2.cloned.1.call-update) | async-done | bytes 7864336 | tf_op jit(solution)/shard_map/all_gather | solution.py:499
  80.8 2.9 %fusion.7.kv_ref.rest_0_ = bf16[320,256]{1,0:T(8,128)(2,1)S(1)} fusion(bf16[320,5120]{1,0:T(8,128)(2,1)S(1)} %hidden.1, bf16[5120,768]{1,0:T(8,128)(2,1)} %all-gather.2.cloned.1.call-done), kind=kOutput, calls=%fused_computation.5 | convolution fusion | flops 838942720 | bytes 6062080 | tf_op jit(solution)/shard_map/dot_general | solution.py:437
  83.7 1.1 copy-done.5
  84.8 2.6 %fusion.4.own_ref = bf16[320,512]{1,0:T(8,128)(2,1)} fusion(bf16[320,5120]{1,0:T(8,128)(2,1)S(1)} %hidden.1, bf16[5120,768]{1,0:T(8,128)(2,1)S(1)} %copy-done.5), kind=kOutput, calls=%fused_computation.4 | convolution fusion | flops 1677885440 | bytes 8847360 | tf_op jit(solution)/shard_map/dot_general | solution.py:437
  87.4 0.3 collective-permute-start.3
  87.7 2.4 %collective-permute-start.5 = (bf16[320,256]{1,0:T(8,128)(2,1)S(1)}, bf16[320,256]{1,0:T(8,128)(2,1)S(1)}, u32[]{:S(2)}, u32[]{:S(2)}) collective-permute-start(bf16[320,256]{1,0:T(8,128)(2,1)S(1)} %fusion.7.kv_ref.rest_0_), channel_id=1, source_target_pairs={{0,48},{8,56},{16,0},{24,8},{32,16},{40,24},{48,32},{56,40},{64,11... | collective-permute-start | bytes 491528 | tf_op jit(solution)/shard_map/ppermute | solution.py:408
  90.1 1.3 collective-permute-start.8
  91.4 0.5 collective-permute-start.7
  91.9 0.1 add_convert_fusion.flag_ref
  92.0 2.3 %collective-permute-start.6 = (bf16[320,256]{1,0:T(8,128)(2,1)S(1)}, bf16[320,256]{1,0:T(8,128)(2,1)S(1)}, u32[]{:S(2)}, u32[]{:S(2)}) collective-permute-start(bf16[320,256]{1,0:T(8,128)(2,1)S(1)} %fusion.7.kv_ref.rest_0_), channel_id=1, source_target_pairs={{0,64},{8,72},{16,80},{24,88},{32,96},{40,104},{48,112},{56,120},{... | collective-permute-start | bytes 491528 | tf_op jit(solution)/shard_map/ppermute | solution.py:404
  94.2 3.0 %first.1 = (f32[136,2560]{1,0:T(8,128)S(1)}, bf16[2560,128]{1,0:T(8,128)(2,1)S(1)}) custom-call(s32[1]{0:T(128)} %bitcast.3.core_ref, bf16[320,512]{1,0:T(8,128)(2,1)} %fusion.4.own_ref, bf16[320,512]{1,0:T(8,128)(2,1)S(1)} %collective-permute-done.3.pair_ref, bf16[320,256]{1,0:T(8,128)(2,1)S(1)} %fusion.7.kv_ref.rest_0_), custom_call_target="tpu_custom_call" | custom-call | flops 419430400 | bytes 3145728 | tf_op jit(solution)/shard_map/first/pallas_call | solution.py:248
  97.2 0.5 collective-permute-done.4.rest_0_.rest_1_
  97.8 1.9 %collective-permute-start.12 = (bf16[640,256]{1,0:T(8,128)(2,1)S(1)}, bf16[640,256]{1,0:T(8,128)(2,1)S(1)}, u32[]{:S(2)}, u32[]{:S(2)}) collective-permute-start(bf16[640,256]{1,0:T(8,128)(2,1)S(1)} %pad_maximum_fusion), channel_id=1, source_target_pairs={{0,128},{8,136},{16,144},{24,152},{32,160},{40,168},{48,176},{56,1... | collective-permute-start | bytes 983048 | tf_op jit(solution)/shard_map/ppermute | solution.py:404
  99.6 0.9 collective-permute-start.11
  100.5 1.8 %collective-permute-start.10 = (bf16[640,256]{1,0:T(8,128)(2,1)S(1)}, bf16[640,256]{1,0:T(8,128)(2,1)S(1)}, u32[]{:S(2)}, u32[]{:S(2)}) collective-permute-start(bf16[640,256]{1,0:T(8,128)(2,1)S(1)} %pad_maximum_fusion), channel_id=1, source_target_pairs={{0,64},{8,72},{16,80},{24,88},{32,96},{40,104},{48,112},{56,120},{... | collective-permute-start | bytes 983048 | tf_op jit(solution)/shard_map/ppermute | solution.py:404
  102.3 2.3 %collective-permute-start.9 = (bf16[320,256]{1,0:T(8,128)(2,1)S(1)}, bf16[320,256]{1,0:T(8,128)(2,1)S(1)}, u32[]{:S(2)}, u32[]{:S(2)}) collective-permute-start(bf16[320,256]{1,0:T(8,128)(2,1)S(1)} %fusion.7.kv_ref.rest_0_), channel_id=1, source_target_pairs={{0,32},{8,40},{16,48},{24,56},{32,0},{40,8},{48,16},{56,24},{64,96... | collective-permute-start | bytes 491528 | tf_op jit(solution)/shard_map/ppermute | solution.py:408
  104.6 0.1 add_convert_fusion.1.flag_ref
  104.7 6.3 %more.4.state_ref = f32[136,2560]{1,0:T(8,128)S(1)} custom-call(s32[3]{0:T(128)S(1)} %add_convert_fusion.flag_ref, bf16[2560,128]{1,0:T(8,128)(2,1)S(1)} %get-tuple-element.35.q_ref, f32[136,2560]{1,0:T(8,128)S(1)} %get-tuple-element.37.state_ref, bf16[320,256]{1,0:T(8,128)(2,1)S(1)} %collective-permute-done.6.rest_0_.rest_4_, ...), custom_call_target="tpu_custom_call" | custom-call | flops 1258291200 | bytes 3145728 | tf_op jit(solution)/shard_map/more/pallas_call | solution.py:300
  111.0 1.0 collective-permute-done.9.rest_2_
  112.0 0.6 collective-permute-start.15
  112.7 1.3 collective-permute-start.14
  114.0 1.3 more.5.state_ref
  115.3 1.6 %collective-permute-start.13 = (bf16[320,256]{1,0:T(8,128)(2,1)S(1)}, bf16[320,256]{1,0:T(8,128)(2,1)S(1)}, u32[]{:S(2)}, u32[]{:S(2)}) collective-permute-start(bf16[320,256]{1,0:T(8,128)(2,1)S(1)} %collective-permute-done.9.rest_2_), channel_id=1, source_target_pairs={{0,64},{8,72},{16,80},{24,88},{32,96},{40,104},{48,112},{56,120},{... | collective-permute-start | bytes 491528 | tf_op jit(solution)/shard_map/ppermute | solution.py:404
  117.0 9.6 %more.6.state_ref = f32[136,2560]{1,0:T(8,128)S(1)} custom-call(s32[3]{0:T(128)S(1)} %add_convert_fusion.flag_ref, bf16[2560,128]{1,0:T(8,128)(2,1)S(1)} %get-tuple-element.35.q_ref, f32[136,2560]{1,0:T(8,128)S(1)} %more.5.state_ref, bf16[640,256]{1,0:T(8,128)(2,1)S(1)} %collective-permute-done.10.rest_0_.rest_7_, ...), custom_call_target="tpu_custom_call" | custom-call | flops 2516582400 | bytes 3145728 | tf_op jit(solution)/shard_map/more/pallas_call | solution.py:300
  126.6 6.4 %more.7 = (f32[136,1280]{1,0:T(8,128)S(1)}, f32[136,1280]{1,0:T(8,128)S(1)}) custom-call(s32[3]{0:T(128)S(1)} %add_convert_fusion.flag_ref, bf16[2560,128]{1,0:T(8,128)(2,1)S(1)} %get-tuple-element.35.q_ref, f32[136,2560]{1,0:T(8,128)S(1)} %more.6.state_ref, bf16[320,256]{1,0:T(8,128)(2,1)S(1)} %collective-permute-done.13.rest_0_.rest_10_, ...), custom_call_target="tpu_custom_call" | custom-call | flops 1258291200 | bytes 3145728 | tf_op jit(solution)/shard_map/more/pallas_call | solution.py:300
  133.0 2.3 %collective-permute-start.16 = (f32[136,1280]{1,0:T(8,128)S(1)}, f32[136,1280]{1,0:T(8,128)S(1)}, u32[]{:S(2)}, u32[]{:S(2)}) collective-permute-start(f32[136,1280]{1,0:T(8,128)S(1)} %get-tuple-element.53), channel_id=1, source_target_pairs={{0,8},{8,0},{16,24},{24,16},{32,40},{40,32},{48,56},{56,48},{64,72... | collective-permute-start | bytes 2088968 | tf_op jit(solution)/shard_map/ppermute | solution.py:412
  135.3 0.1 pad_add_fusion.place_ref
  135.4 4.1 %pages.1 = (bf16[320,256]{1,0:T(8,128)(2,1)S(1)}, bf16[320,256]{1,0:T(8,128)(2,1)S(1)}) custom-call(s32[3]{0:T(128)S(1)} %pad_add_fusion.place_ref, s32[192]{0:T(256)S(1)} %reshape.132.code_ref, bf16[320,256]{1,0:T(8,128)(2,1)S(1)} %fusion.7.kv_ref.rest_0_, bf16[320,256]{1,0:T(8,128)(2,1)S(1)} %collective-permute-done.4.rest_0_.rest_1_, ...), custom_call_target="tpu_custom_call" | custom-call | tf_op jit(solution)/shard_map/pages/pallas_call | solution.py:378
  139.5 0.1 collective-permute-start.17
  139.6 1.4 collective-permute-done.17
  141.0 0.9 broadcast_select_fusion
  141.9 1.0 finish.1
  (35 shorter events, 0.2 us)
Async XLA Ops:
  7.2 73.6 %all-gather.2.cloned.1.call-start = ((), (), s32[]{:S(2)}) async-start(), calls=%async_computation.1 | async-start | bytes 8110080 | tf_op jit(solution)/shard_map/all_gather | solution.py:499
  7.9 1.0 copy-start.1
  8.9 0.8 copy-start.3
  11.8 14.9 %all-to-all-start = ((f32[32,1,512]{2,1,0:T(1,128)}), f32[32,1,512]{2,1,0:T(1,128)S(1)}, u32[]{:S(2)}, u32[]{:S(2)}) async-start(f32[32,1,512]{2,1,0:T(1,128)} %all_to_all.8), calls=%async_computation | async-start | bytes 131072 | tf_op jit(solution)/shard_map/all_to_all | solution.py:507
  26.9 0.7 copy-start.4
  28.3 7.0 %collective-permute-start = (f32[16,384]{1,0:T(8,128)S(1)}, f32[16,384]{1,0:T(8,128)S(1)}, u32[]{:S(2)}, u32[]{:S(2)}) collective-permute-start(f32[16,384]{1,0:T(8,128)S(1)} %place.1), channel_id=1, source_target_pairs={{0,1},{1,0},{2,3},{3,2},{4,5},{5,4},{6,7},{7,6},{8,9},{9,8},{10,11... | collective-permute-start | bytes 73736 | tf_op jit(solution)/shard_map/ppermute | solution.py:515
  35.3 3.1 %collective-permute-start.1 = (f32[16,384]{1,0:T(8,128)S(1)}, f32[16,384]{1,0:T(8,128)S(1)}, u32[]{:S(2)}, u32[]{:S(2)}) collective-permute-start(f32[16,384]{1,0:T(8,128)S(1)} %add.134), channel_id=1, source_target_pairs={{0,2},{1,3},{2,0},{3,1},{4,6},{5,7},{6,4},{7,5},{8,10},{9,11},{10,... | collective-permute-start | bytes 73736 | tf_op jit(solution)/shard_map/ppermute | solution.py:515
  38.4 4.4 %collective-permute-start.2 = (f32[16,384]{1,0:T(8,128)S(1)}, f32[16,384]{1,0:T(8,128)S(1)}, u32[]{:S(2)}, u32[]{:S(2)}) collective-permute-start(f32[16,384]{1,0:T(8,128)S(1)} %add.135), channel_id=1, source_target_pairs={{0,4},{1,5},{2,6},{3,7},{4,0},{5,1},{6,2},{7,3},{8,12},{9,13},{10,... | collective-permute-start | bytes 73736 | tf_op jit(solution)/shard_map/ppermute | solution.py:515
  43.5 2.0 %copy-start = (bf16[320,5120]{1,0:T(8,128)(2,1)S(1)}, bf16[320,5120]{1,0:T(8,128)(2,1)}, u32[]{:S(2)}) copy-start(bf16[320,5120]{1,0:T(8,128)(2,1)} %table_ref.1) | copy-start | bytes 9830404
  45.5 0.9 copy-start.2
  80.8 4.0 %copy-start.5 = (bf16[5120,768]{1,0:T(8,128)(2,1)S(1)}, bf16[5120,768]{1,0:T(8,128)(2,1)}, u32[]{:S(2)}) copy-start(bf16[5120,768]{1,0:T(8,128)(2,1)} %all-gather.2.cloned.1.call-done) | copy-start | bytes 23592964
  87.4 4.5 %collective-permute-start.3 = (bf16[320,512]{1,0:T(8,128)(2,1)}, bf16[320,512]{1,0:T(8,128)(2,1)S(1)}, u32[]{:S(2)}, u32[]{:S(2)}) collective-permute-start(bf16[320,512]{1,0:T(8,128)(2,1)} %fusion.4.own_ref), channel_id=1, source_target_pairs={{0,8},{8,0},{16,24},{24,16},{32,40},{40,32},{48,56},{56,48},{64,72... | collective-permute-start | bytes 983048 | tf_op jit(solution)/shard_map/ppermute | solution.py:412
  87.7 9.5 %collective-permute-start.5 = (bf16[320,256]{1,0:T(8,128)(2,1)S(1)}, bf16[320,256]{1,0:T(8,128)(2,1)S(1)}, u32[]{:S(2)}, u32[]{:S(2)}) collective-permute-start(bf16[320,256]{1,0:T(8,128)(2,1)S(1)} %fusion.7.kv_ref.rest_0_), channel_id=1, source_target_pairs={{0,48},{8,56},{16,0},{24,8},{32,16},{40,24},{48,32},{56,40},{64,11... | collective-permute-start | bytes 491528 | tf_op jit(solution)/shard_map/ppermute | solution.py:408
  90.1 7.6 %collective-permute-start.4 = (bf16[320,256]{1,0:T(8,128)(2,1)S(1)}, bf16[320,256]{1,0:T(8,128)(2,1)S(1)}, u32[]{:S(2)}, u32[]{:S(2)}) collective-permute-start(bf16[320,256]{1,0:T(8,128)(2,1)S(1)} %fusion.7.kv_ref.rest_0_), channel_id=1, source_target_pairs={{0,16},{8,24},{16,32},{24,40},{32,48},{40,56},{48,0},{56,8},{64,80... | collective-permute-start | bytes 491528 | tf_op jit(solution)/shard_map/ppermute | solution.py:408
  90.1 10.4 %collective-permute-start.8 = (bf16[320,256]{1,0:T(8,128)(2,1)S(1)}, bf16[320,256]{1,0:T(8,128)(2,1)S(1)}, u32[]{:S(2)}, u32[]{:S(2)}) collective-permute-start(bf16[320,256]{1,0:T(8,128)(2,1)S(1)} %fusion.7.kv_ref.rest_0_), channel_id=1, source_target_pairs={{0,128},{8,136},{16,144},{24,152},{32,160},{40,168},{48,176},{56,1... | collective-permute-start | bytes 491528 | tf_op jit(solution)/shard_map/ppermute | solution.py:404
  91.4 10.9 %collective-permute-start.7 = (bf16[320,256]{1,0:T(8,128)(2,1)S(1)}, bf16[320,256]{1,0:T(8,128)(2,1)S(1)}, u32[]{:S(2)}, u32[]{:S(2)}) collective-permute-start(bf16[320,256]{1,0:T(8,128)(2,1)S(1)} %fusion.7.kv_ref.rest_0_), channel_id=1, source_target_pairs={{0,192},{8,200},{16,208},{24,216},{32,224},{40,232},{48,240},{56,2... | collective-permute-start | bytes 491528 | tf_op jit(solution)/shard_map/ppermute | solution.py:404
  92.0 12.7 %collective-permute-start.6 = (bf16[320,256]{1,0:T(8,128)(2,1)S(1)}, bf16[320,256]{1,0:T(8,128)(2,1)S(1)}, u32[]{:S(2)}, u32[]{:S(2)}) collective-permute-start(bf16[320,256]{1,0:T(8,128)(2,1)S(1)} %fusion.7.kv_ref.rest_0_), channel_id=1, source_target_pairs={{0,64},{8,72},{16,80},{24,88},{32,96},{40,104},{48,112},{56,120},{... | collective-permute-start | bytes 491528 | tf_op jit(solution)/shard_map/ppermute | solution.py:404
  97.8 17.6 %collective-permute-start.12 = (bf16[640,256]{1,0:T(8,128)(2,1)S(1)}, bf16[640,256]{1,0:T(8,128)(2,1)S(1)}, u32[]{:S(2)}, u32[]{:S(2)}) collective-permute-start(bf16[640,256]{1,0:T(8,128)(2,1)S(1)} %pad_maximum_fusion), channel_id=1, source_target_pairs={{0,128},{8,136},{16,144},{24,152},{32,160},{40,168},{48,176},{56,1... | collective-permute-start | bytes 983048 | tf_op jit(solution)/shard_map/ppermute | solution.py:404
  99.6 17.4 %collective-permute-start.11 = (bf16[640,256]{1,0:T(8,128)(2,1)S(1)}, bf16[640,256]{1,0:T(8,128)(2,1)S(1)}, u32[]{:S(2)}, u32[]{:S(2)}) collective-permute-start(bf16[640,256]{1,0:T(8,128)(2,1)S(1)} %pad_maximum_fusion), channel_id=1, source_target_pairs={{0,192},{8,200},{16,208},{24,216},{32,224},{40,232},{48,240},{56,2... | collective-permute-start | bytes 983048 | tf_op jit(solution)/shard_map/ppermute | solution.py:404
  100.5 16.5 %collective-permute-start.10 = (bf16[640,256]{1,0:T(8,128)(2,1)S(1)}, bf16[640,256]{1,0:T(8,128)(2,1)S(1)}, u32[]{:S(2)}, u32[]{:S(2)}) collective-permute-start(bf16[640,256]{1,0:T(8,128)(2,1)S(1)} %pad_maximum_fusion), channel_id=1, source_target_pairs={{0,64},{8,72},{16,80},{24,88},{32,96},{40,104},{48,112},{56,120},{... | collective-permute-start | bytes 983048 | tf_op jit(solution)/shard_map/ppermute | solution.py:404
  102.3 9.7 %collective-permute-start.9 = (bf16[320,256]{1,0:T(8,128)(2,1)S(1)}, bf16[320,256]{1,0:T(8,128)(2,1)S(1)}, u32[]{:S(2)}, u32[]{:S(2)}) collective-permute-start(bf16[320,256]{1,0:T(8,128)(2,1)S(1)} %fusion.7.kv_ref.rest_0_), channel_id=1, source_target_pairs={{0,32},{8,40},{16,48},{24,56},{32,0},{40,8},{48,16},{56,24},{64,96... | collective-permute-start | bytes 491528 | tf_op jit(solution)/shard_map/ppermute | solution.py:408
  112.0 14.6 %collective-permute-start.15 = (bf16[320,256]{1,0:T(8,128)(2,1)S(1)}, bf16[320,256]{1,0:T(8,128)(2,1)S(1)}, u32[]{:S(2)}, u32[]{:S(2)}) collective-permute-start(bf16[320,256]{1,0:T(8,128)(2,1)S(1)} %collective-permute-done.9.rest_2_), channel_id=1, source_target_pairs={{0,128},{8,136},{16,144},{24,152},{32,160},{40,168},{48,176},{56,1... | collective-permute-start | bytes 491528 | tf_op jit(solution)/shard_map/ppermute | solution.py:404
  112.7 13.9 %collective-permute-start.14 = (bf16[320,256]{1,0:T(8,128)(2,1)S(1)}, bf16[320,256]{1,0:T(8,128)(2,1)S(1)}, u32[]{:S(2)}, u32[]{:S(2)}) collective-permute-start(bf16[320,256]{1,0:T(8,128)(2,1)S(1)} %collective-permute-done.9.rest_2_), channel_id=1, source_target_pairs={{0,192},{8,200},{16,208},{24,216},{32,224},{40,232},{48,240},{56,2... | collective-permute-start | bytes 491528 | tf_op jit(solution)/shard_map/ppermute | solution.py:404
  115.3 11.3 %collective-permute-start.13 = (bf16[320,256]{1,0:T(8,128)(2,1)S(1)}, bf16[320,256]{1,0:T(8,128)(2,1)S(1)}, u32[]{:S(2)}, u32[]{:S(2)}) collective-permute-start(bf16[320,256]{1,0:T(8,128)(2,1)S(1)} %collective-permute-done.9.rest_2_), channel_id=1, source_target_pairs={{0,64},{8,72},{16,80},{24,88},{32,96},{40,104},{48,112},{56,120},{... | collective-permute-start | bytes 491528 | tf_op jit(solution)/shard_map/ppermute | solution.py:404
  133.0 8.9 %collective-permute-start.16 = (f32[136,1280]{1,0:T(8,128)S(1)}, f32[136,1280]{1,0:T(8,128)S(1)}, u32[]{:S(2)}, u32[]{:S(2)}) collective-permute-start(f32[136,1280]{1,0:T(8,128)S(1)} %get-tuple-element.53), channel_id=1, source_target_pairs={{0,8},{8,0},{16,24},{24,16},{32,40},{40,32},{48,56},{56,48},{64,72... | collective-permute-start | bytes 2088968 | tf_op jit(solution)/shard_map/ppermute | solution.py:412
  139.5 1.5 collective-permute-start.17
Sparse Core Ops, SparseCore 0:
  9.9 70.8 all-gather.1
